TPU v7x, 256 devices: a whole 4x4x8 slice. The times are simulated.
256 devices in a mesh: seq: 32 (over x, z), head: 8 (over y, core).
Axes of the slice: x: 4, y: 4, z: 8, core: 2. Of those that a mesh axis runs over, the one named last changes fastest.
Arguments:
- tokens: bfloat16 [8192, 4096], P('seq', 'head'), may hold values from -6 to 6
- neighbour_shard: int32 [128, 2], P('seq'), may hold values from 0 to 31, as said below
- neighbour_row: int32 [128, 2], P('seq'), may hold values from 0 to 15
- store_rows: bfloat16 [512, 128, 896], P('seq'), may hold values from -6 to 6
- context_weight: bfloat16 [4096, 896], P('head'), may hold values from -0.1875 to 0.1875
- query_weight: bfloat16 [4096, 2048], P(None, 'head'), may hold values from -0.09375 to 0.09375
- key_weight: bfloat16 [896, 2048], P(None, 'head'), may hold values from -0.25 to 0.25
- value_weight: bfloat16 [896, 2048], P(None, 'head'), may hold values from -0.1875 to 0.1875
- output_weight: bfloat16 [2048, 4096], P(None, 'head'), may hold values from -0.25 to 0.25
Outputs:
- attended: bfloat16 [8192, 4096], P('seq', 'head')
Inputs may be any that keep to these rules, and one draw needn't show every extreme that they name: `neighbour_shard`: among the 8 neighbours of the spans of one seq index, at most 2 lie in any one store shard; in every draw one shard holds exactly 2 neighbours of every seq index's spans.
All inputs are finite; a program needn't handle non-finite values.
Results may differ from a plain program's by a relative error of at most 0.015.
The roundings to bfloat16 on the way count: a program that leaves them out, or rounds other values in their place, can miss the bound.
Values may be sent and summed in bfloat16 or wider, within the bound.
No kernel may reach another device: no remote copies, remote signals or barrier semaphores. Data moves between devices by JAX's collectives and lax.ppermute only.
A program may use at most 192 MiB of HBM per device.

v0:
```python
import math

import jax
import jax.numpy as jnp
from jax import lax
from jax.sharding import PartitionSpec as P

HD = 128
E = 896
CL = 64
NL = 128
KN = 2
EHD = 128


def encode(neighbour, context):
    batch_count = neighbour.shape[0]
    row_count = neighbour.shape[1]
    head_count = E // EHD
    query_side = neighbour.reshape(batch_count, row_count, head_count, EHD)
    key_side = context.reshape(batch_count, CL, head_count, EHD)
    scores = jnp.einsum(
        "nkgd,nqgd->ngkq", key_side, query_side, preferred_element_type=jnp.float32
    ) * (1.0 / math.sqrt(EHD))
    weights = jnp.exp(scores - jnp.max(scores, axis=2, keepdims=True))
    weights = (weights / jnp.sum(weights, axis=2, keepdims=True)).astype(jnp.bfloat16)
    mixed_in = jnp.einsum("ngkq,nkgd->nqgd", weights, key_side, preferred_element_type=jnp.float32)
    return (neighbour.astype(jnp.float32) + mixed_in.reshape(batch_count, row_count, E)).astype(
        jnp.bfloat16
    )


def local(
    tokens,
    neighbour_shard,
    neighbour_row,
    store_rows,
    context_weight,
    query_weight,
    key_weight,
    value_weight,
    output_weight,
):
    tok_rows = tokens.shape[0]
    span_count = tok_rows // CL
    requests = span_count * KN
    seq_count = lax.axis_size("seq")
    capacity = 2 * ((requests + 2 * seq_count - 5) // (2 * seq_count - 4))
    width_local = query_weight.shape[1]
    heads_local = width_local // HD
    partial_context = jnp.dot(tokens, context_weight, preferred_element_type=jnp.float32)
    context = lax.psum(partial_context, "head").astype(jnp.bfloat16)
    weight_rows = query_weight
    queries = jnp.dot(
        lax.all_gather(tokens, "head", axis=1, tiled=True),
        weight_rows,
        preferred_element_type=jnp.float32,
    ).astype(jnp.bfloat16)
    row_take = NL
    owners = neighbour_shard.reshape(requests)
    row_ids = neighbour_row.reshape(requests)
    owner_hot = (owners[:, None] == jnp.arange(seq_count, dtype=jnp.int32)[None, :]).astype(
        jnp.int32
    )
    earlier = jnp.cumsum(owner_hot, axis=0) - owner_hot
    slot_index = jnp.sum(earlier * owner_hot, axis=1)
    target = owners * capacity + slot_index
    placing = target[None, :] == jnp.arange(seq_count * capacity, dtype=jnp.int32)[:, None]
    row_buffer = jnp.sum(placing.astype(jnp.int32) * row_ids[None, :], axis=1).reshape(
        seq_count, capacity
    )
    request_context = jnp.repeat(context.reshape(span_count, CL * E), KN, axis=0)
    context_buffer = jnp.dot(
        placing.astype(jnp.bfloat16), request_context, preferred_element_type=jnp.float32
    )
    context_buffer = context_buffer.astype(jnp.bfloat16).reshape(seq_count, capacity, CL, E)
    context_in = lax.all_to_all(context_buffer, "seq", split_axis=0, concat_axis=0, tiled=True)
    rows_in = lax.all_to_all(row_buffer, "seq", split_axis=0, concat_axis=0, tiled=True)
    senders, slot_count = rows_in.shape
    neighbour = jnp.take(store_rows, rows_in.reshape(senders * slot_count), axis=0)
    encoded = encode(neighbour, context_in.reshape(senders * slot_count, CL, E))
    returned = lax.all_to_all(
        encoded.reshape(senders, slot_count, row_take, E),
        "seq",
        split_axis=0,
        concat_axis=0,
        tiled=True,
    )
    encoded_requests = jnp.take(returned.reshape(seq_count * capacity, row_take, E), target, axis=0)
    flat_encoded = encoded_requests.reshape(requests * NL, E)
    keys_local = (
        jnp.dot(flat_encoded, key_weight, preferred_element_type=jnp.float32)
        .astype(jnp.bfloat16)
        .reshape(span_count, KN * NL, heads_local, HD)
    )
    values_local = (
        jnp.dot(flat_encoded, value_weight, preferred_element_type=jnp.float32)
        .astype(jnp.bfloat16)
        .reshape(span_count, KN * NL, heads_local, HD)
    )
    queries_block = queries.reshape(span_count, CL, heads_local, HD)
    scores = jnp.einsum(
        "cqhd,ckhd->chqk", queries_block, keys_local, preferred_element_type=jnp.float32
    ) * (1.0 / math.sqrt(HD))
    weights = jnp.exp(scores - jnp.max(scores, axis=-1, keepdims=True))
    weights = (weights / jnp.sum(weights, axis=-1, keepdims=True)).astype(jnp.bfloat16)
    attention = jnp.einsum(
        "chqk,ckhd->cqhd", weights, values_local, preferred_element_type=jnp.float32
    )
    attention = attention.astype(jnp.bfloat16).reshape(tok_rows, width_local)
    weight_rows = output_weight
    summed = jnp.dot(
        lax.all_gather(attention, "head", axis=1, tiled=True),
        weight_rows,
        preferred_element_type=jnp.float32,
    )
    return summed.astype(jnp.bfloat16)


def solution(mesh):
    placed = (
        P("seq", "head"),
        P("seq", None),
        P("seq", None),
        P("seq", None, None),
        P("head", None),
        P(None, "head"),
        P(None, "head"),
        P(None, "head"),
        P(None, "head"),
    )
    return jax.shard_map(
        local, mesh=mesh, in_specs=placed, out_specs=P("seq", "head"), check_vma=False
    )
```

profile of v0, /device:TPU:1, one launch (start us, length us, event | category | flops | bytes accessed | tf_op | source)
XLA Modules:
  0.0 761.9 jit_solution(10370522824051820627)
XLA Ops:
  9.5 11.9 %all-to-all-start = ((s32[32,1,2]{2,1,0:T(1,128)}), s32[32,1,2]{2,1,0:T(1,128)S(1)}, u32[]{:S(2)}, u32[]{:S(2)}) async-start(s32[32,1,2]{2,1,0:T(1,128)} %bitcast.1), calls=%async_computation | async-start | bytes 32768 | tf_op jit(solution)/shard_map/all_to_all | solution.py:78
  23.1 29.8 %all-reduce.1 = bf16[256,896]{1,0:T(8,128)(2,1)S(1)} all-reduce(f32[256,896]{1,0:T(8,128)S(1)} %fusion.30), channel_id=1, replica_groups=mesh['seq'=32,'head'=8] {'head'}, use_global_device_ids=true, to_apply=%region_3.4 | all-reduce | flops 229376 | bytes 1376256 | tf_op jit(solution)/shard_map/psum | solution.py:52
  56.0 2.2 convolution_convert_fusion
  58.2 4.4 copy.80
  62.6 9.2 %all-to-all-start.1 = ((bf16[32,2,64,896]{3,2,1,0:T(8,128)(2,1)}), bf16[32,2,64,896]{3,2,1,0:T(8,128)(2,1)}, u32[]{:S(2)}, u32[]{:S(2)}) async-start(bf16[32,2,64,896]{3,2,1,0:T(8,128)(2,1)} %bitcast.49), calls=%async_computation.1 | async-start | bytes 14680064 | tf_op jit(solution)/shard_map/all_to_all | solution.py:77
  73.1 10.0 %gather_fusion = bf16[64,128,896]{2,1,0:T(8,128)(2,1)} fusion(bf16[16,128,896]{2,1,0:T(8,128)(2,1)} %param.12, s32[1024]{0:T(1024)S(1)} %pad_clamp_fusion.1), kind=kCustom, calls=%fused_computation | custom fusion | bytes 29360384 | tf_op jit(solution)/shard_map/jit(_take)/gather | solution.py:80
  83.1 20.8 %copy.69 = bf16[64,128,896]{1,2,0:T(8,128)(2,1)} copy(bf16[64,128,896]{2,1,0:T(8,128)(2,1)} %gather_fusion) | data formatting | bytes 29360128 | tf_op jit(solution)/shard_map/jit(_take)/gather | solution.py:80
  104.0 20.9 %copy.68 = bf16[32,2,128,896]{2,3,1,0:T(8,128)(2,1)} copy(bf16[32,2,128,896]{3,2,1,0:T(8,128)(2,1)} %bitcast.47) | data formatting | bytes 29360128 | tf_op jit(solution)/shard_map/jit(_take)/gather | solution.py:80
  125.1 107.5 %all-to-all-done.1 = bf16[32,2,64,896]{3,2,1,0:T(8,128)(2,1)} async-done(((bf16[32,2,64,896]{3,2,1,0:T(8,128)(2,1)}), bf16[32,2,64,896]{3,2,1,0:T(8,128)(2,1)}, u32[]{:S(2)}, u32[]{:S(2)}) %all-to-all-start.1) | async-done | bytes 7340064 | tf_op jit(solution)/shard_map/all_to_all | solution.py:77
  232.6 15.0 %reshape_reshape.3 = bf16[64,64,7,128]{3,2,1,0:T(8,128)(2,1)} reshape(bf16[32,2,64,896]{3,2,1,0:T(8,128)(2,1)} %all-to-all-done.1) | data formatting | bytes 14680064 | tf_op jit(solution)/shard_map/reshape;reshape | solution.py:21
  247.6 13.1 %fusion.2 = f32[64,7,64,128]{3,2,1,0:T(8,128)} fusion(bf16[64,128,7,128]{1,3,2,0:T(8,128)(2,1)} %bitcast.48, pred[64]{0:T(512)(128)(4,1)S(1)} %compare_and_fusion, bf16[64,64,7,128]{3,2,1,0:T(8,128)(2,1)} %reshape_reshape.3), kind=kOutput, calls=%fused_computation.8 | convolution fusion | flops 946864128 | bytes 36700224 | tf_op jit(solution)/shard_map/nkgd,nqgd->ngkq/dot_general | solution.py:22
  260.7 18.2 %fusion.28 = (f32[64,7,128]{2,1,0:T(8,128)S(1)}, f32[64,7,64,128]{3,2,1,0:T(8,128)}) fusion(f32[64,7,64,128]{3,2,1,0:T(8,128)} %fusion.2), kind=kOutput, calls=%fused_computation.60 | output fusion | flops 14680127 | bytes 29589504 | tf_op jit(solution)/shard_map/sub | solution.py:25
  278.9 18.2 %fusion.8 = f32[64,7,128,128]{3,2,1,0:T(8,128)} fusion(f32[64,7,64,128]{3,2,1,0:T(8,128)} %get-tuple-element.8, f32[64,7,128]{2,1,0:T(8,128)S(1)} %get-tuple-element.7, bf16[64,64,7,128]{3,2,1,0:T(8,128)(2,1)} %reshape_reshape.3), kind=kOutput, calls=%fused_computation.13 | convolution fusion | flops 946864128 | bytes 51609600 | tf_op jit(solution)/shard_map/ngkq,nkgd->nqgd/dot_general | solution.py:27
  297.1 20.5 %add_convert_fusion = bf16[32,2,128,896]{2,3,1,0:T(8,128)(2,1)} fusion(f32[32,2,128,896]{2,3,1,0:T(8,128)} %bitcast.51, bf16[32,2,128,896]{2,3,1,0:T(8,128)(2,1)} %copy.68, pred[32,2]{1,0:T(8,128)(4,1)S(1)} %copy.67), kind=kLoop, calls=%fused_computation.5 | loop fusion | flops 29360128 | bytes 58720320 | tf_op jit(solution)/shard_map/convert_element_type | solution.py:28
  317.6 9.4 %all-to-all-start.2 = ((bf16[32,2,128,896]{2,3,1,0:T(8,128)(2,1)}), bf16[32,2,128,896]{2,3,1,0:T(8,128)(2,1)}, u32[]{:S(2)}, u32[]{:S(2)}) async-start(bf16[32,2,128,896]{2,3,1,0:T(8,128)(2,1)} %add_convert_fusion), calls=%async_computation.2 | async-start | bytes 29360128 | tf_op jit(solution)/shard_map/all_to_all | solution.py:82
  328.1 44.9 %all-gather.3.cloned.1.call-done = bf16[256,4096]{1,0:T(8,128)(2,1)} async-done(((bf16[256,512]{1,0:T(8,128)(2,1)}), bf16[256,4096]{1,0:T(8,128)(2,1)}) %all-gather.3.cloned.1.call-update) | async-done | bytes 2097168 | tf_op jit(solution)/shard_map/all_gather | solution.py:55
  373.0 2.9 convolution_convert_fusion.5
  376.0 282.4 %all-to-all-done.2 = bf16[32,2,128,896]{2,3,1,0:T(8,128)(2,1)} async-done(((bf16[32,2,128,896]{2,3,1,0:T(8,128)(2,1)}), bf16[32,2,128,896]{2,3,1,0:T(8,128)(2,1)}, u32[]{:S(2)}, u32[]{:S(2)}) %all-to-all-start.2) | async-done | bytes 14680096 | tf_op jit(solution)/shard_map/all_to_all | solution.py:82
  658.4 19.5 %copy.73 = bf16[32,2,128,896]{3,2,1,0:T(8,128)(2,1)} copy(bf16[32,2,128,896]{2,3,1,0:T(8,128)(2,1)} %all-to-all-done.2) | data formatting | bytes 29360128 | tf_op jit(solution)/shard_map/all_to_all | solution.py:82
  677.9 7.2 gather_fusion.1
  685.1 1.8 bitcast_select_fusion
  689.6 3.1 convolution_convert_fusion.2
  695.7 56.7 %all-gather.5.cloned.1.call-done = bf16[256,2048]{1,0:T(8,128)(2,1)} async-done(((bf16[256,256]{1,0:T(8,128)(2,1)}), bf16[256,2048]{1,0:T(8,128)(2,1)}) %all-gather.5.cloned.1.call-update) | async-done | bytes 1048592 | tf_op jit(solution)/shard_map/all_gather | solution.py:113
  752.4 2.6 convolution_convert_fusion.3
  (52 shorter events, 16.0 us)
Async XLA Ops:
  6.5 745.9 %copy-start = (bf16[2048,512]{1,0:T(8,128)(2,1)S(1)}, bf16[2048,512]{1,0:T(8,128)(2,1)}, u32[]{:S(2)}) copy-start(bf16[2048,512]{1,0:T(8,128)(2,1)} %param.17) | copy-start | bytes 6291460
  9.5 53.1 %all-to-all-start = ((s32[32,1,2]{2,1,0:T(1,128)}), s32[32,1,2]{2,1,0:T(1,128)S(1)}, u32[]{:S(2)}, u32[]{:S(2)}) async-start(s32[32,1,2]{2,1,0:T(1,128)} %bitcast.1), calls=%async_computation | async-start | bytes 32768 | tf_op jit(solution)/shard_map/all_to_all | solution.py:78
  62.6 170.0 %all-to-all-start.1 = ((bf16[32,2,64,896]{3,2,1,0:T(8,128)(2,1)}), bf16[32,2,64,896]{3,2,1,0:T(8,128)(2,1)}, u32[]{:S(2)}, u32[]{:S(2)}) async-start(bf16[32,2,64,896]{3,2,1,0:T(8,128)(2,1)} %bitcast.49), calls=%async_computation.1 | async-start | bytes 14680064 | tf_op jit(solution)/shard_map/all_to_all | solution.py:77
  317.6 10.2 %copy-start.2 = (s32[4,2]{0,1:T(2,128)S(1)}, s32[4,2]{0,1:T(2,128)}, u32[]{:S(2)}) copy-start(s32[4,2]{0,1:T(2,128)} %param.10) | copy-start | bytes 100
  317.6 340.8 %all-to-all-start.2 = ((bf16[32,2,128,896]{2,3,1,0:T(8,128)(2,1)}), bf16[32,2,128,896]{2,3,1,0:T(8,128)(2,1)}, u32[]{:S(2)}, u32[]{:S(2)}) async-start(bf16[32,2,128,896]{2,3,1,0:T(8,128)(2,1)} %add_convert_fusion), calls=%async_computation.2 | async-start | bytes 29360128 | tf_op jit(solution)/shard_map/all_to_all | solution.py:82
  327.0 46.0 %all-gather.3.cloned.1.call-start = ((), (), s32[]{:S(2)}) async-start(), calls=%async_computation.3 | async-start | bytes 2359296 | tf_op jit(solution)/shard_map/all_gather | solution.py:55
  327.8 424.6 %all-gather.5.cloned.1.call-start = ((), (), s32[]{:S(2)}) async-start(), calls=%async_computation.4 | async-start | bytes 1179648 | tf_op jit(solution)/shard_map/all_gather | solution.py:113
  376.0 312.2 %copy-start.3 = (bf16[896,256]{1,0:T(8,128)(2,1)S(1)}, bf16[896,256]{1,0:T(8,128)(2,1)}, u32[]{:S(2)}) copy-start(bf16[896,256]{1,0:T(8,128)(2,1)} %param.15) | copy-start | bytes 1376260
  686.9 1.3 copy-start.1
Sparse Core Ops, SparseCore 0:
  329.7 43.2 all-gather.2
  695.8 56.5 all-gather.4
where the time goes:
time: 764 us; the launch traced here: 762 us
  waiting for transfers between devices  492 us (64%)
  local copies, waits for them, and re-layouts  108 us (14%)
  matrix products  45.8 us (6%)
  other arithmetic  41.9 us (5%)
  starting transfers between devices  30.6 us (4%)
  blocking collectives  29.8 us (4%)
  between operations  13.6 us (2%)
    all_to_all x1, waiting for transfers between devices, local(): lax.all_to_all(encoded.reshape(senders, slot_count, row_take, E), 'seq',...  282 us
    all_to_all x1, waiting for transfers between devices, local(): lax.all_to_all(context_buffer, 'seq', split_axis=0, concat_axis=0, tiled=...  107 us
    all_gather x1, waiting for transfers between devices, local(): lax.all_gather(attention, 'head', axis=1, tiled=True)  56.7 us
    gather x3, local copies, waits for them, and re-layouts, local(): jnp.take(store_rows, rows_in.reshape(senders * slot_count), axis=0)  51.7 us
    all_gather x1, waiting for transfers between devices, local(): lax.all_gather(tokens, 'head', axis=1, tiled=True)  44.9 us
    psum x1, blocking collectives, local(): context = lax.psum(partial_context, 'head').astype(jnp.bfloat16)  29.8 us
    convert_element_type x1, other arithmetic, encode(): (neighbour.astype(jnp.float32) + mixed_in.reshape(batch_count, row_count,...  20.5 us
    all_to_all x1, local copies, waits for them, and re-layouts, local(): lax.all_to_all(encoded.reshape(senders, slot_count, row_take, E), 'seq',...  19.5 us
  transfers between devices with their start and end apart: 5, of which 4 were waited for; matrix products, arithmetic and copies ran while one was open for 9% of the time, Pallas kernels for 0%

commit v1 on v0

v1 whole, which is shorter than its diff:
```python
import functools
import math

import jax
import jax.numpy as jnp
from jax import lax
from jax.experimental import pallas as pl
from jax.experimental.pallas import tpu as pltpu
from jax.sharding import PartitionSpec as P

HD = 128
E = 896
CL = 64
NL = 128
KN = 2
EHD = 128
NX, NZ, NY, NC = 4, 8, 4, 2
NS = NX * NZ
NH = NY * NC
CAP = 2
ROWS = NL // NH
BF = jnp.bfloat16
F32 = jnp.float32


def y_shift(a, r):
    pairs = [(y * NC + c, ((y + r) % NY) * NC + c) for y in range(NY) for c in range(NC)]
    return lax.ppermute(a, "head", pairs)


def core_swap(a):
    return lax.ppermute(a, "head", [(h, h ^ 1) for h in range(NH)])


def head_blocks(a):
    own = [a] + [y_shift(a, r) for r in (1, 3, 2)]
    own = [own[0], own[1], own[3], own[2]]
    return [(b, core_swap(b)) for b in own]


def block_order(y, c):
    return jnp.stack(
        [((y - r) % NY) * NC + (c if s == 0 else 1 - c) for r in range(NY) for s in range(NC)]
    ).astype(jnp.int32)


def blocked_dot_kernel(depth, order, *refs):
    blocks, w, out = refs[:NH], refs[NH], refs[NH + 1]
    total = None
    for k in range(NH):
        start = pl.multiple_of(order[k] * depth, depth)
        part = jnp.dot(blocks[k][...], w[pl.ds(start, depth), :], preferred_element_type=F32)
        total = part if total is None else total + part
    out[...] = total.astype(out.dtype)


def blocked_dot(blocks, order, w, name):
    rows, depth = blocks[0].shape
    width = w.shape[1]
    vmem = pl.BlockSpec(memory_space=pltpu.VMEM)
    return pl.pallas_call(
        functools.partial(blocked_dot_kernel, depth),
        out_shape=jax.ShapeDtypeStruct((rows, width), BF),
        in_specs=[pl.BlockSpec(memory_space=pltpu.SMEM)] + [vmem] * (NH + 1),
        out_specs=vmem,
        compiler_params=pltpu.CompilerParams(vmem_limit_bytes=24 * 2**20),
        cost_estimate=pl.CostEstimate(
            flops=2 * rows * depth * NH * width,
            bytes_accessed=2 * (rows * depth * NH + depth * NH * width + rows * width),
            transcendentals=0,
        ),
        name=name,
    )(order, *blocks, w)


def encode_kernel(order, nb, *refs):
    ctx, out = refs[: NY * NC], refs[NY * NC]
    heads = E // EHD
    for r in range(NY):
        span = order[NC * r] // NC
        context = jnp.concatenate([ctx[NC * r][...], ctx[NC * r + 1][...]], axis=0)
        rows = nb[pl.ds(span * KN, KN)].reshape(KN * ROWS, E)
        scores = jnp.concatenate(
            [
                lax.dot_general(
                    rows[:, g * EHD : (g + 1) * EHD],
                    context[:, g * EHD : (g + 1) * EHD],
                    (((1,), (1,)), ((), ())),
                    preferred_element_type=F32,
                )
                for g in range(heads)
            ],
            axis=0,
        ) * (1.0 / math.sqrt(EHD))
        weights = jnp.exp(scores - jnp.max(scores, axis=1, keepdims=True))
        weights = (weights / jnp.sum(weights, axis=1, keepdims=True)).astype(BF)
        mixed = jnp.concatenate(
            [
                jnp.dot(
                    weights[g * KN * ROWS : (g + 1) * KN * ROWS],
                    context[:, g * EHD : (g + 1) * EHD],
                    preferred_element_type=F32,
                )
                for g in range(heads)
            ],
            axis=1,
        )
        encoded = (rows.astype(F32) + mixed).astype(BF)
        out[pl.ds(span * KN, KN)] = encoded.reshape(KN, ROWS, E)


def encode(order, nb, ctx_blocks):
    vmem = pl.BlockSpec(memory_space=pltpu.VMEM)
    return pl.pallas_call(
        encode_kernel,
        out_shape=jax.ShapeDtypeStruct(nb.shape, BF),
        in_specs=[pl.BlockSpec(memory_space=pltpu.SMEM)] + [vmem] * (1 + NH),
        out_specs=vmem,
        compiler_params=pltpu.CompilerParams(vmem_limit_bytes=24 * 2**20),
        cost_estimate=pl.CostEstimate(
            flops=4 * nb.shape[0] * ROWS * CL * E,
            bytes_accessed=2 * 2 * nb.size + 2 * 256 * E,
            transcendentals=nb.shape[0] * ROWS * CL * 7,
        ),
        name="encode",
    )(order, nb, *ctx_blocks)


def attend_kernel(*refs):
    blocks = refs[:NH]
    q, wk, wv, out, rows, sems = refs[NH:]
    spans = rows.shape[0]
    copies = [
        pltpu.make_async_copy(blocks[b], rows.at[:, b], sems.at[b]) for b in range(NH)
    ]
    for copy in copies:
        copy.start()
    for copy in copies:
        copy.wait()
    flat = rows[...].reshape(spans * KN * NL, E)
    keys = jnp.dot(flat, wk[...], preferred_element_type=F32).astype(BF)
    values = jnp.dot(flat, wv[...], preferred_element_type=F32).astype(BF)
    heads = q.shape[1] // HD
    span_rows = KN * NL
    units = [(s, h) for s in range(spans) for h in range(heads)]
    scores = jnp.concatenate(
        [
            lax.dot_general(
                q[s * CL : (s + 1) * CL, h * HD : (h + 1) * HD],
                keys[s * span_rows : (s + 1) * span_rows, h * HD : (h + 1) * HD],
                (((1,), (1,)), ((), ())),
                preferred_element_type=F32,
            )
            for s, h in units
        ],
        axis=0,
    ) * (1.0 / math.sqrt(HD))
    weights = jnp.exp(scores - jnp.max(scores, axis=1, keepdims=True))
    weights = (weights / jnp.sum(weights, axis=1, keepdims=True)).astype(BF)
    for i, (s, h) in enumerate(units):
        out[s * CL : (s + 1) * CL, h * HD : (h + 1) * HD] = jnp.dot(
            weights[i * CL : (i + 1) * CL],
            values[s * span_rows : (s + 1) * span_rows, h * HD : (h + 1) * HD],
            preferred_element_type=F32,
        ).astype(BF)


def attend(blocks, queries, key_weight, value_weight):
    tokens, width = queries.shape
    spans = tokens // CL
    vmem = pl.BlockSpec(memory_space=pltpu.VMEM)
    blocks = [b.reshape(spans, KN * ROWS, E) for b in blocks]
    return pl.pallas_call(
        attend_kernel,
        out_shape=jax.ShapeDtypeStruct((tokens, width), BF),
        in_specs=[pl.BlockSpec(memory_space=pl.ANY)] * NH + [vmem] * 3,
        out_specs=vmem,
        scratch_shapes=[
            pltpu.VMEM((spans, NH, KN * ROWS, E), BF),
            pltpu.SemaphoreType.DMA((NH,)),
        ],
        compiler_params=pltpu.CompilerParams(vmem_limit_bytes=32 * 2**20),
        cost_estimate=pl.CostEstimate(
            flops=4 * spans * KN * NL * E * width + 4 * tokens * KN * NL * width,
            bytes_accessed=2 * (spans * KN * NL * E + 2 * E * width + 2 * tokens * width),
            transcendentals=tokens * KN * NL * 2,
        ),
        name="attend",
    )(*blocks, queries, key_weight, value_weight)


def sum_context(partial, y, c):
    parts = partial.reshape(NY, NC, -1, E)
    mine = lax.dynamic_index_in_dim(parts, c, axis=1, keepdims=False)
    theirs = lax.dynamic_index_in_dim(parts, 1 - c, axis=1, keepdims=False)
    chip = mine + core_swap(theirs)
    total = lax.dynamic_index_in_dim(chip, y, axis=0, keepdims=False)
    for r in (1, 3, 2):
        sent = lax.dynamic_index_in_dim(chip, (y + r) % NY, axis=0, keepdims=False)
        total = total + y_shift(sent, r)
    return total.astype(BF)


def fetch(store, neighbour_shard, neighbour_row, head):
    requests = neighbour_shard.size
    owners = neighbour_shard.reshape(requests)
    row_ids = neighbour_row.reshape(requests)
    hot = (owners[:, None] == jnp.arange(NS, dtype=jnp.int32)[None, :]).astype(jnp.int32)
    earlier = jnp.cumsum(hot, axis=0) - hot
    target = owners * CAP + jnp.sum(earlier * hot, axis=1)
    placing = target[None, :] == jnp.arange(NS * CAP, dtype=jnp.int32)[:, None]
    row_buffer = jnp.sum(placing.astype(jnp.int32) * row_ids[None, :], axis=1).reshape(NS, CAP)
    rows_in = lax.all_to_all(row_buffer, "seq", split_axis=0, concat_axis=0, tiled=True)
    slices = lax.dynamic_slice_in_dim(store, head * ROWS, ROWS, axis=1)
    sent = jnp.take(slices, rows_in.reshape(NS * CAP), axis=0)
    got = lax.all_to_all(sent, "seq", split_axis=0, concat_axis=0, tiled=True)
    return jnp.take(got, target, axis=0)


def local(
    tokens,
    neighbour_shard,
    neighbour_row,
    store_rows,
    context_weight,
    query_weight,
    key_weight,
    value_weight,
    output_weight,
):
    head = lax.axis_index("head")
    y, c = head // NC, head % NC
    order = block_order(y, c)
    neighbour = fetch(store_rows, neighbour_shard, neighbour_row, head)
    partial = jnp.dot(tokens, context_weight, preferred_element_type=F32)
    context = sum_context(partial, y, c)
    ctx_blocks = [b for pair in head_blocks(context) for b in pair]
    tok_blocks = [b for pair in head_blocks(tokens) for b in pair]
    queries = blocked_dot(tok_blocks, order, query_weight, "queries")
    encoded = encode(order, neighbour, ctx_blocks)
    enc_blocks = [b for pair in head_blocks(encoded) for b in pair]
    attention = attend(enc_blocks, queries, key_weight, value_weight)
    att_blocks = [b for pair in head_blocks(attention) for b in pair]
    return blocked_dot(att_blocks, order, output_weight, "project")


def solution(mesh):
    placed = (
        P("seq", "head"),
        P("seq", None),
        P("seq", None),
        P("seq", None, None),
        P("head", None),
        P(None, "head"),
        P(None, "head"),
        P(None, "head"),
        P(None, "head"),
    )
    return jax.shard_map(
        local, mesh=mesh, in_specs=placed, out_specs=P("seq", "head"), check_vma=False
    )
```

time: 764 us -> 120 us (0.16)
  waiting for transfers between devices: 492 us -> 43.3 us
  local copies, waits for them, and re-layouts: 108 us -> 11.2 us
  matrix products: 45.8 us -> 0.44 us
  other arithmetic: 41.9 us -> 5.36 us
  blocking collectives: 29.8 us -> 0 us
  starting transfers between devices: 30.6 us -> 49.9 us
  between operations: 13.6 us -> 0.37 us
  Pallas kernels: 0 us -> 8.64 us
    all_to_all x3 -> x2, waiting for transfers between devices: 390 us -> 16.3 us  [the longest x1 8.8 us: fetch(): got = lax.all_to_all(sent, 'seq', split_axis=0, concat_axis=0, tiled=True)]
    all_gather x2 -> x0, waiting for transfers between devices: 102 us -> none  [the longest x1 56.7 us: local(): lax.all_gather(attention, 'head', axis=1, tiled=True)]
    gather x4 -> x2, local copies, waits for them, and re-layouts: 58.8 us -> 3.6 us  [the longest x1 2.76 us: fetch(): return jnp.take(got, target, axis=0)]
    dot_general x10 -> x1, matrix products: 45.8 us -> 0.44 us  [local(): partial = jnp.dot(tokens, context_weight, preferred_element_type=F32)]
    ppermute x0 -> x32, starting transfers between devices: none -> 33.2 us  [the longest x15 18.4 us: y_shift(): return lax.ppermute(a, 'head', pairs)]
    psum x1 -> x0, blocking collectives: 29.8 us -> none  [local(): context = lax.psum(partial_context, 'head').astype(jnp.bfloat16)]
    ppermute x0 -> x32, waiting for transfers between devices: none -> 27.1 us  [the longest x15 25.6 us: y_shift(): return lax.ppermute(a, 'head', pairs)]
    all_to_all x4 -> x2, local copies, waits for them, and re-layouts: 20.8 us -> 1.23 us  [fetch(): lax.all_to_all(row_buffer, 'seq', split_axis=0, concat_axis=0, tiled=True)]
  transfers between devices with their start and end apart: 5 -> 34, of which waited for: 4 -> 12; matrix products, arithmetic and copies ran while one was open for 9% -> 7% of each run, Pallas kernels for 0% -> 4%
where the time goes in v1:
time: 120 us; the launch traced here: 119 us
  starting transfers between devices  49.9 us (42%)
  waiting for transfers between devices  43.3 us (36%)
  local copies, waits for them, and re-layouts  11.2 us (9%)
  Pallas kernels  8.64 us (7%)
  other arithmetic  5.36 us (4%)
    ppermute x15, waiting for transfers between devices, y_shift(): return lax.ppermute(a, 'head', pairs)  25.6 us
    ppermute x15, starting transfers between devices, y_shift(): return lax.ppermute(a, 'head', pairs)  18.4 us
    ppermute x17, starting transfers between devices, core_swap(): return lax.ppermute(a, 'head', [(h, h ^ 1) for h in range(NH)])  14.8 us
    all_to_all x1, starting transfers between devices, fetch(): lax.all_to_all(row_buffer, 'seq', split_axis=0, concat_axis=0, tiled=True)  11.9 us
    all_to_all x1, waiting for transfers between devices, fetch(): got = lax.all_to_all(sent, 'seq', split_axis=0, concat_axis=0, tiled=True)  8.8 us
    all_to_all x1, waiting for transfers between devices, fetch(): lax.all_to_all(row_buffer, 'seq', split_axis=0, concat_axis=0, tiled=True)  7.49 us
    all_to_all x1, starting transfers between devices, fetch(): got = lax.all_to_all(sent, 'seq', split_axis=0, concat_axis=0, tiled=True)  4.86 us
    unnamed x22, local copies, waits for them, and re-layouts  3.85 us
  transfers between devices with their start and end apart: 34, of which 12 were waited for; matrix products, arithmetic and copies ran while one was open for 7% of the time, Pallas kernels for 4%

profile of v1, /device:TPU:1, one launch (start us, length us, event | category | flops | bytes accessed | tf_op | source)
XLA Modules:
  0.0 119.2 jit_solution(14329882930417780463)
XLA Ops:
  2.9 11.9 %all-to-all-start = ((s32[32,1,2]{2,1,0:T(1,128)}), s32[32,1,2]{2,1,0:T(1,128)S(1)}, u32[]{:S(2)}, u32[]{:S(2)}) async-start(s32[32,1,2]{2,1,0:T(1,128)} %bitcast.8), calls=%async_computation | async-start | bytes 32768 | tf_op jit(solution)/shard_map/all_to_all | solution.py:213
  15.8 7.5 %all-to-all-done = s32[32,1,2]{2,1,0:T(1,128)S(1)} async-done(((s32[32,1,2]{2,1,0:T(1,128)}), s32[32,1,2]{2,1,0:T(1,128)S(1)}, u32[]{:S(2)}, u32[]{:S(2)}) %all-to-all-start) | async-done | bytes 288 | tf_op jit(solution)/shard_map/all_to_all | solution.py:213
  25.6 1.5 %broadcast_select_fusion = bf16[64,16,896]{2,1,0:T(8,128)(2,1)} fusion(bf16[64,16,896]{2,1,0:T(8,128)(2,1)S(1)} %gather_fusion, pred[64]{0:T(512)(128)(4,1)S(1)} %compare_and_fusion), kind=kLoop, calls=%fused_computation.2 | loop fusion | flops 917504 | bytes 3670080 | tf_op jit(solution)/shard_map/jit(_take)/select_n | solution.py:215
  27.1 4.9 %all-to-all-start.1 = ((bf16[64,16,896]{2,1,0:T(8,128)(2,1)}), bf16[64,16,896]{2,1,0:T(8,128)(2,1)}, u32[]{:S(2)}, u32[]{:S(2)}) async-start(bf16[64,16,896]{2,1,0:T(8,128)(2,1)} %broadcast_select_fusion), calls=%async_computation.1 | async-start | bytes 3670016 | tf_op jit(solution)/shard_map/all_to_all | solution.py:216
  32.5 2.2 %collective-permute-start = (f32[4,32,896]{2,1,0:T(8,128)S(1)}, f32[4,32,896]{2,1,0:T(8,128)S(1)}, u32[]{:S(2)}, u32[]{:S(2)}) collective-permute-start(f32[4,32,896]{2,1,0:T(8,128)S(1)} %dynamic-slice_bitcast_fusion), channel_id=1, source_target_pairs={{0,1},{1,0},{2,3},{3,2},{4,5},{5,4},{6,7},{7,6},{8,9},{9,8},{10,11... | collective-permute-start | bytes 1376264 | tf_op jit(solution)/shard_map/ppermute | solution.py:32
  36.0 2.6 %collective-permute-start.21 = (bf16[256,512]{1,0:T(8,128)(2,1)S(1)}, bf16[256,512]{1,0:T(8,128)(2,1)}, u32[]{:S(2)}, u32[]{:S(2)}) collective-permute-start(bf16[256,512]{1,0:T(8,128)(2,1)S(1)} %copy-done.3), channel_id=1, source_target_pairs={{0,4},{1,5},{2,6},{3,7},{4,0},{5,1},{6,2},{7,3},{8,12},{9,13},{10,... | collective-permute-start | bytes 786440 | tf_op jit(solution)/shard_map/ppermute | solution.py:28
  42.3 11.0 %collective-permute-done.3 = f32[32,896]{1,0:T(8,128)} collective-permute-done((f32[32,896]{1,0:T(8,128)}, f32[32,896]{1,0:T(8,128)}, u32[]{:S(2)}, u32[]{:S(2)}) %collective-permute-start.3) | collective-permute-done | bytes 114720 | tf_op jit(solution)/shard_map/ppermute | solution.py:28
  53.3 2.8 %collective-permute-done.1 = f32[32,896]{1,0:T(8,128)} collective-permute-done((f32[32,896]{1,0:T(8,128)}, f32[32,896]{1,0:T(8,128)}, u32[]{:S(2)}, u32[]{:S(2)}) %collective-permute-start.1) | collective-permute-done | bytes 114720 | tf_op jit(solution)/shard_map/ppermute | solution.py:28
  56.0 1.7 %fusion.2.refs_0_ = bf16[32,896]{1,0:T(8,128)(2,1)} fusion(f32[32,896]{1,0:T(8,128)} %collective-permute-done.3, f32[32,896]{1,0:T(8,128)} %collective-permute-done.2, f32[32,896]{1,0:T(8,128)} %collective-permute-done.1, f32[4,32,896]{2,1,0:T(8,128)} %copy-done.8, s32[]{:T(128)S(6)} %select_n.125), kind=kLoop, calls=%fused_computation.9 | loop fusion | flops 114688 | bytes 516100 | tf_op jit(solution)/shard_map/convert_element_type | solution.py:201
  58.2 1.5 %collective-permute-start.7 = (bf16[32,896]{1,0:T(8,128)(2,1)}, bf16[32,896]{1,0:T(8,128)(2,1)}, u32[]{:S(2)}, u32[]{:S(2)}) collective-permute-start(bf16[32,896]{1,0:T(8,128)(2,1)} %fusion.2.refs_0_), channel_id=1, source_target_pairs={{0,4},{1,5},{2,6},{3,7},{4,0},{5,1},{6,2},{7,3},{8,12},{9,13},{10,... | collective-permute-start | bytes 172040 | tf_op jit(solution)/shard_map/ppermute | solution.py:28
  62.5 2.1 %collective-permute-done.5.refs_2_ = bf16[32,896]{1,0:T(8,128)(2,1)} collective-permute-done((bf16[32,896]{1,0:T(8,128)(2,1)}, bf16[32,896]{1,0:T(8,128)(2,1)}, u32[]{:S(2)}, u32[]{:S(2)}) %collective-permute-start.5) | collective-permute-done | bytes 57376 | tf_op jit(solution)/shard_map/ppermute | solution.py:28
  65.5 8.8 %all-to-all-done.1 = bf16[64,16,896]{2,1,0:T(8,128)(2,1)} async-done(((bf16[64,16,896]{2,1,0:T(8,128)(2,1)}), bf16[64,16,896]{2,1,0:T(8,128)(2,1)}, u32[]{:S(2)}, u32[]{:S(2)}) %all-to-all-start.1) | async-done | bytes 1835040 | tf_op jit(solution)/shard_map/all_to_all | solution.py:216
  74.3 2.8 %gather_fusion.1 = bf16[8,16,896]{2,1,0:T(8,128)(2,1)} fusion(bf16[64,16,896]{2,1,0:T(8,128)(2,1)} %all-to-all-done.1, s32[1024]{0:T(1024)S(1)} %pad_clamp_fusion), kind=kCustom, calls=%fused_computation.1 | custom fusion | bytes 458784 | tf_op jit(solution)/shard_map/jit(_take)/gather | solution.py:217
  77.1 3.5 %collective-permute-start.20 = (bf16[256,512]{1,0:T(8,128)(2,1)S(1)}, bf16[256,512]{1,0:T(8,128)(2,1)S(1)}, u32[]{:S(2)}, u32[]{:S(2)}) collective-permute-start(bf16[256,512]{1,0:T(8,128)(2,1)S(1)} %collective-permute-done.19.refs_2_), channel_id=1, source_target_pairs={{0,1},{1,0},{2,3},{3,2},{4,5},{5,4},{6,7},{7,6},{8,9},{9,8},{10,11... | collective-permute-start | bytes 786440 | tf_op jit(solution)/shard_map/ppermute | solution.py:32
  83.2 2.5 %encode.1 = bf16[8,16,896]{2,1,0:T(8,128)(2,1)S(1)} custom-call(s32[8]{0:T(128)S(1)} %stack.35.order, bf16[8,16,896]{2,1,0:T(8,128)(2,1)S(1)} %broadcast_select_fusion.1.nb, bf16[32,896]{1,0:T(8,128)(2,1)} %fusion.2.refs_0_, bf16[32,896]{1,0:T(8,128)(2,1)S(1)} %copy-done.5, bf16[32,896]{1,0:T(8,128)(2,1)} %collective-permute-done.5.refs_2_, ...), custom_call_target="tpu_custom_call" | custom-call | flops 29360128 | bytes 917504 | tf_op jit(solution)/shard_map/encode/pallas_call | solution.py:114
  85.7 1.4 %collective-permute-start.12 = (bf16[8,16,896]{2,1,0:T(8,128)(2,1)S(1)}, bf16[8,16,896]{2,1,0:T(8,128)(2,1)S(1)}, u32[]{:S(2)}, u32[]{:S(2)}) collective-permute-start(bf16[8,16,896]{2,1,0:T(8,128)(2,1)S(1)} %encode.1), channel_id=1, source_target_pairs={{0,2},{1,3},{2,4},{3,5},{4,6},{5,7},{6,0},{7,1},{8,10},{9,11},{10,... | collective-permute-start | bytes 688136 | tf_op jit(solution)/shard_map/ppermute | solution.py:28
  87.1 2.6 %collective-permute-start.14 = (bf16[8,16,896]{2,1,0:T(8,128)(2,1)S(1)}, bf16[8,16,896]{2,1,0:T(8,128)(2,1)S(1)}, u32[]{:S(2)}, u32[]{:S(2)}) collective-permute-start(bf16[8,16,896]{2,1,0:T(8,128)(2,1)S(1)} %encode.1), channel_id=1, source_target_pairs={{0,4},{1,5},{2,6},{3,7},{4,0},{5,1},{6,2},{7,3},{8,12},{9,13},{10,... | collective-permute-start | bytes 688136 | tf_op jit(solution)/shard_map/ppermute | solution.py:28
  92.1 1.9 %collective-permute-done.12 = bf16[8,16,896]{2,1,0:T(8,128)(2,1)S(1)} collective-permute-done((bf16[8,16,896]{2,1,0:T(8,128)(2,1)S(1)}, bf16[8,16,896]{2,1,0:T(8,128)(2,1)S(1)}, u32[]{:S(2)}, u32[]{:S(2)}) %collective-permute-start.12) | collective-permute-done | bytes 229408 | tf_op jit(solution)/shard_map/ppermute | solution.py:28
  95.1 4.9 %collective-permute-done.14 = bf16[8,16,896]{2,1,0:T(8,128)(2,1)S(1)} collective-permute-done((bf16[8,16,896]{2,1,0:T(8,128)(2,1)S(1)}, bf16[8,16,896]{2,1,0:T(8,128)(2,1)S(1)}, u32[]{:S(2)}, u32[]{:S(2)}) %collective-permute-start.14) | collective-permute-done | bytes 229408 | tf_op jit(solution)/shard_map/ppermute | solution.py:28
  101.2 1.8 %queries.1.refs_8_ = bf16[256,256]{1,0:T(8,128)(2,1)S(1)} custom-call(s32[8]{0:T(128)S(1)} %stack.35.order, bf16[256,512]{1,0:T(8,128)(2,1)S(1)} %copy-done.3, bf16[256,512]{1,0:T(8,128)(2,1)} %collective-permute-done.18.refs_1_, bf16[256,512]{1,0:T(8,128)(2,1)S(1)} %collective-permute-done.19.refs_2_, bf16[256,512]{1,0:T(8,128)(2,1)S(1)} %collective-permute-done.20.refs_3_, ...), custom_call_target="tpu_custom_call" | custom-call | flops 536870912 | bytes 4325376 | tf_op jit(solution)/shard_map/queries/pallas_call | solution.py:61
  103.1 2.4 %attend.1.refs_0_ = bf16[256,256]{1,0:T(8,128)(2,1)S(1)} custom-call(bf16[4,32,896]{2,1,0:T(8,128)(2,1)S(1)} %bitcast.47, bf16[4,32,896]{2,1,0:T(8,128)(2,1)S(1)} %bitcast.51, bf16[4,32,896]{2,1,0:T(8,128)(2,1)S(1)} %bitcast.48, bf16[4,32,896]{2,1,0:T(8,128)(2,1)S(1)} %bitcast.52, bf16[4,32,896]{2,1,0:T(8,128)(2,1)S(1)} %bitcast.49, ...), custom_call_target="tpu_custom_call" | custom-call | flops 1006632960 | bytes 3014656 | tf_op jit(solution)/shard_map/attend/pallas_call | solution.py:173
  106.5 2.1 %collective-permute-start.28 = (bf16[256,256]{1,0:T(8,128)(2,1)S(1)}, bf16[256,256]{1,0:T(8,128)(2,1)S(1)}, u32[]{:S(2)}, u32[]{:S(2)}) collective-permute-start(bf16[256,256]{1,0:T(8,128)(2,1)S(1)} %attend.1.refs_0_), channel_id=1, source_target_pairs={{0,4},{1,5},{2,6},{3,7},{4,0},{5,1},{6,2},{7,3},{8,12},{9,13},{10,... | collective-permute-start | bytes 393224 | tf_op jit(solution)/shard_map/ppermute | solution.py:28
  112.7 2.4 %collective-permute-done.28.refs_4_ = bf16[256,256]{1,0:T(8,128)(2,1)S(1)} collective-permute-done((bf16[256,256]{1,0:T(8,128)(2,1)S(1)}, bf16[256,256]{1,0:T(8,128)(2,1)S(1)}, u32[]{:S(2)}, u32[]{:S(2)}) %collective-permute-start.28) | collective-permute-done | bytes 131104 | tf_op jit(solution)/shard_map/ppermute | solution.py:28
  117.2 2.0 %project.1 = bf16[256,512]{1,0:T(8,128)(2,1)} custom-call(s32[8]{0:T(128)S(1)} %stack.35.order, bf16[256,256]{1,0:T(8,128)(2,1)S(1)} %attend.1.refs_0_, bf16[256,256]{1,0:T(8,128)(2,1)S(1)} %collective-permute-done.25.refs_1_, bf16[256,256]{1,0:T(8,128)(2,1)S(1)} %collective-permute-done.26.refs_2_, bf16[256,256]{1,0:T(8,128)(2,1)S(1)} %collective-permute-done.27.refs_3_, ...), custom_call_target="tpu_custom_call" | custom-call | flops 536870912 | bytes 3407872 | tf_op jit(solution)/shard_map/project/pallas_call | solution.py:61
  (101 shorter events, 30.3 us)
Async XLA Ops:
  2.9 20.4 %all-to-all-start = ((s32[32,1,2]{2,1,0:T(1,128)}), s32[32,1,2]{2,1,0:T(1,128)S(1)}, u32[]{:S(2)}, u32[]{:S(2)}) async-start(s32[32,1,2]{2,1,0:T(1,128)} %bitcast.8), calls=%async_computation | async-start | bytes 32768 | tf_op jit(solution)/shard_map/all_to_all | solution.py:213
  27.1 47.2 %all-to-all-start.1 = ((bf16[64,16,896]{2,1,0:T(8,128)(2,1)}), bf16[64,16,896]{2,1,0:T(8,128)(2,1)}, u32[]{:S(2)}, u32[]{:S(2)}) async-start(bf16[64,16,896]{2,1,0:T(8,128)(2,1)} %broadcast_select_fusion), calls=%async_computation.1 | async-start | bytes 3670016 | tf_op jit(solution)/shard_map/all_to_all | solution.py:216
  34.7 25.0 %collective-permute-start.19 = (bf16[256,512]{1,0:T(8,128)(2,1)S(1)}, bf16[256,512]{1,0:T(8,128)(2,1)S(1)}, u32[]{:S(2)}, u32[]{:S(2)}) collective-permute-start(bf16[256,512]{1,0:T(8,128)(2,1)S(1)} %copy-done.3), channel_id=1, source_target_pairs={{0,2},{1,3},{2,4},{3,5},{4,6},{5,7},{6,0},{7,1},{8,10},{9,11},{10,... | collective-permute-start | bytes 786440 | tf_op jit(solution)/shard_map/ppermute | solution.py:28
  36.0 24.3 %collective-permute-start.21 = (bf16[256,512]{1,0:T(8,128)(2,1)S(1)}, bf16[256,512]{1,0:T(8,128)(2,1)}, u32[]{:S(2)}, u32[]{:S(2)}) collective-permute-start(bf16[256,512]{1,0:T(8,128)(2,1)S(1)} %copy-done.3), channel_id=1, source_target_pairs={{0,4},{1,5},{2,6},{3,7},{4,0},{5,1},{6,2},{7,3},{8,12},{9,13},{10,... | collective-permute-start | bytes 786440 | tf_op jit(solution)/shard_map/ppermute | solution.py:28
  40.2 13.1 %collective-permute-start.3 = (f32[32,896]{1,0:T(8,128)}, f32[32,896]{1,0:T(8,128)}, u32[]{:S(2)}, u32[]{:S(2)}) collective-permute-start(f32[32,896]{1,0:T(8,128)} %get-tuple-element.8), channel_id=1, source_target_pairs={{0,4},{1,5},{2,6},{3,7},{4,0},{5,1},{6,2},{7,3},{8,12},{9,13},{10,... | collective-permute-start | bytes 344072 | tf_op jit(solution)/shard_map/ppermute | solution.py:28
  40.6 12.6 %collective-permute-start.2 = (f32[32,896]{1,0:T(8,128)}, f32[32,896]{1,0:T(8,128)}, u32[]{:S(2)}, u32[]{:S(2)}) collective-permute-start(f32[32,896]{1,0:T(8,128)} %get-tuple-element.9), channel_id=1, source_target_pairs={{0,6},{1,7},{2,0},{3,1},{4,2},{5,3},{6,4},{7,5},{8,14},{9,15},{10,... | collective-permute-start | bytes 344072 | tf_op jit(solution)/shard_map/ppermute | solution.py:28
  42.0 14.1 %collective-permute-start.1 = (f32[32,896]{1,0:T(8,128)}, f32[32,896]{1,0:T(8,128)}, u32[]{:S(2)}, u32[]{:S(2)}) collective-permute-start(f32[32,896]{1,0:T(8,128)} %get-tuple-element.7), channel_id=1, source_target_pairs={{0,2},{1,3},{2,4},{3,5},{4,6},{5,7},{6,0},{7,1},{8,10},{9,11},{10,... | collective-permute-start | bytes 344072 | tf_op jit(solution)/shard_map/ppermute | solution.py:28
  58.2 6.4 %collective-permute-start.5 = (bf16[32,896]{1,0:T(8,128)(2,1)}, bf16[32,896]{1,0:T(8,128)(2,1)}, u32[]{:S(2)}, u32[]{:S(2)}) collective-permute-start(bf16[32,896]{1,0:T(8,128)(2,1)} %fusion.2.refs_0_), channel_id=1, source_target_pairs={{0,2},{1,3},{2,4},{3,5},{4,6},{5,7},{6,0},{7,1},{8,10},{9,11},{10,... | collective-permute-start | bytes 172040 | tf_op jit(solution)/shard_map/ppermute | solution.py:28
  58.2 7.1 %collective-permute-start.7 = (bf16[32,896]{1,0:T(8,128)(2,1)}, bf16[32,896]{1,0:T(8,128)(2,1)}, u32[]{:S(2)}, u32[]{:S(2)}) collective-permute-start(bf16[32,896]{1,0:T(8,128)(2,1)} %fusion.2.refs_0_), channel_id=1, source_target_pairs={{0,4},{1,5},{2,6},{3,7},{4,0},{5,1},{6,2},{7,3},{8,12},{9,13},{10,... | collective-permute-start | bytes 172040 | tf_op jit(solution)/shard_map/ppermute | solution.py:28
  59.8 27.3 %collective-permute-start.18 = (bf16[256,512]{1,0:T(8,128)(2,1)S(1)}, bf16[256,512]{1,0:T(8,128)(2,1)}, u32[]{:S(2)}, u32[]{:S(2)}) collective-permute-start(bf16[256,512]{1,0:T(8,128)(2,1)S(1)} %copy-done.3), channel_id=1, source_target_pairs={{0,1},{1,0},{2,3},{3,2},{4,5},{5,4},{6,7},{7,6},{8,9},{9,8},{10,11... | collective-permute-start | bytes 786440 | tf_op jit(solution)/shard_map/ppermute | solution.py:32
  60.3 29.4 %collective-permute-start.23 = (bf16[256,512]{1,0:T(8,128)(2,1)S(1)}, bf16[256,512]{1,0:T(8,128)(2,1)}, u32[]{:S(2)}, u32[]{:S(2)}) collective-permute-start(bf16[256,512]{1,0:T(8,128)(2,1)S(1)} %copy-done.3), channel_id=1, source_target_pairs={{0,6},{1,7},{2,0},{3,1},{4,2},{5,3},{6,4},{7,5},{8,14},{9,15},{10,... | collective-permute-start | bytes 786440 | tf_op jit(solution)/shard_map/ppermute | solution.py:28
  62.1 14.9 %collective-permute-start.9 = (bf16[32,896]{1,0:T(8,128)(2,1)}, bf16[32,896]{1,0:T(8,128)(2,1)}, u32[]{:S(2)}, u32[]{:S(2)}) collective-permute-start(bf16[32,896]{1,0:T(8,128)(2,1)} %fusion.2.refs_0_), channel_id=1, source_target_pairs={{0,6},{1,7},{2,0},{3,1},{4,2},{5,3},{6,4},{7,5},{8,14},{9,15},{10,... | collective-permute-start | bytes 172040 | tf_op jit(solution)/shard_map/ppermute | solution.py:28
  64.6 16.0 %collective-permute-start.6 = (bf16[32,896]{1,0:T(8,128)(2,1)}, bf16[32,896]{1,0:T(8,128)(2,1)}, u32[]{:S(2)}, u32[]{:S(2)}) collective-permute-start(bf16[32,896]{1,0:T(8,128)(2,1)} %collective-permute-done.5.refs_2_), channel_id=1, source_target_pairs={{0,1},{1,0},{2,3},{3,2},{4,5},{5,4},{6,7},{7,6},{8,9},{9,8},{10,11... | collective-permute-start | bytes 172040 | tf_op jit(solution)/shard_map/ppermute | solution.py:32
  65.3 15.3 %collective-permute-start.8 = (bf16[32,896]{1,0:T(8,128)(2,1)}, bf16[32,896]{1,0:T(8,128)(2,1)}, u32[]{:S(2)}, u32[]{:S(2)}) collective-permute-start(bf16[32,896]{1,0:T(8,128)(2,1)} %collective-permute-done.7.refs_4_), channel_id=1, source_target_pairs={{0,1},{1,0},{2,3},{3,2},{4,5},{5,4},{6,7},{7,6},{8,9},{9,8},{10,11... | collective-permute-start | bytes 172040 | tf_op jit(solution)/shard_map/ppermute | solution.py:32
  77.1 13.7 %collective-permute-start.20 = (bf16[256,512]{1,0:T(8,128)(2,1)S(1)}, bf16[256,512]{1,0:T(8,128)(2,1)S(1)}, u32[]{:S(2)}, u32[]{:S(2)}) collective-permute-start(bf16[256,512]{1,0:T(8,128)(2,1)S(1)} %collective-permute-done.19.refs_2_), channel_id=1, source_target_pairs={{0,1},{1,0},{2,3},{3,2},{4,5},{5,4},{6,7},{7,6},{8,9},{9,8},{10,11... | collective-permute-start | bytes 786440 | tf_op jit(solution)/shard_map/ppermute | solution.py:32
  80.6 11.4 %collective-permute-start.22 = (bf16[256,512]{1,0:T(8,128)(2,1)}, bf16[256,512]{1,0:T(8,128)(2,1)S(1)}, u32[]{:S(2)}, u32[]{:S(2)}) collective-permute-start(bf16[256,512]{1,0:T(8,128)(2,1)} %collective-permute-done.21.refs_4_), channel_id=1, source_target_pairs={{0,1},{1,0},{2,3},{3,2},{4,5},{5,4},{6,7},{7,6},{8,9},{9,8},{10,11... | collective-permute-start | bytes 786440 | tf_op jit(solution)/shard_map/ppermute | solution.py:32
  85.7 8.2 %collective-permute-start.12 = (bf16[8,16,896]{2,1,0:T(8,128)(2,1)S(1)}, bf16[8,16,896]{2,1,0:T(8,128)(2,1)S(1)}, u32[]{:S(2)}, u32[]{:S(2)}) collective-permute-start(bf16[8,16,896]{2,1,0:T(8,128)(2,1)S(1)} %encode.1), channel_id=1, source_target_pairs={{0,2},{1,3},{2,4},{3,5},{4,6},{5,7},{6,0},{7,1},{8,10},{9,11},{10,... | collective-permute-start | bytes 688136 | tf_op jit(solution)/shard_map/ppermute | solution.py:28
  87.1 12.9 %collective-permute-start.14 = (bf16[8,16,896]{2,1,0:T(8,128)(2,1)S(1)}, bf16[8,16,896]{2,1,0:T(8,128)(2,1)S(1)}, u32[]{:S(2)}, u32[]{:S(2)}) collective-permute-start(bf16[8,16,896]{2,1,0:T(8,128)(2,1)S(1)} %encode.1), channel_id=1, source_target_pairs={{0,4},{1,5},{2,6},{3,7},{4,0},{5,1},{6,2},{7,3},{8,12},{9,13},{10,... | collective-permute-start | bytes 688136 | tf_op jit(solution)/shard_map/ppermute | solution.py:28
  89.7 11.5 %collective-permute-start.16 = (bf16[8,16,896]{2,1,0:T(8,128)(2,1)S(1)}, bf16[8,16,896]{2,1,0:T(8,128)(2,1)S(1)}, u32[]{:S(2)}, u32[]{:S(2)}) collective-permute-start(bf16[8,16,896]{2,1,0:T(8,128)(2,1)S(1)} %encode.1), channel_id=1, source_target_pairs={{0,6},{1,7},{2,0},{3,1},{4,2},{5,3},{6,4},{7,5},{8,14},{9,15},{10,... | collective-permute-start | bytes 688136 | tf_op jit(solution)/shard_map/ppermute | solution.py:28
  90.8 10.4 %collective-permute-start.24 = (bf16[256,512]{1,0:T(8,128)(2,1)}, bf16[256,512]{1,0:T(8,128)(2,1)S(1)}, u32[]{:S(2)}, u32[]{:S(2)}) collective-permute-start(bf16[256,512]{1,0:T(8,128)(2,1)} %collective-permute-done.23.refs_6_), channel_id=1, source_target_pairs={{0,1},{1,0},{2,3},{3,2},{4,5},{5,4},{6,7},{7,6},{8,9},{9,8},{10,11... | collective-permute-start | bytes 786440 | tf_op jit(solution)/shard_map/ppermute | solution.py:32
  92.0 11.0 %collective-permute-start.11 = (bf16[8,16,896]{2,1,0:T(8,128)(2,1)S(1)}, bf16[8,16,896]{2,1,0:T(8,128)(2,1)S(1)}, u32[]{:S(2)}, u32[]{:S(2)}) collective-permute-start(bf16[8,16,896]{2,1,0:T(8,128)(2,1)S(1)} %encode.1), channel_id=1, source_target_pairs={{0,1},{1,0},{2,3},{3,2},{4,5},{5,4},{6,7},{7,6},{8,9},{9,8},{10,11... | collective-permute-start | bytes 688136 | tf_op jit(solution)/shard_map/ppermute | solution.py:32
  93.9 9.1 %collective-permute-start.13 = (bf16[8,16,896]{2,1,0:T(8,128)(2,1)S(1)}, bf16[8,16,896]{2,1,0:T(8,128)(2,1)S(1)}, u32[]{:S(2)}, u32[]{:S(2)}) collective-permute-start(bf16[8,16,896]{2,1,0:T(8,128)(2,1)S(1)} %collective-permute-done.12), channel_id=1, source_target_pairs={{0,1},{1,0},{2,3},{3,2},{4,5},{5,4},{6,7},{7,6},{8,9},{9,8},{10,11... | collective-permute-start | bytes 688136 | tf_op jit(solution)/shard_map/ppermute | solution.py:32
  106.5 8.6 %collective-permute-start.28 = (bf16[256,256]{1,0:T(8,128)(2,1)S(1)}, bf16[256,256]{1,0:T(8,128)(2,1)S(1)}, u32[]{:S(2)}, u32[]{:S(2)}) collective-permute-start(bf16[256,256]{1,0:T(8,128)(2,1)S(1)} %attend.1.refs_0_), channel_id=1, source_target_pairs={{0,4},{1,5},{2,6},{3,7},{4,0},{5,1},{6,2},{7,3},{8,12},{9,13},{10,... | collective-permute-start | bytes 393224 | tf_op jit(solution)/shard_map/ppermute | solution.py:28
  108.6 7.3 %collective-permute-start.30 = (bf16[256,256]{1,0:T(8,128)(2,1)S(1)}, bf16[256,256]{1,0:T(8,128)(2,1)S(1)}, u32[]{:S(2)}, u32[]{:S(2)}) collective-permute-start(bf16[256,256]{1,0:T(8,128)(2,1)S(1)} %attend.1.refs_0_), channel_id=1, source_target_pairs={{0,6},{1,7},{2,0},{3,1},{4,2},{5,3},{6,4},{7,5},{8,14},{9,15},{10,... | collective-permute-start | bytes 393224 | tf_op jit(solution)/shard_map/ppermute | solution.py:28
  (20 other events, 195.9 us)

commit v2 on v1

v2 whole, which is shorter than its diff:
```python
import functools
import math

import jax
import jax.numpy as jnp
from jax import lax
from jax.experimental import pallas as pl
from jax.experimental.pallas import tpu as pltpu
from jax.sharding import PartitionSpec as P

HD = 128
E = 896
CL = 64
NL = 128
KN = 2
EHD = 128
NX, NZ, NY, NC = 4, 8, 4, 2
NS = NX * NZ
NH = NY * NC
STORE_DEV = 16
SLOTS = 8
ROWS = NL // NH
PIECES = ((0, 512), (512, 896))
BF = jnp.bfloat16
F32 = jnp.float32

VMEM = pl.BlockSpec(memory_space=pltpu.VMEM)
SMEM = pl.BlockSpec(memory_space=pltpu.SMEM)
ANY = pl.BlockSpec(memory_space=pl.ANY)


def without(count, at, kernel, *refs):
    kernel(*refs[:at], *refs[at + count :])


def whole(body, arrays, outs, name, lists=(), after=(), scratch=(), limit=8):
    size = sum(a.size * a.dtype.itemsize for a in [*arrays, *outs])
    return pl.pallas_call(
        functools.partial(without, len(after), len(lists) + len(arrays), body),
        out_shape=outs,
        in_specs=[SMEM] * len(lists) + [VMEM] * len(arrays) + [ANY] * len(after),
        out_specs=[VMEM] * len(outs),
        scratch_shapes=scratch,
        compiler_params=pltpu.CompilerParams(vmem_limit_bytes=limit * 2**20),
        cost_estimate=pl.CostEstimate(flops=0, bytes_accessed=size, transcendentals=0),
        name=name,
    )(*lists, *arrays, *after)


def y_shift(a, r):
    pairs = [(y * NC + c, ((y + r) % NY) * NC + c) for y in range(NY) for c in range(NC)]
    return lax.ppermute(a, "head", pairs)


def core_swap(a):
    return lax.ppermute(a, "head", [(h, h ^ 1) for h in range(NH)])


def z_shift(a, r):
    pairs = [(x * NZ + z, x * NZ + (z + r) % NZ) for x in range(NX) for z in range(NZ)]
    return lax.ppermute(a, "seq", pairs)


def x_shift(a, r):
    pairs = [(x * NZ + z, ((x + r) % NX) * NZ + z) for x in range(NX) for z in range(NZ)]
    return lax.ppermute(a, "seq", pairs)


def far_shift(a):
    pairs = []
    for x in range(NX):
        for z in range(NZ):
            for h in range(NH):
                step = 2 if h % NC else -2
                pairs.append(((x * NZ + z) * NH + h, (x * NZ + (z + step) % NZ) * NH + h))
    return lax.ppermute(a, ("seq", "head"), pairs)


def chip_blocks(a):
    one, three, two = [y_shift(a, r) for r in (1, 3, 2)]
    return [a, one, two, three]


def chip_blocks_in_turn(a):
    one, three = y_shift(a, 1), y_shift(a, 3)
    return [a, one, y_shift(one, 1), three]


def with_swaps(blocks):
    return [b for own in blocks for b in (own, core_swap(own))]


def source_head(k):
    head = lax.axis_index("head")
    y, c = head // NC, head % NC
    return ((y - k // NC + NY) % NY) * NC + (c if k % NC == 0 else 1 - c)


def partial_kernel(tokens, weight, mine, theirs):
    c = lax.axis_index("head") % NC
    total = jnp.dot(tokens[...], weight[...], preferred_element_type=F32)
    parts = total.reshape(NY, NC, -1, E)
    mine[...] = jnp.where(c == 0, parts[:, 0], parts[:, 1])
    theirs[...] = jnp.where(c == 0, parts[:, 1], parts[:, 0])


def chip_sum_kernel(mine, received, *outs):
    y = lax.axis_index("head") // NC
    for r, out in enumerate(outs):
        to = (y + r) % NY
        out[...] = mine[to] + received[to]


def pack_kernel(one, two, three, four, tokens, out):
    rows = tokens.shape[0]
    part = one.shape[0]
    out[:rows] = tokens[...]
    context = (one[...] + two[...] + three[...] + four[...]).astype(BF)
    for i, (first, last) in enumerate(PIECES):
        start = rows + i * part
        out[start : start + part, : last - first] = context[:, first:last]


def packed_context(tokens, weight, after):
    rows, width = tokens.shape
    part = rows // NH
    half = jax.ShapeDtypeStruct((NY, part, E), F32)
    mine, theirs = whole(partial_kernel, [tokens, weight], [half, half], "partial", after=after)
    outs = [jax.ShapeDtypeStruct((part, E), F32)] * NY
    own, *sent = whole(chip_sum_kernel, [mine, core_swap(theirs)], outs, "chip_sum")
    received = [y_shift(sent[r - 1], r) for r in (1, 3, 2)]
    out = jax.ShapeDtypeStruct((rows + len(PIECES) * part, width), BF)
    return whole(pack_kernel, [own, *received, tokens], [out], "pack")[0]


def z_lists(lists, shifts):
    for r in shifts:
        lists = jnp.concatenate([lists, z_shift(lists, r)], axis=0)
    return lists


def slab_of(store):
    own = lax.dynamic_slice_in_dim(store, lax.axis_index("head") * ROWS, ROWS, axis=1)
    one, three, two = [x_shift(own, r) for r in (1, 3, 2)]
    return [own, one, two, three]


def locate(value):
    seq = lax.axis_index("seq")
    shard = value // STORE_DEV
    away = (shard % NZ - seq % NZ + NZ) % NZ
    back = (seq // NZ - shard // NZ + NX) % NX
    return away, back, value % STORE_DEV


def from_slab(slab, back, row):
    value = slab[0][row]
    for r in range(1, NX):
        value = jnp.where(back == r, slab[r][row], value)
    return value


def first_kernel(look, s0, s1, s2, s3, minus, plus, far):
    slab = (s0, s1, s2, s3)
    for k, out, base in [
        (1, minus, 0),
        (3, minus, SLOTS),
        (7, plus, 0),
        (5, plus, SLOTS),
        (4, far, 0),
    ]:
        for q in range(SLOTS):
            _, back, row = locate(look[k, q])
            out[base + q] = from_slab(slab, back, row)


def second_kernel(look, s0, s1, s2, s3, minus_in, plus_in, far_in, minus, plus, mine):
    slab = (s0, s1, s2, s3)
    for k, out, near, d in [(2, minus, minus_in, 1), (6, plus, plus_in, 7)]:
        for q in range(SLOTS):
            away, back, row = locate(look[k, q])
            value = jnp.where(away == d, near[SLOTS + q], far_in[q])
            out[q] = jnp.where(away == 0, from_slab(slab, back, row), value)
    for q in range(SLOTS):
        away, back, row = locate(look[0, q])
        value = jnp.where(away == 1, minus_in[q], plus_in[q])
        mine[q] = jnp.where(away == 0, from_slab(slab, back, row), value)


def slots(count):
    return jax.ShapeDtypeStruct((count, ROWS, E), BF)


def fetch(slab, look, before_first, before_second):
    outs = [slots(2 * SLOTS), slots(2 * SLOTS), slots(SLOTS)]
    minus, plus, far = whole(first_kernel, slab, outs, "first", [look], before_first)
    sent = [z_shift(minus, -1), z_shift(plus, 1), far_shift(far)]
    outs = [slots(SLOTS)] * 3
    minus, plus, mine = whole(second_kernel, slab + sent, outs, "second", [look], before_second)
    return [mine, z_shift(minus, -2), z_shift(plus, 2)]


def queries_kernel(*refs):
    blocks, w, (out, context) = refs[:NH], refs[NH], refs[NH + 1 :]
    rows = out.shape[0]
    part = context.shape[0] // NH
    depth = w.shape[0] // NH
    total = None
    for k in range(NH):
        start = pl.multiple_of(source_head(k) * depth, depth)
        dot = jnp.dot(blocks[k][:rows], w[pl.ds(start, depth), :], preferred_element_type=F32)
        total = dot if total is None else total + dot
        for i, (first, last) in enumerate(PIECES):
            at = rows + i * part
            context[k * part : (k + 1) * part, first:last] = blocks[k][at : at + part, : last - first]
    out[...] = total.astype(out.dtype)


def encode_kernel(look, mine, ahead_in, behind_in, ctx, out, nb):
    width = nb.shape[-1]
    part = ctx.shape[0] // NH
    core = lax.axis_index("head") % NC
    for q in range(SLOTS):
        away, _, _ = locate(look[0, q])
        ahead = (away == 2) | (away == 3) | ((away == 4) & (core == 0))
        near = (away == 0) | (away == 1) | (away == NZ - 1)
        nb[q] = jnp.where(near, mine[q], jnp.where(ahead, ahead_in[q], behind_in[q]))
    heads = range(width // EHD)
    for r in range(NY):
        span = source_head(NC * r) // NC
        context = ctx[NC * r * part : NC * (r + 1) * part]
        rows = nb[pl.ds(span * KN, KN)].reshape(KN * ROWS, width)
        scores = jnp.concatenate(
            [
                lax.dot_general(
                    rows[:, g * EHD : (g + 1) * EHD],
                    context[:, g * EHD : (g + 1) * EHD],
                    (((1,), (1,)), ((), ())),
                    preferred_element_type=F32,
                )
                for g in heads
            ],
            axis=0,
        ) * (1.0 / math.sqrt(EHD))
        weights = jnp.exp(scores - jnp.max(scores, axis=1, keepdims=True))
        weights = (weights / jnp.sum(weights, axis=1, keepdims=True)).astype(BF)
        mixed = jnp.concatenate(
            [
                jnp.dot(
                    weights[g * KN * ROWS : (g + 1) * KN * ROWS],
                    context[:, g * EHD : (g + 1) * EHD],
                    preferred_element_type=F32,
                )
                for g in heads
            ],
            axis=1,
        )
        encoded = (rows.astype(F32) + mixed).astype(BF)
        out[pl.ds(span * KN, KN)] = encoded.reshape(KN, ROWS, width)


def attend_kernel(*refs):
    blocks = refs[:NH]
    q_hbm, wk_hbm, wv_hbm, out, rows, q, wk, wv, sems = refs[NH:]
    spans = rows.shape[0]
    pairs = [(block, rows.at[:, k]) for k, block in enumerate(blocks)]
    pairs += [(wk_hbm, wk), (wv_hbm, wv), (q_hbm, q)]
    copies = [pltpu.make_async_copy(a, b, sems.at[i]) for i, (a, b) in enumerate(pairs)]
    for copy in copies:
        copy.start()
    for copy in copies:
        copy.wait()
    flat = rows[...].reshape(spans * KN * NL, E)
    keys = jnp.dot(flat, wk[...], preferred_element_type=F32).astype(BF)
    values = jnp.dot(flat, wv[...], preferred_element_type=F32).astype(BF)
    heads = q.shape[1] // HD
    span_rows = KN * NL
    units = [(s, h) for s in range(spans) for h in range(heads)]
    scores = jnp.concatenate(
        [
            lax.dot_general(
                q[s * CL : (s + 1) * CL, h * HD : (h + 1) * HD],
                keys[s * span_rows : (s + 1) * span_rows, h * HD : (h + 1) * HD],
                (((1,), (1,)), ((), ())),
                preferred_element_type=F32,
            )
            for s, h in units
        ],
        axis=0,
    ) * (1.0 / math.sqrt(HD))
    weights = jnp.exp(scores - jnp.max(scores, axis=1, keepdims=True))
    weights = (weights / jnp.sum(weights, axis=1, keepdims=True)).astype(BF)
    for i, (s, h) in enumerate(units):
        out[s * CL : (s + 1) * CL, h * HD : (h + 1) * HD] = jnp.dot(
            weights[i * CL : (i + 1) * CL],
            values[s * span_rows : (s + 1) * span_rows, h * HD : (h + 1) * HD],
            preferred_element_type=F32,
        ).astype(BF)


def attend(blocks, queries, key_weight, value_weight):
    tokens, width = queries.shape
    spans = tokens // CL
    blocks = [b.reshape(spans, KN * ROWS, E) for b in blocks]
    arrays = [queries, key_weight, value_weight]
    return pl.pallas_call(
        attend_kernel,
        out_shape=jax.ShapeDtypeStruct((tokens, width), BF),
        in_specs=[ANY] * (NH + 3),
        out_specs=VMEM,
        scratch_shapes=[
            pltpu.VMEM((spans, NH, KN * ROWS, E), BF),
            *[pltpu.VMEM(a.shape, BF) for a in arrays],
            pltpu.SemaphoreType.DMA((NH + 3,)),
        ],
        compiler_params=pltpu.CompilerParams(vmem_limit_bytes=14 * 2**20),
        cost_estimate=pl.CostEstimate(
            flops=4 * spans * KN * NL * E * width,
            bytes_accessed=2 * (spans * KN * NL * E + 2 * E * width + 2 * tokens * width),
            transcendentals=0,
        ),
        name="attend",
    )(*blocks, *arrays)


def project_kernel(*refs):
    blocks, w, out = refs[:NH], refs[NH], refs[NH + 1]
    depth = w.shape[0] // NH
    total = None
    for k in range(NH):
        start = pl.multiple_of(source_head(k) * depth, depth)
        dot = jnp.dot(blocks[k][...], w[pl.ds(start, depth), :], preferred_element_type=F32)
        total = dot if total is None else total + dot
    out[...] = total.astype(out.dtype)


def project(blocks, w):
    rows = blocks[0].shape[0]
    return pl.pallas_call(
        project_kernel,
        out_shape=jax.ShapeDtypeStruct((rows, w.shape[1]), BF),
        in_specs=[VMEM] * (NH + 1),
        out_specs=VMEM,
        compiler_params=pltpu.CompilerParams(vmem_limit_bytes=8 * 2**20),
        cost_estimate=pl.CostEstimate(
            flops=2 * rows * w.size, bytes_accessed=4 * w.size, transcendentals=0
        ),
        name="project",
    )(*blocks, w)


def local(
    tokens,
    neighbour_shard,
    neighbour_row,
    store_rows,
    context_weight,
    query_weight,
    key_weight,
    value_weight,
    output_weight,
):
    rows = tokens.shape[0]
    slab = slab_of(store_rows)
    own = (neighbour_shard * STORE_DEV + neighbour_row).reshape(1, SLOTS)
    look = z_lists(own, (1,))
    packed = packed_context(tokens, context_weight, [look])
    look = z_lists(look, (2, 4))
    chips = chip_blocks_in_turn(packed)
    fetched = fetch(slab, look, (), ())
    outs = [
        jax.ShapeDtypeStruct((rows, query_weight.shape[1]), BF),
        jax.ShapeDtypeStruct((rows, E), BF),
    ]
    queries, context = whole(
        queries_kernel, [*with_swaps(chips), query_weight], outs, "queries"
    )
    scratch = [pltpu.VMEM((SLOTS, ROWS, E), BF)]
    encoded = whole(
        encode_kernel, [*fetched, context], [slots(SLOTS)], "encode", [look], scratch=scratch
    )[0]
    attention = attend(with_swaps(chip_blocks(encoded)), queries, key_weight, value_weight)
    return project(with_swaps(chip_blocks(attention)), output_weight)


def solution(mesh):
    placed = (
        P("seq", "head"),
        P("seq", None),
        P("seq", None),
        P("seq", None, None),
        P("head", None),
        P(None, "head"),
        P(None, "head"),
        P(None, "head"),
        P(None, "head"),
    )
    return jax.shard_map(
        local, mesh=mesh, in_specs=placed, out_specs=P("seq", "head"), check_vma=False
    )
```

time: 120 us -> 109 us (0.908)
  local copies, waits for them, and re-layouts: 11.2 us -> 4.48 us
  starting transfers between devices: 49.9 us -> 55.6 us
  waiting for transfers between devices: 43.3 us -> 37.9 us
  other arithmetic: 5.36 us -> 0.73 us
  Pallas kernels: 8.64 us -> 10.4 us
    ppermute x0 -> x11, waiting for transfers between devices: none -> 24.3 us  [the longest x7 17 us: z_shift(): return lax.ppermute(a, 'seq', pairs)]
    ppermute x0 -> x11, starting transfers between devices: none -> 17.2 us  [the longest x7 12.3 us: z_shift(): return lax.ppermute(a, 'seq', pairs)]
    all_to_all x2 -> x0, starting transfers between devices: 16.7 us -> none  [the longest x1 11.9 us: fetch(): lax.all_to_all(row_buffer, 'seq', split_axis=0, concat_axis=0, tiled=True)]
    all_to_all x2 -> x0, waiting for transfers between devices: 16.3 us -> none  [the longest x1 8.8 us: fetch(): got = lax.all_to_all(sent, 'seq', split_axis=0, concat_axis=0, tiled=True)]
    ppermute x15 -> x12, waiting for transfers between devices: 25.6 us -> 11.1 us  [y_shift(): return lax.ppermute(a, 'head', pairs)]
    ppermute x17 -> x13, starting transfers between devices: 14.8 us -> 21.7 us  [core_swap(): return lax.ppermute(a, 'head', [(h, h ^ 1) for h in range(NH)])]
    gather x2 -> x0, local copies, waits for them, and re-layouts: 3.6 us -> none  [the longest x1 2.76 us: fetch(): return jnp.take(got, target, axis=0)]
    select_n x4 -> x0, other arithmetic: 2.52 us -> none  [the longest x2 1.48 us: fetch(): sent = jnp.take(slices, rows_in.reshape(NS * CAP), axis=0)]
  transfers between devices with their start and end apart: 34 -> 36, of which waited for: 12 -> 16; matrix products, arithmetic and copies ran while one was open for 7% -> 1% of each run, Pallas kernels for 4% -> 3%
where the time goes in v2:
time: 109 us
  starting transfers between devices  55.6 us (51%)
  waiting for transfers between devices  37.9 us (35%)
  Pallas kernels  10.4 us (10%)
  local copies, waits for them, and re-layouts  4.48 us (4%)
    ppermute x13, starting transfers between devices, core_swap(): return lax.ppermute(a, 'head', [(h, h ^ 1) for h in range(NH)])  21.7 us
    ppermute x7, waiting for transfers between devices, z_shift(): return lax.ppermute(a, 'seq', pairs)  17 us
    ppermute x12, starting transfers between devices, y_shift(): return lax.ppermute(a, 'head', pairs)  16.7 us
    ppermute x7, starting transfers between devices, z_shift(): return lax.ppermute(a, 'seq', pairs)  12.3 us
    ppermute x12, waiting for transfers between devices, y_shift(): return lax.ppermute(a, 'head', pairs)  11.1 us
    ppermute x1, waiting for transfers between devices, far_shift(): return lax.ppermute(a, ('seq', 'head'), pairs)  6.3 us
    pallas_call x7, Pallas kernels, whole(): pl.pallas_call(functools.partial(without, len(after), len(lists) + len(ar...  5.88 us
    ppermute x3, starting transfers between devices, x_shift(): return lax.ppermute(a, 'seq', pairs)  4.89 us
  transfers between devices with their start and end apart: 36, of which 16 were waited for; matrix products, arithmetic and copies ran while one was open for 1% of the time, Pallas kernels for 3%

profile of v2, /device:TPU:1, one launch (start us, length us, event | category | flops | bytes accessed | tf_op | source)
XLA Modules:
  0.0 109.3 jit_solution(17081584144116261537)
XLA Ops:
  0.9 2.5 %collective-permute-start = (s32[1,8]{1,0:T(1,128)S(1)}, s32[1,8]{1,0:T(1,128)S(1)}, u32[]{:S(2)}, u32[]{:S(2)}) collective-permute-start(s32[1,8]{1,0:T(1,128)S(1)} %reshape.27), channel_id=1, source_target_pairs={{0,8},{8,16},{16,24},{24,32},{32,40},{40,48},{48,56},{56,0},{64,72... | collective-permute-start | bytes 104 | tf_op jit(solution)/shard_map/ppermute | solution.py:61
  3.3 4.9 %collective-permute-done = s32[1,8]{1,0:T(1,128)S(1)} collective-permute-done((s32[1,8]{1,0:T(1,128)S(1)}, s32[1,8]{1,0:T(1,128)S(1)}, u32[]{:S(2)}, u32[]{:S(2)}) %collective-permute-start) | collective-permute-done | bytes 64 | tf_op jit(solution)/shard_map/ppermute | solution.py:61
  10.8 1.6 %collective-permute-start.11 = (f32[4,32,896]{2,1,0:T(8,128)S(1)}, f32[4,32,896]{2,1,0:T(8,128)S(1)}, u32[]{:S(2)}, u32[]{:S(2)}) collective-permute-start(f32[4,32,896]{2,1,0:T(8,128)S(1)} %get-tuple-element.26), channel_id=1, source_target_pairs={{0,1},{1,0},{2,3},{3,2},{4,5},{5,4},{6,7},{7,6},{8,9},{9,8},{10,11... | collective-permute-start | bytes 1376264 | tf_op jit(solution)/shard_map/ppermute | solution.py:56
  14.9 2.5 %collective-permute-start.4 = (bf16[16,16,896]{2,1,0:T(8,128)(2,1)S(1)}, bf16[16,16,896]{2,1,0:T(8,128)(2,1)S(1)}, u32[]{:S(2)}, u32[]{:S(2)}) collective-permute-start(bf16[16,16,896]{2,1,0:T(8,128)(2,1)S(1)} %constant_dynamic-slice_fusion.refs_1_), channel_id=1, source_target_pairs={{0,128},{8,136},{16,144},{24,152},{32,160},{40,168},{48,176},{56,1... | collective-permute-start | bytes 1376264 | tf_op jit(solution)/shard_map/ppermute | solution.py:66
  21.5 2.4 %collective-permute-done.12.refs_1_ = f32[32,896]{1,0:T(8,128)S(1)} collective-permute-done((f32[32,896]{1,0:T(8,128)S(1)}, f32[32,896]{1,0:T(8,128)S(1)}, u32[]{:S(2)}, u32[]{:S(2)}) %collective-permute-start.12) | collective-permute-done | bytes 114720 | tf_op jit(solution)/shard_map/ppermute | solution.py:52
  23.9 1.6 %collective-permute-start.14 = (f32[32,896]{1,0:T(8,128)S(1)}, f32[32,896]{1,0:T(8,128)S(1)}, u32[]{:S(2)}, u32[]{:S(2)}) collective-permute-start(f32[32,896]{1,0:T(8,128)S(1)} %get-tuple-element.30), channel_id=1, source_target_pairs={{0,4},{1,5},{2,6},{3,7},{4,0},{5,1},{6,2},{7,3},{8,12},{9,13},{10,... | collective-permute-start | bytes 344072 | tf_op jit(solution)/shard_map/ppermute | solution.py:52
  25.5 3.8 %collective-permute-done.14.refs_3_ = f32[32,896]{1,0:T(8,128)S(1)} collective-permute-done((f32[32,896]{1,0:T(8,128)S(1)}, f32[32,896]{1,0:T(8,128)S(1)}, u32[]{:S(2)}, u32[]{:S(2)}) %collective-permute-start.14) | collective-permute-done | bytes 114720 | tf_op jit(solution)/shard_map/ppermute | solution.py:52
  30.4 4.4 %collective-permute-start.2 = (s32[4,8]{1,0:T(4,128)S(1)}, s32[4,8]{1,0:T(4,128)S(1)}, u32[]{:S(2)}, u32[]{:S(2)}) collective-permute-start(s32[4,8]{1,0:T(4,128)S(1)} %pad_add_fusion.1), channel_id=1, source_target_pairs={{0,32},{8,40},{16,48},{24,56},{32,0},{40,8},{48,16},{56,24},{64,96... | collective-permute-start | bytes 392 | tf_op jit(solution)/shard_map/ppermute | solution.py:61
  34.8 2.1 %collective-permute-done.2 = s32[4,8]{1,0:T(4,128)S(1)} collective-permute-done((s32[4,8]{1,0:T(4,128)S(1)}, s32[4,8]{1,0:T(4,128)S(1)}, u32[]{:S(2)}, u32[]{:S(2)}) %collective-permute-start.2) | collective-permute-done | bytes 160 | tf_op jit(solution)/shard_map/ppermute | solution.py:61
  39.1 1.8 %collective-permute-start.6 = (bf16[16,16,896]{2,1,0:T(8,128)(2,1)S(1)}, bf16[16,16,896]{2,1,0:T(8,128)(2,1)S(1)}, u32[]{:S(2)}, u32[]{:S(2)}) collective-permute-start(bf16[16,16,896]{2,1,0:T(8,128)(2,1)S(1)} %get-tuple-element.19), channel_id=1, source_target_pairs={{0,56},{8,0},{16,8},{24,16},{32,24},{40,32},{48,40},{56,48},{64,12... | collective-permute-start | bytes 1376264 | tf_op jit(solution)/shard_map/ppermute | solution.py:61
  41.0 2.7 %collective-permute-start.20 = (bf16[320,512]{1,0:T(8,128)(2,1)S(1)}, bf16[320,512]{1,0:T(8,128)(2,1)S(1)}, u32[]{:S(2)}, u32[]{:S(2)}) collective-permute-start(bf16[320,512]{1,0:T(8,128)(2,1)S(1)} %pack.1.refs_0_), channel_id=1, source_target_pairs={{0,6},{1,7},{2,0},{3,1},{4,2},{5,3},{6,4},{7,5},{8,14},{9,15},{10,... | collective-permute-start | bytes 983048 | tf_op jit(solution)/shard_map/ppermute | solution.py:52
  43.7 6.3 %collective-permute-done.8.refs_7_ = bf16[8,16,896]{2,1,0:T(8,128)(2,1)S(1)} collective-permute-done((bf16[8,16,896]{2,1,0:T(8,128)(2,1)S(1)}, bf16[8,16,896]{2,1,0:T(8,128)(2,1)S(1)}, u32[]{:S(2)}, u32[]{:S(2)}) %collective-permute-start.8) | collective-permute-done | bytes 229408 | tf_op jit(solution)/shard_map/ppermute | solution.py:76
  50.0 6.6 %collective-permute-start.15 = (bf16[320,512]{1,0:T(8,128)(2,1)S(1)}, bf16[320,512]{1,0:T(8,128)(2,1)S(1)}, u32[]{:S(2)}, u32[]{:S(2)}) collective-permute-start(bf16[320,512]{1,0:T(8,128)(2,1)S(1)} %pack.1.refs_0_), channel_id=1, source_target_pairs={{0,1},{1,0},{2,3},{3,2},{4,5},{5,4},{6,7},{7,6},{8,9},{9,8},{10,11... | collective-permute-start | bytes 983048 | tf_op jit(solution)/shard_map/ppermute | solution.py:56
  59.1 3.7 %collective-permute-start.9 = (bf16[8,16,896]{2,1,0:T(8,128)(2,1)S(1)}, bf16[8,16,896]{2,1,0:T(8,128)(2,1)S(1)}, u32[]{:S(2)}, u32[]{:S(2)}) collective-permute-start(bf16[8,16,896]{2,1,0:T(8,128)(2,1)S(1)} %get-tuple-element.23), channel_id=1, source_target_pairs={{0,48},{8,56},{16,0},{24,8},{32,16},{40,24},{48,32},{56,40},{64,11... | collective-permute-start | bytes 688136 | tf_op jit(solution)/shard_map/ppermute | solution.py:61
  63.6 9.0 %collective-permute-done.9.refs_2_ = bf16[8,16,896]{2,1,0:T(8,128)(2,1)S(1)} collective-permute-done((bf16[8,16,896]{2,1,0:T(8,128)(2,1)S(1)}, bf16[8,16,896]{2,1,0:T(8,128)(2,1)S(1)}, u32[]{:S(2)}, u32[]{:S(2)}) %collective-permute-start.9) | collective-permute-done | bytes 229408 | tf_op jit(solution)/shard_map/ppermute | solution.py:61
  73.6 2.2 %encode.1 = bf16[8,16,896]{2,1,0:T(8,128)(2,1)S(1)} custom-call(s32[8,8]{1,0:T(8,128)S(1)} %pad_add_fusion.refs_0_, bf16[8,16,896]{2,1,0:T(8,128)(2,1)S(1)} %get-tuple-element.22.refs_1_, bf16[8,16,896]{2,1,0:T(8,128)(2,1)S(1)} %collective-permute-done.9.refs_2_, bf16[8,16,896]{2,1,0:T(8,128)(2,1)S(1)} %collective-permute-done.10.refs_3_, ...), custom_call_target="tpu_custom_call" | custom-call | bytes 1376256 | tf_op jit(solution)/shard_map/encode/pallas_call | solution.py:38
  77.3 2.6 %collective-permute-start.25 = (bf16[8,16,896]{2,1,0:T(8,128)(2,1)S(1)}, bf16[8,16,896]{2,1,0:T(8,128)(2,1)S(1)}, u32[]{:S(2)}, u32[]{:S(2)}) collective-permute-start(bf16[8,16,896]{2,1,0:T(8,128)(2,1)S(1)} %encode.1), channel_id=1, source_target_pairs={{0,4},{1,5},{2,6},{3,7},{4,0},{5,1},{6,2},{7,3},{8,12},{9,13},{10,... | collective-permute-start | bytes 688136 | tf_op jit(solution)/shard_map/ppermute | solution.py:52
  80.9 2.2 %collective-permute-start.22 = (bf16[8,16,896]{2,1,0:T(8,128)(2,1)S(1)}, bf16[8,16,896]{2,1,0:T(8,128)(2,1)S(1)}, u32[]{:S(2)}, u32[]{:S(2)}) collective-permute-start(bf16[8,16,896]{2,1,0:T(8,128)(2,1)S(1)} %encode.1), channel_id=1, source_target_pairs={{0,1},{1,0},{2,3},{3,2},{4,5},{5,4},{6,7},{7,6},{8,9},{9,8},{10,11... | collective-permute-start | bytes 688136 | tf_op jit(solution)/shard_map/ppermute | solution.py:56
  83.2 2.8 %collective-permute-start.24 = (bf16[8,16,896]{2,1,0:T(8,128)(2,1)S(1)}, bf16[8,16,896]{2,1,0:T(8,128)(2,1)S(1)}, u32[]{:S(2)}, u32[]{:S(2)}) collective-permute-start(bf16[8,16,896]{2,1,0:T(8,128)(2,1)S(1)} %collective-permute-done.23), channel_id=1, source_target_pairs={{0,1},{1,0},{2,3},{3,2},{4,5},{5,4},{6,7},{7,6},{8,9},{9,8},{10,11... | collective-permute-start | bytes 688136 | tf_op jit(solution)/shard_map/ppermute | solution.py:56
  86.0 3.1 %collective-permute-done.25 = bf16[8,16,896]{2,1,0:T(8,128)(2,1)S(1)} collective-permute-done((bf16[8,16,896]{2,1,0:T(8,128)(2,1)S(1)}, bf16[8,16,896]{2,1,0:T(8,128)(2,1)S(1)}, u32[]{:S(2)}, u32[]{:S(2)}) %collective-permute-start.25) | collective-permute-done | bytes 229408 | tf_op jit(solution)/shard_map/ppermute | solution.py:52
  89.1 2.3 %collective-permute-start.26 = (bf16[8,16,896]{2,1,0:T(8,128)(2,1)S(1)}, bf16[8,16,896]{2,1,0:T(8,128)(2,1)S(1)}, u32[]{:S(2)}, u32[]{:S(2)}) collective-permute-start(bf16[8,16,896]{2,1,0:T(8,128)(2,1)S(1)} %collective-permute-done.25), channel_id=1, source_target_pairs={{0,1},{1,0},{2,3},{3,2},{4,5},{5,4},{6,7},{7,6},{8,9},{9,8},{10,11... | collective-permute-start | bytes 688136 | tf_op jit(solution)/shard_map/ppermute | solution.py:56
  92.9 3.1 %attend.1.refs_0_ = bf16[256,256]{1,0:T(8,128)(2,1)S(1)} custom-call(bf16[4,32,896]{2,1,0:T(8,128)(2,1)S(1)} %bitcast.8, bf16[4,32,896]{2,1,0:T(8,128)(2,1)S(1)} %bitcast.12, bf16[4,32,896]{2,1,0:T(8,128)(2,1)S(1)} %bitcast.9, bf16[4,32,896]{2,1,0:T(8,128)(2,1)S(1)} %bitcast.13, bf16[4,32,896]{2,1,0:T(8,128)(2,1)S(1)} %bitcast.10, ...), custom_call_target="tpu_custom_call" | custom-call | flops 939524096 | bytes 3014656 | tf_op jit(solution)/shard_map/attend/pallas_call | solution.py:306
  96.9 2.1 %collective-permute-start.32 = (bf16[256,256]{1,0:T(8,128)(2,1)S(1)}, bf16[256,256]{1,0:T(8,128)(2,1)S(1)}, u32[]{:S(2)}, u32[]{:S(2)}) collective-permute-start(bf16[256,256]{1,0:T(8,128)(2,1)S(1)} %attend.1.refs_0_), channel_id=1, source_target_pairs={{0,4},{1,5},{2,6},{3,7},{4,0},{5,1},{6,2},{7,3},{8,12},{9,13},{10,... | collective-permute-start | bytes 393224 | tf_op jit(solution)/shard_map/ppermute | solution.py:52
  102.4 1.9 %collective-permute-start.31 = (bf16[256,256]{1,0:T(8,128)(2,1)S(1)}, bf16[256,256]{1,0:T(8,128)(2,1)S(1)}, u32[]{:S(2)}, u32[]{:S(2)}) collective-permute-start(bf16[256,256]{1,0:T(8,128)(2,1)S(1)} %collective-permute-done.30.refs_2_), channel_id=1, source_target_pairs={{0,1},{1,0},{2,3},{3,2},{4,5},{5,4},{6,7},{7,6},{8,9},{9,8},{10,11... | collective-permute-start | bytes 393224 | tf_op jit(solution)/shard_map/ppermute | solution.py:56
  (78 shorter events, 30.9 us)
Async XLA Ops:
  0.9 7.3 %collective-permute-start = (s32[1,8]{1,0:T(1,128)S(1)}, s32[1,8]{1,0:T(1,128)S(1)}, u32[]{:S(2)}, u32[]{:S(2)}) collective-permute-start(s32[1,8]{1,0:T(1,128)S(1)} %reshape.27), channel_id=1, source_target_pairs={{0,8},{8,16},{16,24},{24,32},{32,40},{40,48},{48,56},{56,0},{64,72... | collective-permute-start | bytes 104 | tf_op jit(solution)/shard_map/ppermute | solution.py:61
  10.8 7.7 %collective-permute-start.11 = (f32[4,32,896]{2,1,0:T(8,128)S(1)}, f32[4,32,896]{2,1,0:T(8,128)S(1)}, u32[]{:S(2)}, u32[]{:S(2)}) collective-permute-start(f32[4,32,896]{2,1,0:T(8,128)S(1)} %get-tuple-element.26), channel_id=1, source_target_pairs={{0,1},{1,0},{2,3},{3,2},{4,5},{5,4},{6,7},{7,6},{8,9},{9,8},{10,11... | collective-permute-start | bytes 1376264 | tf_op jit(solution)/shard_map/ppermute | solution.py:56
  13.6 23.2 %collective-permute-start.3 = (bf16[16,16,896]{2,1,0:T(8,128)(2,1)S(1)}, bf16[16,16,896]{2,1,0:T(8,128)(2,1)S(1)}, u32[]{:S(2)}, u32[]{:S(2)}) collective-permute-start(bf16[16,16,896]{2,1,0:T(8,128)(2,1)S(1)} %constant_dynamic-slice_fusion.refs_1_), channel_id=1, source_target_pairs={{0,64},{8,72},{16,80},{24,88},{32,96},{40,104},{48,112},{56,120},{... | collective-permute-start | bytes 1376264 | tf_op jit(solution)/shard_map/ppermute | solution.py:66
  14.9 22.9 %collective-permute-start.4 = (bf16[16,16,896]{2,1,0:T(8,128)(2,1)S(1)}, bf16[16,16,896]{2,1,0:T(8,128)(2,1)S(1)}, u32[]{:S(2)}, u32[]{:S(2)}) collective-permute-start(bf16[16,16,896]{2,1,0:T(8,128)(2,1)S(1)} %constant_dynamic-slice_fusion.refs_1_), channel_id=1, source_target_pairs={{0,128},{8,136},{16,144},{24,152},{32,160},{40,168},{48,176},{56,1... | collective-permute-start | bytes 1376264 | tf_op jit(solution)/shard_map/ppermute | solution.py:66
  17.4 20.5 %collective-permute-start.5 = (bf16[16,16,896]{2,1,0:T(8,128)(2,1)S(1)}, bf16[16,16,896]{2,1,0:T(8,128)(2,1)S(1)}, u32[]{:S(2)}, u32[]{:S(2)}) collective-permute-start(bf16[16,16,896]{2,1,0:T(8,128)(2,1)S(1)} %constant_dynamic-slice_fusion.refs_1_), channel_id=1, source_target_pairs={{0,192},{8,200},{16,208},{24,216},{32,224},{40,232},{48,240},{56,2... | collective-permute-start | bytes 1376264 | tf_op jit(solution)/shard_map/ppermute | solution.py:66
  30.3 13.4 %collective-permute-start.16 = (bf16[320,512]{1,0:T(8,128)(2,1)S(1)}, bf16[320,512]{1,0:T(8,128)(2,1)S(1)}, u32[]{:S(2)}, u32[]{:S(2)}) collective-permute-start(bf16[320,512]{1,0:T(8,128)(2,1)S(1)} %pack.1.refs_0_), channel_id=1, source_target_pairs={{0,2},{1,3},{2,4},{3,5},{4,6},{5,7},{6,0},{7,1},{8,10},{9,11},{10,... | collective-permute-start | bytes 983048 | tf_op jit(solution)/shard_map/ppermute | solution.py:52
  30.4 6.4 %collective-permute-start.2 = (s32[4,8]{1,0:T(4,128)S(1)}, s32[4,8]{1,0:T(4,128)S(1)}, u32[]{:S(2)}, u32[]{:S(2)}) collective-permute-start(s32[4,8]{1,0:T(4,128)S(1)} %pad_add_fusion.1), channel_id=1, source_target_pairs={{0,32},{8,40},{16,48},{24,56},{32,0},{40,8},{48,16},{56,24},{64,96... | collective-permute-start | bytes 392 | tf_op jit(solution)/shard_map/ppermute | solution.py:61
  39.1 17.5 %collective-permute-start.6 = (bf16[16,16,896]{2,1,0:T(8,128)(2,1)S(1)}, bf16[16,16,896]{2,1,0:T(8,128)(2,1)S(1)}, u32[]{:S(2)}, u32[]{:S(2)}) collective-permute-start(bf16[16,16,896]{2,1,0:T(8,128)(2,1)S(1)} %get-tuple-element.19), channel_id=1, source_target_pairs={{0,56},{8,0},{16,8},{24,16},{32,24},{40,32},{48,40},{56,48},{64,12... | collective-permute-start | bytes 1376264 | tf_op jit(solution)/shard_map/ppermute | solution.py:61
  41.0 9.1 %collective-permute-start.8 = (bf16[8,16,896]{2,1,0:T(8,128)(2,1)S(1)}, bf16[8,16,896]{2,1,0:T(8,128)(2,1)S(1)}, u32[]{:S(2)}, u32[]{:S(2)}) collective-permute-start(bf16[8,16,896]{2,1,0:T(8,128)(2,1)S(1)} %get-tuple-element.21), channel_id=1, source_target_pairs={{0,48},{1,17},{2,50},{3,19},{4,52},{5,21},{6,54},{7,23},{8,56},{9,... | collective-permute-start | bytes 688136 | tf_op jit(solution)/shard_map/ppermute | solution.py:76
  41.0 17.0 %collective-permute-start.7 = (bf16[16,16,896]{2,1,0:T(8,128)(2,1)S(1)}, bf16[16,16,896]{2,1,0:T(8,128)(2,1)S(1)}, u32[]{:S(2)}, u32[]{:S(2)}) collective-permute-start(bf16[16,16,896]{2,1,0:T(8,128)(2,1)S(1)} %get-tuple-element.20), channel_id=1, source_target_pairs={{0,8},{8,16},{16,24},{24,32},{32,40},{40,48},{48,56},{56,0},{64,72... | collective-permute-start | bytes 1376264 | tf_op jit(solution)/shard_map/ppermute | solution.py:61
  41.0 15.7 %collective-permute-start.20 = (bf16[320,512]{1,0:T(8,128)(2,1)S(1)}, bf16[320,512]{1,0:T(8,128)(2,1)S(1)}, u32[]{:S(2)}, u32[]{:S(2)}) collective-permute-start(bf16[320,512]{1,0:T(8,128)(2,1)S(1)} %pack.1.refs_0_), channel_id=1, source_target_pairs={{0,6},{1,7},{2,0},{3,1},{4,2},{5,3},{6,4},{7,5},{8,14},{9,15},{10,... | collective-permute-start | bytes 983048 | tf_op jit(solution)/shard_map/ppermute | solution.py:52
  43.7 13.4 %collective-permute-start.18 = (bf16[320,512]{1,0:T(8,128)(2,1)S(1)}, bf16[320,512]{1,0:T(8,128)(2,1)S(1)}, u32[]{:S(2)}, u32[]{:S(2)}) collective-permute-start(bf16[320,512]{1,0:T(8,128)(2,1)S(1)} %collective-permute-done.16.refs_2_), channel_id=1, source_target_pairs={{0,2},{1,3},{2,4},{3,5},{4,6},{5,7},{6,0},{7,1},{8,10},{9,11},{10,... | collective-permute-start | bytes 983048 | tf_op jit(solution)/shard_map/ppermute | solution.py:52
  50.0 12.8 %collective-permute-start.15 = (bf16[320,512]{1,0:T(8,128)(2,1)S(1)}, bf16[320,512]{1,0:T(8,128)(2,1)S(1)}, u32[]{:S(2)}, u32[]{:S(2)}) collective-permute-start(bf16[320,512]{1,0:T(8,128)(2,1)S(1)} %pack.1.refs_0_), channel_id=1, source_target_pairs={{0,1},{1,0},{2,3},{3,2},{4,5},{5,4},{6,7},{7,6},{8,9},{9,8},{10,11... | collective-permute-start | bytes 983048 | tf_op jit(solution)/shard_map/ppermute | solution.py:56
  59.1 13.5 %collective-permute-start.9 = (bf16[8,16,896]{2,1,0:T(8,128)(2,1)S(1)}, bf16[8,16,896]{2,1,0:T(8,128)(2,1)S(1)}, u32[]{:S(2)}, u32[]{:S(2)}) collective-permute-start(bf16[8,16,896]{2,1,0:T(8,128)(2,1)S(1)} %get-tuple-element.23), channel_id=1, source_target_pairs={{0,48},{8,56},{16,0},{24,8},{32,16},{40,24},{48,32},{56,40},{64,11... | collective-permute-start | bytes 688136 | tf_op jit(solution)/shard_map/ppermute | solution.py:61
  62.8 10.8 %collective-permute-start.10 = (bf16[8,16,896]{2,1,0:T(8,128)(2,1)S(1)}, bf16[8,16,896]{2,1,0:T(8,128)(2,1)S(1)}, u32[]{:S(2)}, u32[]{:S(2)}) collective-permute-start(bf16[8,16,896]{2,1,0:T(8,128)(2,1)S(1)} %get-tuple-element.24), channel_id=1, source_target_pairs={{0,16},{8,24},{16,32},{24,40},{32,48},{40,56},{48,0},{56,8},{64,80... | collective-permute-start | bytes 688136 | tf_op jit(solution)/shard_map/ppermute | solution.py:61
  75.8 7.4 %collective-permute-start.23 = (bf16[8,16,896]{2,1,0:T(8,128)(2,1)S(1)}, bf16[8,16,896]{2,1,0:T(8,128)(2,1)S(1)}, u32[]{:S(2)}, u32[]{:S(2)}) collective-permute-start(bf16[8,16,896]{2,1,0:T(8,128)(2,1)S(1)} %encode.1), channel_id=1, source_target_pairs={{0,2},{1,3},{2,4},{3,5},{4,6},{5,7},{6,0},{7,1},{8,10},{9,11},{10,... | collective-permute-start | bytes 688136 | tf_op jit(solution)/shard_map/ppermute | solution.py:52
  77.3 11.8 %collective-permute-start.25 = (bf16[8,16,896]{2,1,0:T(8,128)(2,1)S(1)}, bf16[8,16,896]{2,1,0:T(8,128)(2,1)S(1)}, u32[]{:S(2)}, u32[]{:S(2)}) collective-permute-start(bf16[8,16,896]{2,1,0:T(8,128)(2,1)S(1)} %encode.1), channel_id=1, source_target_pairs={{0,4},{1,5},{2,6},{3,7},{4,0},{5,1},{6,2},{7,3},{8,12},{9,13},{10,... | collective-permute-start | bytes 688136 | tf_op jit(solution)/shard_map/ppermute | solution.py:52
  80.0 11.5 %collective-permute-start.27 = (bf16[8,16,896]{2,1,0:T(8,128)(2,1)S(1)}, bf16[8,16,896]{2,1,0:T(8,128)(2,1)S(1)}, u32[]{:S(2)}, u32[]{:S(2)}) collective-permute-start(bf16[8,16,896]{2,1,0:T(8,128)(2,1)S(1)} %encode.1), channel_id=1, source_target_pairs={{0,6},{1,7},{2,0},{3,1},{4,2},{5,3},{6,4},{7,5},{8,14},{9,15},{10,... | collective-permute-start | bytes 688136 | tf_op jit(solution)/shard_map/ppermute | solution.py:52
  80.9 10.5 %collective-permute-start.22 = (bf16[8,16,896]{2,1,0:T(8,128)(2,1)S(1)}, bf16[8,16,896]{2,1,0:T(8,128)(2,1)S(1)}, u32[]{:S(2)}, u32[]{:S(2)}) collective-permute-start(bf16[8,16,896]{2,1,0:T(8,128)(2,1)S(1)} %encode.1), channel_id=1, source_target_pairs={{0,1},{1,0},{2,3},{3,2},{4,5},{5,4},{6,7},{7,6},{8,9},{9,8},{10,11... | collective-permute-start | bytes 688136 | tf_op jit(solution)/shard_map/ppermute | solution.py:56
  83.2 8.2 %collective-permute-start.24 = (bf16[8,16,896]{2,1,0:T(8,128)(2,1)S(1)}, bf16[8,16,896]{2,1,0:T(8,128)(2,1)S(1)}, u32[]{:S(2)}, u32[]{:S(2)}) collective-permute-start(bf16[8,16,896]{2,1,0:T(8,128)(2,1)S(1)} %collective-permute-done.23), channel_id=1, source_target_pairs={{0,1},{1,0},{2,3},{3,2},{4,5},{5,4},{6,7},{7,6},{8,9},{9,8},{10,11... | collective-permute-start | bytes 688136 | tf_op jit(solution)/shard_map/ppermute | solution.py:56
  96.1 6.3 %collective-permute-start.30 = (bf16[256,256]{1,0:T(8,128)(2,1)S(1)}, bf16[256,256]{1,0:T(8,128)(2,1)S(1)}, u32[]{:S(2)}, u32[]{:S(2)}) collective-permute-start(bf16[256,256]{1,0:T(8,128)(2,1)S(1)} %attend.1.refs_0_), channel_id=1, source_target_pairs={{0,2},{1,3},{2,4},{3,5},{4,6},{5,7},{6,0},{7,1},{8,10},{9,11},{10,... | collective-permute-start | bytes 393224 | tf_op jit(solution)/shard_map/ppermute | solution.py:52
  96.9 8.1 %collective-permute-start.32 = (bf16[256,256]{1,0:T(8,128)(2,1)S(1)}, bf16[256,256]{1,0:T(8,128)(2,1)S(1)}, u32[]{:S(2)}, u32[]{:S(2)}) collective-permute-start(bf16[256,256]{1,0:T(8,128)(2,1)S(1)} %attend.1.refs_0_), channel_id=1, source_target_pairs={{0,4},{1,5},{2,6},{3,7},{4,0},{5,1},{6,2},{7,3},{8,12},{9,13},{10,... | collective-permute-start | bytes 393224 | tf_op jit(solution)/shard_map/ppermute | solution.py:52
  99.0 7.3 %collective-permute-start.34 = (bf16[256,256]{1,0:T(8,128)(2,1)S(1)}, bf16[256,256]{1,0:T(8,128)(2,1)S(1)}, u32[]{:S(2)}, u32[]{:S(2)}) collective-permute-start(bf16[256,256]{1,0:T(8,128)(2,1)S(1)} %attend.1.refs_0_), channel_id=1, source_target_pairs={{0,6},{1,7},{2,0},{3,1},{4,2},{5,3},{6,4},{7,5},{8,14},{9,15},{10,... | collective-permute-start | bytes 393224 | tf_op jit(solution)/shard_map/ppermute | solution.py:52
  100.3 6.6 %collective-permute-start.29 = (bf16[256,256]{1,0:T(8,128)(2,1)S(1)}, bf16[256,256]{1,0:T(8,128)(2,1)S(1)}, u32[]{:S(2)}, u32[]{:S(2)}) collective-permute-start(bf16[256,256]{1,0:T(8,128)(2,1)S(1)} %attend.1.refs_0_), channel_id=1, source_target_pairs={{0,1},{1,0},{2,3},{3,2},{4,5},{5,4},{6,7},{7,6},{8,9},{9,8},{10,11... | collective-permute-start | bytes 393224 | tf_op jit(solution)/shard_map/ppermute | solution.py:56
  (19 other events, 218.4 us)

commit v3 on v2

--- a/solution.py
+++ b/solution.py
@@ -121,16 +121,23 @@
         out[start : start + part, : last - first] = context[:, first:last]
 
 
-def packed_context(tokens, weight, after):
+def half_sums(tokens, weight, y, c):
+    rows = tokens.shape[0]
+    part = rows // NH
+    parts = jnp.dot(tokens, weight, preferred_element_type=F32).reshape(NY, NC, part, E)
+    mine = lax.dynamic_index_in_dim(parts, c, axis=1, keepdims=False)
+    theirs = lax.dynamic_index_in_dim(parts, 1 - c, axis=1, keepdims=False)
+    return mine, core_swap(theirs)
+
+
+def packed_context(halves, tokens, after, after_sum):
     rows, width = tokens.shape
     part = rows // NH
-    half = jax.ShapeDtypeStruct((NY, part, E), F32)
-    mine, theirs = whole(partial_kernel, [tokens, weight], [half, half], "partial", after=after)
     outs = [jax.ShapeDtypeStruct((part, E), F32)] * NY
-    own, *sent = whole(chip_sum_kernel, [mine, core_swap(theirs)], outs, "chip_sum")
+    own, *sent = whole(chip_sum_kernel, list(halves), outs, "chip_sum", after=after)
     received = [y_shift(sent[r - 1], r) for r in (1, 3, 2)]
     out = jax.ShapeDtypeStruct((rows + len(PIECES) * part, width), BF)
-    return whole(pack_kernel, [own, *received, tokens], [out], "pack")[0]
+    return whole(pack_kernel, [own, *received, tokens], [out], "pack", after=after_sum)[0]
 
 
 def z_lists(lists, shifts):
@@ -191,17 +198,28 @@
     return jax.ShapeDtypeStruct((count, ROWS, E), BF)
 
 
-def fetch(slab, look, before_first, before_second):
+def first_hop(slab, look):
     outs = [slots(2 * SLOTS), slots(2 * SLOTS), slots(SLOTS)]
-    minus, plus, far = whole(first_kernel, slab, outs, "first", [look], before_first)
-    sent = [z_shift(minus, -1), z_shift(plus, 1), far_shift(far)]
-    outs = [slots(SLOTS)] * 3
-    minus, plus, mine = whole(second_kernel, slab + sent, outs, "second", [look], before_second)
-    return [mine, z_shift(minus, -2), z_shift(plus, 2)]
-
-
-def queries_kernel(*refs):
-    blocks, w, (out, context) = refs[:NH], refs[NH], refs[NH + 1 :]
+    return whole(first_kernel, slab, outs, "first", [look])
+
+
+def sent_on(slots_out):
+    minus, plus, far = slots_out
+    return [z_shift(minus, -1), z_shift(plus, 1), far_shift(far)]
+
+
+def second_hop(slab, look, arrays):
+    return whole(second_kernel, slab + arrays, [slots(SLOTS)] * 3, "second", [look])
+
+
+def stack_kernel(*refs):
+    *blocks, out = refs
+    for r, block in enumerate(blocks):
+        out[r] = block[...]
+
+
+def queries_kernel(own, other, w, out, context):
+    blocks = [(own, other)[k % NC].at[k // NC] for k in range(NH)]
     rows = out.shape[0]
     part = context.shape[0] // NH
     depth = w.shape[0] // NH
@@ -361,19 +379,25 @@
     output_weight,
 ):
     rows = tokens.shape[0]
+    head = lax.axis_index("head")
     slab = slab_of(store_rows)
     own = (neighbour_shard * STORE_DEV + neighbour_row).reshape(1, SLOTS)
-    look = z_lists(own, (1,))
-    packed = packed_context(tokens, context_weight, [look])
-    look = z_lists(look, (2, 4))
-    chips = chip_blocks_in_turn(packed)
-    fetched = fetch(slab, look, (), ())
+    look = z_lists(own, (1, 2, 4))
+    halves = half_sums(tokens, context_weight, head // NC, head % NC)
+    sent = first_hop(slab, look)
+    arrays = sent_on(sent)
+    minus, plus, mine = second_hop(slab, look, arrays)
+    fetched = [mine, z_shift(minus, -2), z_shift(plus, 2)]
+    packed = packed_context(halves, tokens, (), arrays[:2])
+    chips = chip_blocks(packed)
+    outs = [jax.ShapeDtypeStruct((NY, *packed.shape), BF)]
+    stacked = whole(stack_kernel, chips, outs, "stack", after=fetched[1:])[0]
     outs = [
         jax.ShapeDtypeStruct((rows, query_weight.shape[1]), BF),
         jax.ShapeDtypeStruct((rows, E), BF),
     ]
     queries, context = whole(
-        queries_kernel, [*with_swaps(chips), query_weight], outs, "queries"
+        queries_kernel, [stacked, core_swap(stacked), query_weight], outs, "queries"
     )
     scratch = [pltpu.VMEM((SLOTS, ROWS, E), BF)]
     encoded = whole(

time: 109 us -> 107 us (0.982)
  waiting for transfers between devices: 37.9 us -> 32.7 us
  starting transfers between devices: 55.6 us -> 58 us
  matrix products: 0 us -> 2.33 us
  local copies, waits for them, and re-layouts: 4.48 us -> 2.61 us
    ppermute x1, waiting for transfers between devices: 6.3 us -> 0.59 us  [far_shift(): return lax.ppermute(a, ('seq', 'head'), pairs)]
    unnamed x14 -> x12, local copies, waits for them, and re-layouts: 3.09 us -> 0.03 us
    ppermute x13 -> x10, waiting for transfers between devices: 2.47 us -> 5.2 us  [core_swap(): return lax.ppermute(a, 'head', [(h, h ^ 1) for h in range(NH)])]
    ppermute x7, starting transfers between devices: 12.3 us -> 15 us  [z_shift(): return lax.ppermute(a, 'seq', pairs)]
    ppermute x7, waiting for transfers between devices: 17 us -> 14.6 us  [z_shift(): return lax.ppermute(a, 'seq', pairs)]
    dot_general x0 -> x1, matrix products: none -> 2.33 us  [half_sums(): jnp.dot(tokens, weight, preferred_element_type=F32).reshape(NY, NC, part, E)]
    ppermute x13 -> x10, starting transfers between devices: 21.7 us -> 20.1 us  [core_swap(): return lax.ppermute(a, 'head', [(h, h ^ 1) for h in range(NH)])]
    squeeze x0 -> x1, local copies, waits for them, and re-layouts: none -> 1.26 us  [half_sums(): theirs = lax.dynamic_index_in_dim(parts, 1 - c, axis=1, keepdims=False)]
  transfers between devices with their start and end apart: 36 -> 33, of which waited for: 16 -> 17; matrix products, arithmetic and copies ran while one was open for 1% -> 4% of each run, Pallas kernels for 3% -> 2%
where the time goes in v3:
time: 107 us
  starting transfers between devices  58 us (54%)
  waiting for transfers between devices  32.7 us (31%)
  Pallas kernels  10.1 us (9%)
  local copies, waits for them, and re-layouts  2.61 us (2%)
  matrix products  2.33 us (2%)
    ppermute x10, starting transfers between devices, core_swap(): return lax.ppermute(a, 'head', [(h, h ^ 1) for h in range(NH)])  20.1 us
    ppermute x12, starting transfers between devices, y_shift(): return lax.ppermute(a, 'head', pairs)  17.2 us
    ppermute x7, starting transfers between devices, z_shift(): return lax.ppermute(a, 'seq', pairs)  15 us
    ppermute x7, waiting for transfers between devices, z_shift(): return lax.ppermute(a, 'seq', pairs)  14.6 us
    ppermute x12, waiting for transfers between devices, y_shift(): return lax.ppermute(a, 'head', pairs)  12.2 us
    ppermute x3, starting transfers between devices, x_shift(): return lax.ppermute(a, 'seq', pairs)  5.72 us
    pallas_call x7, Pallas kernels, whole(): pl.pallas_call(functools.partial(without, len(after), len(lists) + len(ar...  5.53 us
    ppermute x10, waiting for transfers between devices, core_swap(): return lax.ppermute(a, 'head', [(h, h ^ 1) for h in range(NH)])  5.2 us
  transfers between devices with their start and end apart: 33, of which 17 were waited for; matrix products, arithmetic and copies ran while one was open for 4% of the time, Pallas kernels for 2%

profile of v3, /device:TPU:1, one launch (start us, length us, event | category | flops | bytes accessed | tf_op | source)
XLA Modules:
  0.0 106.6 jit_solution(17888313431735334606)
XLA Ops:
  1.1 2.1 %collective-permute-start.3 = (bf16[16,16,896]{2,1,0:T(8,128)(2,1)S(1)}, bf16[16,16,896]{2,1,0:T(8,128)(2,1)S(1)}, u32[]{:S(2)}, u32[]{:S(2)}) collective-permute-start(bf16[16,16,896]{2,1,0:T(8,128)(2,1)S(1)} %constant_dynamic-slice_fusion.refs_1_), channel_id=1, source_target_pairs={{0,64},{8,72},{16,80},{24,88},{32,96},{40,104},{48,112},{56,120},{... | collective-permute-start | bytes 1376264 | tf_op jit(solution)/shard_map/ppermute | solution.py:66
  3.3 2.5 %collective-permute-start.4 = (bf16[16,16,896]{2,1,0:T(8,128)(2,1)S(1)}, bf16[16,16,896]{2,1,0:T(8,128)(2,1)S(1)}, u32[]{:S(2)}, u32[]{:S(2)}) collective-permute-start(bf16[16,16,896]{2,1,0:T(8,128)(2,1)S(1)} %constant_dynamic-slice_fusion.refs_1_), channel_id=1, source_target_pairs={{0,128},{8,136},{16,144},{24,152},{32,160},{40,168},{48,176},{56,1... | collective-permute-start | bytes 1376264 | tf_op jit(solution)/shard_map/ppermute | solution.py:66
  9.4 2.3 %fusion = f32[256,896]{1,0:T(8,128)} fusion(bf16[256,512]{1,0:T(8,128)(2,1)} %refs_4_.1, bf16[512,896]{1,0:T(8,128)(2,1)S(1)} %copy-done), kind=kOutput, calls=%fused_computation.7 | convolution fusion | flops 234881024 | bytes 2097152 | tf_op jit(solution)/shard_map/dot_general | solution.py:127
  14.9 3.1 %collective-permute-start.1 = (s32[2,8]{1,0:T(2,128)S(1)}, s32[2,8]{1,0:T(2,128)S(1)}, u32[]{:S(2)}, u32[]{:S(2)}) collective-permute-start(s32[2,8]{1,0:T(2,128)S(1)} %pad_add_fusion.2), channel_id=1, source_target_pairs={{0,16},{8,24},{16,32},{24,40},{32,48},{40,56},{48,0},{56,8},{64,80... | collective-permute-start | bytes 200 | tf_op jit(solution)/shard_map/ppermute | solution.py:61
  18.0 3.4 %collective-permute-done.1 = s32[2,8]{1,0:T(2,128)S(1)} collective-permute-done((s32[2,8]{1,0:T(2,128)S(1)}, s32[2,8]{1,0:T(2,128)S(1)}, u32[]{:S(2)}, u32[]{:S(2)}) %collective-permute-start.1) | collective-permute-done | bytes 96 | tf_op jit(solution)/shard_map/ppermute | solution.py:61
  21.3 4.5 %collective-permute-start.2 = (s32[4,8]{1,0:T(4,128)S(1)}, s32[4,8]{1,0:T(4,128)S(1)}, u32[]{:S(2)}, u32[]{:S(2)}) collective-permute-start(s32[4,8]{1,0:T(4,128)S(1)} %pad_add_fusion.1), channel_id=1, source_target_pairs={{0,32},{8,40},{16,48},{24,56},{32,0},{40,8},{48,16},{56,24},{64,96... | collective-permute-start | bytes 392 | tf_op jit(solution)/shard_map/ppermute | solution.py:61
  25.9 1.9 %collective-permute-done.2 = s32[4,8]{1,0:T(4,128)S(1)} collective-permute-done((s32[4,8]{1,0:T(4,128)S(1)}, s32[4,8]{1,0:T(4,128)S(1)}, u32[]{:S(2)}, u32[]{:S(2)}) %collective-permute-start.2) | collective-permute-done | bytes 160 | tf_op jit(solution)/shard_map/ppermute | solution.py:61
  29.1 3.3 %collective-permute-start.6 = (bf16[16,16,896]{2,1,0:T(8,128)(2,1)S(1)}, bf16[16,16,896]{2,1,0:T(8,128)(2,1)S(1)}, u32[]{:S(2)}, u32[]{:S(2)}) collective-permute-start(bf16[16,16,896]{2,1,0:T(8,128)(2,1)S(1)} %get-tuple-element.17), channel_id=1, source_target_pairs={{0,56},{8,0},{16,8},{24,16},{32,24},{40,32},{48,40},{56,48},{64,12... | collective-permute-start | bytes 1376264 | tf_op jit(solution)/shard_map/ppermute | solution.py:61
  35.5 2.0 %collective-permute-done.12.refs_1_ = f32[32,896]{1,0:T(8,128)S(1)} collective-permute-done((f32[32,896]{1,0:T(8,128)S(1)}, f32[32,896]{1,0:T(8,128)S(1)}, u32[]{:S(2)}, u32[]{:S(2)}) %collective-permute-start.12) | collective-permute-done | bytes 114720 | tf_op jit(solution)/shard_map/ppermute | solution.py:52
  37.5 1.9 %collective-permute-start.14 = (f32[32,896]{1,0:T(8,128)S(1)}, f32[32,896]{1,0:T(8,128)S(1)}, u32[]{:S(2)}, u32[]{:S(2)}) collective-permute-start(f32[32,896]{1,0:T(8,128)S(1)} %get-tuple-element.26), channel_id=1, source_target_pairs={{0,4},{1,5},{2,6},{3,7},{4,0},{5,1},{6,2},{7,3},{8,12},{9,13},{10,... | collective-permute-start | bytes 344072 | tf_op jit(solution)/shard_map/ppermute | solution.py:52
  39.4 3.2 %collective-permute-done.14.refs_3_ = f32[32,896]{1,0:T(8,128)S(1)} collective-permute-done((f32[32,896]{1,0:T(8,128)S(1)}, f32[32,896]{1,0:T(8,128)S(1)}, u32[]{:S(2)}, u32[]{:S(2)}) %collective-permute-start.14) | collective-permute-done | bytes 114720 | tf_op jit(solution)/shard_map/ppermute | solution.py:52
  45.6 2.6 %collective-permute-start.16 = (bf16[320,512]{1,0:T(8,128)(2,1)S(1)}, bf16[320,512]{1,0:T(8,128)(2,1)S(1)}, u32[]{:S(2)}, u32[]{:S(2)}) collective-permute-start(bf16[320,512]{1,0:T(8,128)(2,1)S(1)} %pack.1.refs_0_), channel_id=1, source_target_pairs={{0,4},{1,5},{2,6},{3,7},{4,0},{5,1},{6,2},{7,3},{8,12},{9,13},{10,... | collective-permute-start | bytes 983048 | tf_op jit(solution)/shard_map/ppermute | solution.py:52
  51.5 1.9 %collective-permute-start.10 = (bf16[8,16,896]{2,1,0:T(8,128)(2,1)S(1)}, bf16[8,16,896]{2,1,0:T(8,128)(2,1)S(1)}, u32[]{:S(2)}, u32[]{:S(2)}) collective-permute-start(bf16[8,16,896]{2,1,0:T(8,128)(2,1)S(1)} %get-tuple-element.22), channel_id=1, source_target_pairs={{0,16},{8,24},{16,32},{24,40},{32,48},{40,56},{48,0},{56,8},{64,80... | collective-permute-start | bytes 688136 | tf_op jit(solution)/shard_map/ppermute | solution.py:61
  53.5 3.8 %collective-permute-done.9.refs_4_.refs_2_ = bf16[8,16,896]{2,1,0:T(8,128)(2,1)S(1)} collective-permute-done((bf16[8,16,896]{2,1,0:T(8,128)(2,1)S(1)}, bf16[8,16,896]{2,1,0:T(8,128)(2,1)S(1)}, u32[]{:S(2)}, u32[]{:S(2)}) %collective-permute-start.9) | collective-permute-done | bytes 229408 | tf_op jit(solution)/shard_map/ppermute | solution.py:61
  57.3 4.0 %collective-permute-done.10.refs_5_.refs_3_ = bf16[8,16,896]{2,1,0:T(8,128)(2,1)S(1)} collective-permute-done((bf16[8,16,896]{2,1,0:T(8,128)(2,1)S(1)}, bf16[8,16,896]{2,1,0:T(8,128)(2,1)S(1)}, u32[]{:S(2)}, u32[]{:S(2)}) %collective-permute-start.10) | collective-permute-done | bytes 229408 | tf_op jit(solution)/shard_map/ppermute | solution.py:61
  61.4 6.8 %collective-permute-start.18 = (bf16[4,320,512]{2,1,0:T(8,128)(2,1)S(1)}, bf16[4,320,512]{2,1,0:T(8,128)(2,1)S(1)}, u32[]{:S(2)}, u32[]{:S(2)}) collective-permute-start(bf16[4,320,512]{2,1,0:T(8,128)(2,1)S(1)} %stack.1.refs_0_), channel_id=1, source_target_pairs={{0,1},{1,0},{2,3},{3,2},{4,5},{5,4},{6,7},{7,6},{8,9},{9,8},{10,11... | collective-permute-start | bytes 3932168 | tf_op jit(solution)/shard_map/ppermute | solution.py:56
  68.2 2.7 %collective-permute-done.18.refs_1_ = bf16[4,320,512]{2,1,0:T(8,128)(2,1)S(1)} collective-permute-done((bf16[4,320,512]{2,1,0:T(8,128)(2,1)S(1)}, bf16[4,320,512]{2,1,0:T(8,128)(2,1)S(1)}, u32[]{:S(2)}, u32[]{:S(2)}) %collective-permute-start.18) | collective-permute-done | bytes 1310752 | tf_op jit(solution)/shard_map/ppermute | solution.py:56
  71.6 2.2 %encode.1 = bf16[8,16,896]{2,1,0:T(8,128)(2,1)S(1)} custom-call(s32[8,8]{1,0:T(8,128)S(1)} %pad_add_fusion.refs_0_, bf16[8,16,896]{2,1,0:T(8,128)(2,1)S(1)} %get-tuple-element.20.refs_1_, bf16[8,16,896]{2,1,0:T(8,128)(2,1)S(1)} %collective-permute-done.9.refs_4_.refs_2_, bf16[8,16,896]{2,1,0:T(8,128)(2,1)S(1)} %collective-permute-done.10.refs_5_.refs_3_, ...), custom_call_target="tpu_custom_call" | custom-call | bytes 1376256 | tf_op jit(solution)/shard_map/encode/pallas_call | solution.py:38
  74.3 2.1 %collective-permute-start.22 = (bf16[8,16,896]{2,1,0:T(8,128)(2,1)S(1)}, bf16[8,16,896]{2,1,0:T(8,128)(2,1)S(1)}, u32[]{:S(2)}, u32[]{:S(2)}) collective-permute-start(bf16[8,16,896]{2,1,0:T(8,128)(2,1)S(1)} %encode.1), channel_id=1, source_target_pairs={{0,4},{1,5},{2,6},{3,7},{4,0},{5,1},{6,2},{7,3},{8,12},{9,13},{10,... | collective-permute-start | bytes 688136 | tf_op jit(solution)/shard_map/ppermute | solution.py:52
  78.7 3.4 %collective-permute-done.20 = bf16[8,16,896]{2,1,0:T(8,128)(2,1)S(1)} collective-permute-done((bf16[8,16,896]{2,1,0:T(8,128)(2,1)S(1)}, bf16[8,16,896]{2,1,0:T(8,128)(2,1)S(1)}, u32[]{:S(2)}, u32[]{:S(2)}) %collective-permute-start.20) | collective-permute-done | bytes 229408 | tf_op jit(solution)/shard_map/ppermute | solution.py:52
  82.1 5.9 %collective-permute-start.21 = (bf16[8,16,896]{2,1,0:T(8,128)(2,1)S(1)}, bf16[8,16,896]{2,1,0:T(8,128)(2,1)S(1)}, u32[]{:S(2)}, u32[]{:S(2)}) collective-permute-start(bf16[8,16,896]{2,1,0:T(8,128)(2,1)S(1)} %collective-permute-done.20), channel_id=1, source_target_pairs={{0,1},{1,0},{2,3},{3,2},{4,5},{5,4},{6,7},{7,6},{8,9},{9,8},{10,11... | collective-permute-start | bytes 688136 | tf_op jit(solution)/shard_map/ppermute | solution.py:56
  89.9 3.1 %attend.1.refs_0_ = bf16[256,256]{1,0:T(8,128)(2,1)S(1)} custom-call(bf16[4,32,896]{2,1,0:T(8,128)(2,1)S(1)} %bitcast.19, bf16[4,32,896]{2,1,0:T(8,128)(2,1)S(1)} %bitcast.23, bf16[4,32,896]{2,1,0:T(8,128)(2,1)S(1)} %bitcast.20, bf16[4,32,896]{2,1,0:T(8,128)(2,1)S(1)} %bitcast.24, bf16[4,32,896]{2,1,0:T(8,128)(2,1)S(1)} %bitcast.21, ...), custom_call_target="tpu_custom_call" | custom-call | flops 939524096 | bytes 3014656 | tf_op jit(solution)/shard_map/attend/pallas_call | solution.py:324
  93.9 2.7 %collective-permute-start.29 = (bf16[256,256]{1,0:T(8,128)(2,1)S(1)}, bf16[256,256]{1,0:T(8,128)(2,1)S(1)}, u32[]{:S(2)}, u32[]{:S(2)}) collective-permute-start(bf16[256,256]{1,0:T(8,128)(2,1)S(1)} %attend.1.refs_0_), channel_id=1, source_target_pairs={{0,4},{1,5},{2,6},{3,7},{4,0},{5,1},{6,2},{7,3},{8,12},{9,13},{10,... | collective-permute-start | bytes 393224 | tf_op jit(solution)/shard_map/ppermute | solution.py:52
  100.3 2.3 %collective-permute-done.29.refs_4_ = bf16[256,256]{1,0:T(8,128)(2,1)S(1)} collective-permute-done((bf16[256,256]{1,0:T(8,128)(2,1)S(1)}, bf16[256,256]{1,0:T(8,128)(2,1)S(1)}, u32[]{:S(2)}, u32[]{:S(2)}) %collective-permute-start.29) | collective-permute-done | bytes 131104 | tf_op jit(solution)/shard_map/ppermute | solution.py:52
  (72 shorter events, 32.5 us)
Async XLA Ops:
  1.1 26.6 %collective-permute-start.3 = (bf16[16,16,896]{2,1,0:T(8,128)(2,1)S(1)}, bf16[16,16,896]{2,1,0:T(8,128)(2,1)S(1)}, u32[]{:S(2)}, u32[]{:S(2)}) collective-permute-start(bf16[16,16,896]{2,1,0:T(8,128)(2,1)S(1)} %constant_dynamic-slice_fusion.refs_1_), channel_id=1, source_target_pairs={{0,64},{8,72},{16,80},{24,88},{32,96},{40,104},{48,112},{56,120},{... | collective-permute-start | bytes 1376264 | tf_op jit(solution)/shard_map/ppermute | solution.py:66
  3.3 24.5 %collective-permute-start.4 = (bf16[16,16,896]{2,1,0:T(8,128)(2,1)S(1)}, bf16[16,16,896]{2,1,0:T(8,128)(2,1)S(1)}, u32[]{:S(2)}, u32[]{:S(2)}) collective-permute-start(bf16[16,16,896]{2,1,0:T(8,128)(2,1)S(1)} %constant_dynamic-slice_fusion.refs_1_), channel_id=1, source_target_pairs={{0,128},{8,136},{16,144},{24,152},{32,160},{40,168},{48,176},{56,1... | collective-permute-start | bytes 1376264 | tf_op jit(solution)/shard_map/ppermute | solution.py:66
  5.7 22.1 %collective-permute-start.5 = (bf16[16,16,896]{2,1,0:T(8,128)(2,1)S(1)}, bf16[16,16,896]{2,1,0:T(8,128)(2,1)S(1)}, u32[]{:S(2)}, u32[]{:S(2)}) collective-permute-start(bf16[16,16,896]{2,1,0:T(8,128)(2,1)S(1)} %constant_dynamic-slice_fusion.refs_1_), channel_id=1, source_target_pairs={{0,192},{8,200},{16,208},{24,216},{32,224},{40,232},{48,240},{56,2... | collective-permute-start | bytes 1376264 | tf_op jit(solution)/shard_map/ppermute | solution.py:66
  7.7 7.1 %collective-permute-start = (s32[1,8]{1,0:T(1,128)S(1)}, s32[1,8]{1,0:T(1,128)S(1)}, u32[]{:S(2)}, u32[]{:S(2)}) collective-permute-start(s32[1,8]{1,0:T(1,128)S(1)} %reshape.30), channel_id=1, source_target_pairs={{0,8},{8,16},{16,24},{24,32},{32,40},{40,48},{48,56},{56,0},{64,72... | collective-permute-start | bytes 104 | tf_op jit(solution)/shard_map/ppermute | solution.py:61
  13.0 19.4 %collective-permute-start.11 = (f32[4,32,896]{2,1,0:T(8,128)S(1)}, f32[4,32,896]{2,1,0:T(8,128)S(1)}, u32[]{:S(2)}, u32[]{:S(2)}) collective-permute-start(f32[4,32,896]{2,1,0:T(8,128)S(1)} %get-tuple-element.29), channel_id=1, source_target_pairs={{0,1},{1,0},{2,3},{3,2},{4,5},{5,4},{6,7},{7,6},{8,9},{9,8},{10,11... | collective-permute-start | bytes 1376264 | tf_op jit(solution)/shard_map/ppermute | solution.py:56
  14.9 6.5 %collective-permute-start.1 = (s32[2,8]{1,0:T(2,128)S(1)}, s32[2,8]{1,0:T(2,128)S(1)}, u32[]{:S(2)}, u32[]{:S(2)}) collective-permute-start(s32[2,8]{1,0:T(2,128)S(1)} %pad_add_fusion.2), channel_id=1, source_target_pairs={{0,16},{8,24},{16,32},{24,40},{32,48},{40,56},{48,0},{56,8},{64,80... | collective-permute-start | bytes 200 | tf_op jit(solution)/shard_map/ppermute | solution.py:61
  21.3 6.4 %collective-permute-start.2 = (s32[4,8]{1,0:T(4,128)S(1)}, s32[4,8]{1,0:T(4,128)S(1)}, u32[]{:S(2)}, u32[]{:S(2)}) collective-permute-start(s32[4,8]{1,0:T(4,128)S(1)} %pad_add_fusion.1), channel_id=1, source_target_pairs={{0,32},{8,40},{16,48},{24,56},{32,0},{40,8},{48,16},{56,24},{64,96... | collective-permute-start | bytes 392 | tf_op jit(solution)/shard_map/ppermute | solution.py:61
  29.1 13.5 %collective-permute-start.6 = (bf16[16,16,896]{2,1,0:T(8,128)(2,1)S(1)}, bf16[16,16,896]{2,1,0:T(8,128)(2,1)S(1)}, u32[]{:S(2)}, u32[]{:S(2)}) collective-permute-start(bf16[16,16,896]{2,1,0:T(8,128)(2,1)S(1)} %get-tuple-element.17), channel_id=1, source_target_pairs={{0,56},{8,0},{16,8},{24,16},{32,24},{40,32},{48,40},{56,48},{64,12... | collective-permute-start | bytes 1376264 | tf_op jit(solution)/shard_map/ppermute | solution.py:61
  32.4 11.8 %collective-permute-start.7 = (bf16[16,16,896]{2,1,0:T(8,128)(2,1)S(1)}, bf16[16,16,896]{2,1,0:T(8,128)(2,1)S(1)}, u32[]{:S(2)}, u32[]{:S(2)}) collective-permute-start(bf16[16,16,896]{2,1,0:T(8,128)(2,1)S(1)} %get-tuple-element.18), channel_id=1, source_target_pairs={{0,8},{8,16},{16,24},{24,32},{32,40},{40,48},{48,56},{56,0},{64,72... | collective-permute-start | bytes 1376264 | tf_op jit(solution)/shard_map/ppermute | solution.py:61
  33.8 16.0 %collective-permute-start.8 = (bf16[8,16,896]{2,1,0:T(8,128)(2,1)S(1)}, bf16[8,16,896]{2,1,0:T(8,128)(2,1)S(1)}, u32[]{:S(2)}, u32[]{:S(2)}) collective-permute-start(bf16[8,16,896]{2,1,0:T(8,128)(2,1)S(1)} %get-tuple-element.19), channel_id=1, source_target_pairs={{0,48},{1,17},{2,50},{3,19},{4,52},{5,21},{6,54},{7,23},{8,56},{9,... | collective-permute-start | bytes 688136 | tf_op jit(solution)/shard_map/ppermute | solution.py:76
  44.2 17.1 %collective-permute-start.15 = (bf16[320,512]{1,0:T(8,128)(2,1)S(1)}, bf16[320,512]{1,0:T(8,128)(2,1)S(1)}, u32[]{:S(2)}, u32[]{:S(2)}) collective-permute-start(bf16[320,512]{1,0:T(8,128)(2,1)S(1)} %pack.1.refs_0_), channel_id=1, source_target_pairs={{0,2},{1,3},{2,4},{3,5},{4,6},{5,7},{6,0},{7,1},{8,10},{9,11},{10,... | collective-permute-start | bytes 983048 | tf_op jit(solution)/shard_map/ppermute | solution.py:52
  45.6 15.7 %collective-permute-start.16 = (bf16[320,512]{1,0:T(8,128)(2,1)S(1)}, bf16[320,512]{1,0:T(8,128)(2,1)S(1)}, u32[]{:S(2)}, u32[]{:S(2)}) collective-permute-start(bf16[320,512]{1,0:T(8,128)(2,1)S(1)} %pack.1.refs_0_), channel_id=1, source_target_pairs={{0,4},{1,5},{2,6},{3,7},{4,0},{5,1},{6,2},{7,3},{8,12},{9,13},{10,... | collective-permute-start | bytes 983048 | tf_op jit(solution)/shard_map/ppermute | solution.py:52
  48.2 13.1 %collective-permute-start.17 = (bf16[320,512]{1,0:T(8,128)(2,1)S(1)}, bf16[320,512]{1,0:T(8,128)(2,1)S(1)}, u32[]{:S(2)}, u32[]{:S(2)}) collective-permute-start(bf16[320,512]{1,0:T(8,128)(2,1)S(1)} %pack.1.refs_0_), channel_id=1, source_target_pairs={{0,6},{1,7},{2,0},{3,1},{4,2},{5,3},{6,4},{7,5},{8,14},{9,15},{10,... | collective-permute-start | bytes 983048 | tf_op jit(solution)/shard_map/ppermute | solution.py:52
  51.0 6.3 %collective-permute-start.9 = (bf16[8,16,896]{2,1,0:T(8,128)(2,1)S(1)}, bf16[8,16,896]{2,1,0:T(8,128)(2,1)S(1)}, u32[]{:S(2)}, u32[]{:S(2)}) collective-permute-start(bf16[8,16,896]{2,1,0:T(8,128)(2,1)S(1)} %get-tuple-element.21), channel_id=1, source_target_pairs={{0,48},{8,56},{16,0},{24,8},{32,16},{40,24},{48,32},{56,40},{64,11... | collective-permute-start | bytes 688136 | tf_op jit(solution)/shard_map/ppermute | solution.py:61
  51.5 9.7 %collective-permute-start.10 = (bf16[8,16,896]{2,1,0:T(8,128)(2,1)S(1)}, bf16[8,16,896]{2,1,0:T(8,128)(2,1)S(1)}, u32[]{:S(2)}, u32[]{:S(2)}) collective-permute-start(bf16[8,16,896]{2,1,0:T(8,128)(2,1)S(1)} %get-tuple-element.22), channel_id=1, source_target_pairs={{0,16},{8,24},{16,32},{24,40},{32,48},{40,56},{48,0},{56,8},{64,80... | collective-permute-start | bytes 688136 | tf_op jit(solution)/shard_map/ppermute | solution.py:61
  61.4 9.5 %collective-permute-start.18 = (bf16[4,320,512]{2,1,0:T(8,128)(2,1)S(1)}, bf16[4,320,512]{2,1,0:T(8,128)(2,1)S(1)}, u32[]{:S(2)}, u32[]{:S(2)}) collective-permute-start(bf16[4,320,512]{2,1,0:T(8,128)(2,1)S(1)} %stack.1.refs_0_), channel_id=1, source_target_pairs={{0,1},{1,0},{2,3},{3,2},{4,5},{5,4},{6,7},{7,6},{8,9},{9,8},{10,11... | collective-permute-start | bytes 3932168 | tf_op jit(solution)/shard_map/ppermute | solution.py:56
  73.9 8.3 %collective-permute-start.20 = (bf16[8,16,896]{2,1,0:T(8,128)(2,1)S(1)}, bf16[8,16,896]{2,1,0:T(8,128)(2,1)S(1)}, u32[]{:S(2)}, u32[]{:S(2)}) collective-permute-start(bf16[8,16,896]{2,1,0:T(8,128)(2,1)S(1)} %encode.1), channel_id=1, source_target_pairs={{0,2},{1,3},{2,4},{3,5},{4,6},{5,7},{6,0},{7,1},{8,10},{9,11},{10,... | collective-permute-start | bytes 688136 | tf_op jit(solution)/shard_map/ppermute | solution.py:52
  74.3 13.7 %collective-permute-start.22 = (bf16[8,16,896]{2,1,0:T(8,128)(2,1)S(1)}, bf16[8,16,896]{2,1,0:T(8,128)(2,1)S(1)}, u32[]{:S(2)}, u32[]{:S(2)}) collective-permute-start(bf16[8,16,896]{2,1,0:T(8,128)(2,1)S(1)} %encode.1), channel_id=1, source_target_pairs={{0,4},{1,5},{2,6},{3,7},{4,0},{5,1},{6,2},{7,3},{8,12},{9,13},{10,... | collective-permute-start | bytes 688136 | tf_op jit(solution)/shard_map/ppermute | solution.py:52
  76.4 11.7 %collective-permute-start.24 = (bf16[8,16,896]{2,1,0:T(8,128)(2,1)S(1)}, bf16[8,16,896]{2,1,0:T(8,128)(2,1)S(1)}, u32[]{:S(2)}, u32[]{:S(2)}) collective-permute-start(bf16[8,16,896]{2,1,0:T(8,128)(2,1)S(1)} %encode.1), channel_id=1, source_target_pairs={{0,6},{1,7},{2,0},{3,1},{4,2},{5,3},{6,4},{7,5},{8,14},{9,15},{10,... | collective-permute-start | bytes 688136 | tf_op jit(solution)/shard_map/ppermute | solution.py:52
  77.5 11.2 %collective-permute-start.19 = (bf16[8,16,896]{2,1,0:T(8,128)(2,1)S(1)}, bf16[8,16,896]{2,1,0:T(8,128)(2,1)S(1)}, u32[]{:S(2)}, u32[]{:S(2)}) collective-permute-start(bf16[8,16,896]{2,1,0:T(8,128)(2,1)S(1)} %encode.1), channel_id=1, source_target_pairs={{0,1},{1,0},{2,3},{3,2},{4,5},{5,4},{6,7},{7,6},{8,9},{9,8},{10,11... | collective-permute-start | bytes 688136 | tf_op jit(solution)/shard_map/ppermute | solution.py:56
  82.1 7.1 %collective-permute-start.21 = (bf16[8,16,896]{2,1,0:T(8,128)(2,1)S(1)}, bf16[8,16,896]{2,1,0:T(8,128)(2,1)S(1)}, u32[]{:S(2)}, u32[]{:S(2)}) collective-permute-start(bf16[8,16,896]{2,1,0:T(8,128)(2,1)S(1)} %collective-permute-done.20), channel_id=1, source_target_pairs={{0,1},{1,0},{2,3},{3,2},{4,5},{5,4},{6,7},{7,6},{8,9},{9,8},{10,11... | collective-permute-start | bytes 688136 | tf_op jit(solution)/shard_map/ppermute | solution.py:56
  93.9 8.7 %collective-permute-start.29 = (bf16[256,256]{1,0:T(8,128)(2,1)S(1)}, bf16[256,256]{1,0:T(8,128)(2,1)S(1)}, u32[]{:S(2)}, u32[]{:S(2)}) collective-permute-start(bf16[256,256]{1,0:T(8,128)(2,1)S(1)} %attend.1.refs_0_), channel_id=1, source_target_pairs={{0,4},{1,5},{2,6},{3,7},{4,0},{5,1},{6,2},{7,3},{8,12},{9,13},{10,... | collective-permute-start | bytes 393224 | tf_op jit(solution)/shard_map/ppermute | solution.py:52
  96.6 7.3 %collective-permute-start.31 = (bf16[256,256]{1,0:T(8,128)(2,1)S(1)}, bf16[256,256]{1,0:T(8,128)(2,1)S(1)}, u32[]{:S(2)}, u32[]{:S(2)}) collective-permute-start(bf16[256,256]{1,0:T(8,128)(2,1)S(1)} %attend.1.refs_0_), channel_id=1, source_target_pairs={{0,6},{1,7},{2,0},{3,1},{4,2},{5,3},{6,4},{7,5},{8,14},{9,15},{10,... | collective-permute-start | bytes 393224 | tf_op jit(solution)/shard_map/ppermute | solution.py:52
  96.6 7.2 %collective-permute-start.26 = (bf16[256,256]{1,0:T(8,128)(2,1)S(1)}, bf16[256,256]{1,0:T(8,128)(2,1)S(1)}, u32[]{:S(2)}, u32[]{:S(2)}) collective-permute-start(bf16[256,256]{1,0:T(8,128)(2,1)S(1)} %attend.1.refs_0_), channel_id=1, source_target_pairs={{0,1},{1,0},{2,3},{3,2},{4,5},{5,4},{6,7},{7,6},{8,9},{9,8},{10,11... | collective-permute-start | bytes 393224 | tf_op jit(solution)/shard_map/ppermute | solution.py:56
  (15 other events, 185.6 us)

commit v4 on v3

--- a/solution.py
+++ b/solution.py
@@ -213,30 +213,28 @@
 
 
 def stack_kernel(*refs):
-    *blocks, out = refs
+    blocks, (tokens, context) = refs[:NY], refs[NY:]
+    rows, part = tokens.shape[1], context.shape[1]
     for r, block in enumerate(blocks):
-        out[r] = block[...]
-
-
-def queries_kernel(own, other, w, out, context):
+        tokens[r] = block[:rows]
+        for i, (first, last) in enumerate(PIECES):
+            at = rows + i * part
+            context[r, :, first:last] = block[at : at + part, : last - first]
+
+
+def queries_kernel(own, other, w, out):
     blocks = [(own, other)[k % NC].at[k // NC] for k in range(NH)]
-    rows = out.shape[0]
-    part = context.shape[0] // NH
     depth = w.shape[0] // NH
     total = None
     for k in range(NH):
         start = pl.multiple_of(source_head(k) * depth, depth)
-        dot = jnp.dot(blocks[k][:rows], w[pl.ds(start, depth), :], preferred_element_type=F32)
+        dot = jnp.dot(blocks[k][...], w[pl.ds(start, depth), :], preferred_element_type=F32)
         total = dot if total is None else total + dot
-        for i, (first, last) in enumerate(PIECES):
-            at = rows + i * part
-            context[k * part : (k + 1) * part, first:last] = blocks[k][at : at + part, : last - first]
     out[...] = total.astype(out.dtype)
 
 
-def encode_kernel(look, mine, ahead_in, behind_in, ctx, out, nb):
+def encode_kernel(look, mine, ahead_in, behind_in, ctx, other_ctx, out, nb):
     width = nb.shape[-1]
-    part = ctx.shape[0] // NH
     core = lax.axis_index("head") % NC
     for q in range(SLOTS):
         away, _, _ = locate(look[0, q])
@@ -246,7 +244,7 @@
     heads = range(width // EHD)
     for r in range(NY):
         span = source_head(NC * r) // NC
-        context = ctx[NC * r * part : NC * (r + 1) * part]
+        context = jnp.concatenate([ctx[r], other_ctx[r]], axis=0)
         rows = nb[pl.ds(span * KN, KN)].reshape(KN * ROWS, width)
         scores = jnp.concatenate(
             [
@@ -390,19 +388,23 @@
     fetched = [mine, z_shift(minus, -2), z_shift(plus, 2)]
     packed = packed_context(halves, tokens, (), arrays[:2])
     chips = chip_blocks(packed)
-    outs = [jax.ShapeDtypeStruct((NY, *packed.shape), BF)]
-    stacked = whole(stack_kernel, chips, outs, "stack", after=fetched[1:])[0]
     outs = [
-        jax.ShapeDtypeStruct((rows, query_weight.shape[1]), BF),
-        jax.ShapeDtypeStruct((rows, E), BF),
+        jax.ShapeDtypeStruct((NY, *tokens.shape), BF),
+        jax.ShapeDtypeStruct((NY, rows // NH, E), BF),
     ]
-    queries, context = whole(
-        queries_kernel, [stacked, core_swap(stacked), query_weight], outs, "queries"
-    )
+    tok_stack, context = whole(stack_kernel, chips, outs, "stack", after=fetched[1:])
     scratch = [pltpu.VMEM((SLOTS, ROWS, E), BF)]
     encoded = whole(
-        encode_kernel, [*fetched, context], [slots(SLOTS)], "encode", [look], scratch=scratch
+        encode_kernel,
+        [*fetched, context, core_swap(context)],
+        [slots(SLOTS)],
+        "encode",
+        [look],
+        scratch=scratch,
     )[0]
+    outs = [jax.ShapeDtypeStruct((rows, query_weight.shape[1]), BF)]
+    arrays = [tok_stack, core_swap(tok_stack), query_weight]
+    queries = whole(queries_kernel, arrays, outs, "queries", after=[encoded])[0]
     attention = attend(with_swaps(chip_blocks(encoded)), queries, key_weight, value_weight)
     return project(with_swaps(chip_blocks(attention)), output_weight)
 

time: 107 us -> 106 us (level)
    ppermute x10 -> x11, waiting for transfers between devices: 5.2 us -> 4.32 us  [core_swap(): return lax.ppermute(a, 'head', [(h, h ^ 1) for h in range(NH)])]
    ppermute x10 -> x11, starting transfers between devices: 20.1 us -> 20.2 us  [core_swap(): return lax.ppermute(a, 'head', [(h, h ^ 1) for h in range(NH)])]
  transfers between devices with their start and end apart: 33 -> 34, of which waited for: 17 -> 16; matrix products, arithmetic and copies ran while one was open for 4% -> 4% of each run, Pallas kernels for 2% -> 5%
where the time goes in v4:
time: 106 us
  starting transfers between devices  58.2 us (55%)
  waiting for transfers between devices  31.7 us (30%)
  Pallas kernels  10.1 us (10%)
  local copies, waits for them, and re-layouts  2.57 us (2%)
  matrix products  2.33 us (2%)
    ppermute x11, starting transfers between devices, core_swap(): return lax.ppermute(a, 'head', [(h, h ^ 1) for h in range(NH)])  20.2 us
    ppermute x12, starting transfers between devices, y_shift(): return lax.ppermute(a, 'head', pairs)  17.3 us
    ppermute x7, starting transfers between devices, z_shift(): return lax.ppermute(a, 'seq', pairs)  15.1 us
    ppermute x7, waiting for transfers between devices, z_shift(): return lax.ppermute(a, 'seq', pairs)  14.7 us
    ppermute x12, waiting for transfers between devices, y_shift(): return lax.ppermute(a, 'head', pairs)  12.1 us
    ppermute x3, starting transfers between devices, x_shift(): return lax.ppermute(a, 'seq', pairs)  5.72 us
    pallas_call x7, Pallas kernels, whole(): pl.pallas_call(functools.partial(without, len(after), len(lists) + len(ar...  5.52 us
    ppermute x11, waiting for transfers between devices, core_swap(): return lax.ppermute(a, 'head', [(h, h ^ 1) for h in range(NH)])  4.32 us
  transfers between devices with their start and end apart: 34, of which 16 were waited for; matrix products, arithmetic and copies ran while one was open for 4% of the time, Pallas kernels for 5%

profile of v4, /device:TPU:1, one launch (start us, length us, event | category | flops | bytes accessed | tf_op | source)
XLA Modules:
  0.0 105.8 jit_solution(14638231817072244411)
XLA Ops:
  1.2 2.1 %collective-permute-start.3 = (bf16[16,16,896]{2,1,0:T(8,128)(2,1)S(1)}, bf16[16,16,896]{2,1,0:T(8,128)(2,1)S(1)}, u32[]{:S(2)}, u32[]{:S(2)}) collective-permute-start(bf16[16,16,896]{2,1,0:T(8,128)(2,1)S(1)} %constant_dynamic-slice_fusion.refs_1_), channel_id=1, source_target_pairs={{0,64},{8,72},{16,80},{24,88},{32,96},{40,104},{48,112},{56,120},{... | collective-permute-start | bytes 1376264 | tf_op jit(solution)/shard_map/ppermute | solution.py:66
  3.3 2.5 %collective-permute-start.4 = (bf16[16,16,896]{2,1,0:T(8,128)(2,1)S(1)}, bf16[16,16,896]{2,1,0:T(8,128)(2,1)S(1)}, u32[]{:S(2)}, u32[]{:S(2)}) collective-permute-start(bf16[16,16,896]{2,1,0:T(8,128)(2,1)S(1)} %constant_dynamic-slice_fusion.refs_1_), channel_id=1, source_target_pairs={{0,128},{8,136},{16,144},{24,152},{32,160},{40,168},{48,176},{56,1... | collective-permute-start | bytes 1376264 | tf_op jit(solution)/shard_map/ppermute | solution.py:66
  9.4 2.3 %fusion = f32[256,896]{1,0:T(8,128)} fusion(bf16[256,512]{1,0:T(8,128)(2,1)} %refs_4_.1, bf16[512,896]{1,0:T(8,128)(2,1)S(1)} %copy-done), kind=kOutput, calls=%fused_computation.7 | convolution fusion | flops 234881024 | bytes 2097152 | tf_op jit(solution)/shard_map/dot_general | solution.py:127
  13.0 1.9 %collective-permute-start.11 = (f32[4,32,896]{2,1,0:T(8,128)S(1)}, f32[4,32,896]{2,1,0:T(8,128)S(1)}, u32[]{:S(2)}, u32[]{:S(2)}) collective-permute-start(f32[4,32,896]{2,1,0:T(8,128)S(1)} %get-tuple-element.29), channel_id=1, source_target_pairs={{0,1},{1,0},{2,3},{3,2},{4,5},{5,4},{6,7},{7,6},{8,9},{9,8},{10,11... | collective-permute-start | bytes 1376264 | tf_op jit(solution)/shard_map/ppermute | solution.py:56
  14.9 3.1 %collective-permute-start.1 = (s32[2,8]{1,0:T(2,128)S(1)}, s32[2,8]{1,0:T(2,128)S(1)}, u32[]{:S(2)}, u32[]{:S(2)}) collective-permute-start(s32[2,8]{1,0:T(2,128)S(1)} %pad_add_fusion.2), channel_id=1, source_target_pairs={{0,16},{8,24},{16,32},{24,40},{32,48},{40,56},{48,0},{56,8},{64,80... | collective-permute-start | bytes 200 | tf_op jit(solution)/shard_map/ppermute | solution.py:61
  17.9 3.4 %collective-permute-done.1 = s32[2,8]{1,0:T(2,128)S(1)} collective-permute-done((s32[2,8]{1,0:T(2,128)S(1)}, s32[2,8]{1,0:T(2,128)S(1)}, u32[]{:S(2)}, u32[]{:S(2)}) %collective-permute-start.1) | collective-permute-done | bytes 96 | tf_op jit(solution)/shard_map/ppermute | solution.py:61
  21.3 4.6 %collective-permute-start.2 = (s32[4,8]{1,0:T(4,128)S(1)}, s32[4,8]{1,0:T(4,128)S(1)}, u32[]{:S(2)}, u32[]{:S(2)}) collective-permute-start(s32[4,8]{1,0:T(4,128)S(1)} %pad_add_fusion.1), channel_id=1, source_target_pairs={{0,32},{8,40},{16,48},{24,56},{32,0},{40,8},{48,16},{56,24},{64,96... | collective-permute-start | bytes 392 | tf_op jit(solution)/shard_map/ppermute | solution.py:61
  29.1 3.3 %collective-permute-start.6 = (bf16[16,16,896]{2,1,0:T(8,128)(2,1)S(1)}, bf16[16,16,896]{2,1,0:T(8,128)(2,1)S(1)}, u32[]{:S(2)}, u32[]{:S(2)}) collective-permute-start(bf16[16,16,896]{2,1,0:T(8,128)(2,1)S(1)} %get-tuple-element.17), channel_id=1, source_target_pairs={{0,56},{8,0},{16,8},{24,16},{32,24},{40,32},{48,40},{56,48},{64,12... | collective-permute-start | bytes 1376264 | tf_op jit(solution)/shard_map/ppermute | solution.py:61
  35.5 2.0 %collective-permute-done.12.refs_1_ = f32[32,896]{1,0:T(8,128)S(1)} collective-permute-done((f32[32,896]{1,0:T(8,128)S(1)}, f32[32,896]{1,0:T(8,128)S(1)}, u32[]{:S(2)}, u32[]{:S(2)}) %collective-permute-start.12) | collective-permute-done | bytes 114720 | tf_op jit(solution)/shard_map/ppermute | solution.py:52
  37.5 1.9 %collective-permute-start.14 = (f32[32,896]{1,0:T(8,128)S(1)}, f32[32,896]{1,0:T(8,128)S(1)}, u32[]{:S(2)}, u32[]{:S(2)}) collective-permute-start(f32[32,896]{1,0:T(8,128)S(1)} %get-tuple-element.26), channel_id=1, source_target_pairs={{0,4},{1,5},{2,6},{3,7},{4,0},{5,1},{6,2},{7,3},{8,12},{9,13},{10,... | collective-permute-start | bytes 344072 | tf_op jit(solution)/shard_map/ppermute | solution.py:52
  39.4 3.2 %collective-permute-done.14.refs_3_ = f32[32,896]{1,0:T(8,128)S(1)} collective-permute-done((f32[32,896]{1,0:T(8,128)S(1)}, f32[32,896]{1,0:T(8,128)S(1)}, u32[]{:S(2)}, u32[]{:S(2)}) %collective-permute-start.14) | collective-permute-done | bytes 114720 | tf_op jit(solution)/shard_map/ppermute | solution.py:52
  45.6 2.6 %collective-permute-start.16 = (bf16[320,512]{1,0:T(8,128)(2,1)S(1)}, bf16[320,512]{1,0:T(8,128)(2,1)S(1)}, u32[]{:S(2)}, u32[]{:S(2)}) collective-permute-start(bf16[320,512]{1,0:T(8,128)(2,1)S(1)} %pack.1.refs_0_), channel_id=1, source_target_pairs={{0,4},{1,5},{2,6},{3,7},{4,0},{5,1},{6,2},{7,3},{8,12},{9,13},{10,... | collective-permute-start | bytes 983048 | tf_op jit(solution)/shard_map/ppermute | solution.py:52
  51.6 1.9 %collective-permute-start.10 = (bf16[8,16,896]{2,1,0:T(8,128)(2,1)S(1)}, bf16[8,16,896]{2,1,0:T(8,128)(2,1)S(1)}, u32[]{:S(2)}, u32[]{:S(2)}) collective-permute-start(bf16[8,16,896]{2,1,0:T(8,128)(2,1)S(1)} %get-tuple-element.22), channel_id=1, source_target_pairs={{0,16},{8,24},{16,32},{24,40},{32,48},{40,56},{48,0},{56,8},{64,80... | collective-permute-start | bytes 688136 | tf_op jit(solution)/shard_map/ppermute | solution.py:61
  53.4 3.8 %collective-permute-done.9.refs_4_.refs_2_ = bf16[8,16,896]{2,1,0:T(8,128)(2,1)S(1)} collective-permute-done((bf16[8,16,896]{2,1,0:T(8,128)(2,1)S(1)}, bf16[8,16,896]{2,1,0:T(8,128)(2,1)S(1)}, u32[]{:S(2)}, u32[]{:S(2)}) %collective-permute-start.9) | collective-permute-done | bytes 229408 | tf_op jit(solution)/shard_map/ppermute | solution.py:61
  57.3 4.0 %collective-permute-done.10.refs_5_.refs_3_ = bf16[8,16,896]{2,1,0:T(8,128)(2,1)S(1)} collective-permute-done((bf16[8,16,896]{2,1,0:T(8,128)(2,1)S(1)}, bf16[8,16,896]{2,1,0:T(8,128)(2,1)S(1)}, u32[]{:S(2)}, u32[]{:S(2)}) %collective-permute-start.10) | collective-permute-done | bytes 229408 | tf_op jit(solution)/shard_map/ppermute | solution.py:61
  61.4 6.8 %collective-permute-start.26 = (bf16[4,256,512]{2,1,0:T(8,128)(2,1)S(1)}, bf16[4,256,512]{2,1,0:T(8,128)(2,1)S(1)}, u32[]{:S(2)}, u32[]{:S(2)}) collective-permute-start(bf16[4,256,512]{2,1,0:T(8,128)(2,1)S(1)} %get-tuple-element.28.refs_0_), channel_id=1, source_target_pairs={{0,1},{1,0},{2,3},{3,2},{4,5},{5,4},{6,7},{7,6},{8,9},{9,8},{10,11... | collective-permute-start | bytes 3145736 | tf_op jit(solution)/shard_map/ppermute | solution.py:56
  68.3 2.5 %collective-permute-done.18.refs_5_ = bf16[4,32,896]{2,1,0:T(8,128)(2,1)S(1)} collective-permute-done((bf16[4,32,896]{2,1,0:T(8,128)(2,1)S(1)}, bf16[4,32,896]{2,1,0:T(8,128)(2,1)S(1)}, u32[]{:S(2)}, u32[]{:S(2)}) %collective-permute-start.18) | collective-permute-done | bytes 229408 | tf_op jit(solution)/shard_map/ppermute | solution.py:56
  70.8 2.2 %encode.1.refs_3_ = bf16[8,16,896]{2,1,0:T(8,128)(2,1)S(1)} custom-call(s32[8,8]{1,0:T(8,128)S(1)} %pad_add_fusion.refs_0_, bf16[8,16,896]{2,1,0:T(8,128)(2,1)S(1)} %get-tuple-element.20.refs_1_, bf16[8,16,896]{2,1,0:T(8,128)(2,1)S(1)} %collective-permute-done.9.refs_4_.refs_2_, bf16[8,16,896]{2,1,0:T(8,128)(2,1)S(1)} %collective-permute-done.10.refs_5_.refs_3_, ...), custom_call_target="tpu_custom_call" | custom-call | bytes 1376256 | tf_op jit(solution)/shard_map/encode/pallas_call | solution.py:38
  73.5 2.2 %collective-permute-start.22 = (bf16[8,16,896]{2,1,0:T(8,128)(2,1)S(1)}, bf16[8,16,896]{2,1,0:T(8,128)(2,1)S(1)}, u32[]{:S(2)}, u32[]{:S(2)}) collective-permute-start(bf16[8,16,896]{2,1,0:T(8,128)(2,1)S(1)} %encode.1.refs_3_), channel_id=1, source_target_pairs={{0,4},{1,5},{2,6},{3,7},{4,0},{5,1},{6,2},{7,3},{8,12},{9,13},{10,... | collective-permute-start | bytes 688136 | tf_op jit(solution)/shard_map/ppermute | solution.py:52
  77.9 3.3 %collective-permute-done.20 = bf16[8,16,896]{2,1,0:T(8,128)(2,1)S(1)} collective-permute-done((bf16[8,16,896]{2,1,0:T(8,128)(2,1)S(1)}, bf16[8,16,896]{2,1,0:T(8,128)(2,1)S(1)}, u32[]{:S(2)}, u32[]{:S(2)}) %collective-permute-start.20) | collective-permute-done | bytes 229408 | tf_op jit(solution)/shard_map/ppermute | solution.py:52
  81.2 6.0 %collective-permute-start.21 = (bf16[8,16,896]{2,1,0:T(8,128)(2,1)S(1)}, bf16[8,16,896]{2,1,0:T(8,128)(2,1)S(1)}, u32[]{:S(2)}, u32[]{:S(2)}) collective-permute-start(bf16[8,16,896]{2,1,0:T(8,128)(2,1)S(1)} %collective-permute-done.20), channel_id=1, source_target_pairs={{0,1},{1,0},{2,3},{3,2},{4,5},{5,4},{6,7},{7,6},{8,9},{9,8},{10,11... | collective-permute-start | bytes 688136 | tf_op jit(solution)/shard_map/ppermute | solution.py:56
  89.1 3.1 %attend.1.refs_0_ = bf16[256,256]{1,0:T(8,128)(2,1)S(1)} custom-call(bf16[4,32,896]{2,1,0:T(8,128)(2,1)S(1)} %bitcast.19, bf16[4,32,896]{2,1,0:T(8,128)(2,1)S(1)} %bitcast.23, bf16[4,32,896]{2,1,0:T(8,128)(2,1)S(1)} %bitcast.20, bf16[4,32,896]{2,1,0:T(8,128)(2,1)S(1)} %bitcast.24, bf16[4,32,896]{2,1,0:T(8,128)(2,1)S(1)} %bitcast.21, ...), custom_call_target="tpu_custom_call" | custom-call | flops 939524096 | bytes 3014656 | tf_op jit(solution)/shard_map/attend/pallas_call | solution.py:322
  93.1 2.6 %collective-permute-start.30 = (bf16[256,256]{1,0:T(8,128)(2,1)S(1)}, bf16[256,256]{1,0:T(8,128)(2,1)S(1)}, u32[]{:S(2)}, u32[]{:S(2)}) collective-permute-start(bf16[256,256]{1,0:T(8,128)(2,1)S(1)} %attend.1.refs_0_), channel_id=1, source_target_pairs={{0,4},{1,5},{2,6},{3,7},{4,0},{5,1},{6,2},{7,3},{8,12},{9,13},{10,... | collective-permute-start | bytes 393224 | tf_op jit(solution)/shard_map/ppermute | solution.py:52
  99.4 2.4 %collective-permute-done.30.refs_4_ = bf16[256,256]{1,0:T(8,128)(2,1)S(1)} collective-permute-done((bf16[256,256]{1,0:T(8,128)(2,1)S(1)}, bf16[256,256]{1,0:T(8,128)(2,1)S(1)}, u32[]{:S(2)}, u32[]{:S(2)}) %collective-permute-start.30) | collective-permute-done | bytes 131104 | tf_op jit(solution)/shard_map/ppermute | solution.py:52
  (74 shorter events, 31.9 us)
Async XLA Ops:
  1.2 26.6 %collective-permute-start.3 = (bf16[16,16,896]{2,1,0:T(8,128)(2,1)S(1)}, bf16[16,16,896]{2,1,0:T(8,128)(2,1)S(1)}, u32[]{:S(2)}, u32[]{:S(2)}) collective-permute-start(bf16[16,16,896]{2,1,0:T(8,128)(2,1)S(1)} %constant_dynamic-slice_fusion.refs_1_), channel_id=1, source_target_pairs={{0,64},{8,72},{16,80},{24,88},{32,96},{40,104},{48,112},{56,120},{... | collective-permute-start | bytes 1376264 | tf_op jit(solution)/shard_map/ppermute | solution.py:66
  3.3 24.5 %collective-permute-start.4 = (bf16[16,16,896]{2,1,0:T(8,128)(2,1)S(1)}, bf16[16,16,896]{2,1,0:T(8,128)(2,1)S(1)}, u32[]{:S(2)}, u32[]{:S(2)}) collective-permute-start(bf16[16,16,896]{2,1,0:T(8,128)(2,1)S(1)} %constant_dynamic-slice_fusion.refs_1_), channel_id=1, source_target_pairs={{0,128},{8,136},{16,144},{24,152},{32,160},{40,168},{48,176},{56,1... | collective-permute-start | bytes 1376264 | tf_op jit(solution)/shard_map/ppermute | solution.py:66
  5.7 22.1 %collective-permute-start.5 = (bf16[16,16,896]{2,1,0:T(8,128)(2,1)S(1)}, bf16[16,16,896]{2,1,0:T(8,128)(2,1)S(1)}, u32[]{:S(2)}, u32[]{:S(2)}) collective-permute-start(bf16[16,16,896]{2,1,0:T(8,128)(2,1)S(1)} %constant_dynamic-slice_fusion.refs_1_), channel_id=1, source_target_pairs={{0,192},{8,200},{16,208},{24,216},{32,224},{40,232},{48,240},{56,2... | collective-permute-start | bytes 1376264 | tf_op jit(solution)/shard_map/ppermute | solution.py:66
  7.8 7.1 %collective-permute-start = (s32[1,8]{1,0:T(1,128)S(1)}, s32[1,8]{1,0:T(1,128)S(1)}, u32[]{:S(2)}, u32[]{:S(2)}) collective-permute-start(s32[1,8]{1,0:T(1,128)S(1)} %reshape.30), channel_id=1, source_target_pairs={{0,8},{8,16},{16,24},{24,32},{32,40},{40,48},{48,56},{56,0},{64,72... | collective-permute-start | bytes 104 | tf_op jit(solution)/shard_map/ppermute | solution.py:61
  13.0 19.5 %collective-permute-start.11 = (f32[4,32,896]{2,1,0:T(8,128)S(1)}, f32[4,32,896]{2,1,0:T(8,128)S(1)}, u32[]{:S(2)}, u32[]{:S(2)}) collective-permute-start(f32[4,32,896]{2,1,0:T(8,128)S(1)} %get-tuple-element.29), channel_id=1, source_target_pairs={{0,1},{1,0},{2,3},{3,2},{4,5},{5,4},{6,7},{7,6},{8,9},{9,8},{10,11... | collective-permute-start | bytes 1376264 | tf_op jit(solution)/shard_map/ppermute | solution.py:56
  14.9 6.5 %collective-permute-start.1 = (s32[2,8]{1,0:T(2,128)S(1)}, s32[2,8]{1,0:T(2,128)S(1)}, u32[]{:S(2)}, u32[]{:S(2)}) collective-permute-start(s32[2,8]{1,0:T(2,128)S(1)} %pad_add_fusion.2), channel_id=1, source_target_pairs={{0,16},{8,24},{16,32},{24,40},{32,48},{40,56},{48,0},{56,8},{64,80... | collective-permute-start | bytes 200 | tf_op jit(solution)/shard_map/ppermute | solution.py:61
  21.3 6.4 %collective-permute-start.2 = (s32[4,8]{1,0:T(4,128)S(1)}, s32[4,8]{1,0:T(4,128)S(1)}, u32[]{:S(2)}, u32[]{:S(2)}) collective-permute-start(s32[4,8]{1,0:T(4,128)S(1)} %pad_add_fusion.1), channel_id=1, source_target_pairs={{0,32},{8,40},{16,48},{24,56},{32,0},{40,8},{48,16},{56,24},{64,96... | collective-permute-start | bytes 392 | tf_op jit(solution)/shard_map/ppermute | solution.py:61
  29.1 13.6 %collective-permute-start.6 = (bf16[16,16,896]{2,1,0:T(8,128)(2,1)S(1)}, bf16[16,16,896]{2,1,0:T(8,128)(2,1)S(1)}, u32[]{:S(2)}, u32[]{:S(2)}) collective-permute-start(bf16[16,16,896]{2,1,0:T(8,128)(2,1)S(1)} %get-tuple-element.17), channel_id=1, source_target_pairs={{0,56},{8,0},{16,8},{24,16},{32,24},{40,32},{48,40},{56,48},{64,12... | collective-permute-start | bytes 1376264 | tf_op jit(solution)/shard_map/ppermute | solution.py:61
  32.4 11.8 %collective-permute-start.7 = (bf16[16,16,896]{2,1,0:T(8,128)(2,1)S(1)}, bf16[16,16,896]{2,1,0:T(8,128)(2,1)S(1)}, u32[]{:S(2)}, u32[]{:S(2)}) collective-permute-start(bf16[16,16,896]{2,1,0:T(8,128)(2,1)S(1)} %get-tuple-element.18), channel_id=1, source_target_pairs={{0,8},{8,16},{16,24},{24,32},{32,40},{40,48},{48,56},{56,0},{64,72... | collective-permute-start | bytes 1376264 | tf_op jit(solution)/shard_map/ppermute | solution.py:61
  33.9 16.0 %collective-permute-start.8 = (bf16[8,16,896]{2,1,0:T(8,128)(2,1)S(1)}, bf16[8,16,896]{2,1,0:T(8,128)(2,1)S(1)}, u32[]{:S(2)}, u32[]{:S(2)}) collective-permute-start(bf16[8,16,896]{2,1,0:T(8,128)(2,1)S(1)} %get-tuple-element.19), channel_id=1, source_target_pairs={{0,48},{1,17},{2,50},{3,19},{4,52},{5,21},{6,54},{7,23},{8,56},{9,... | collective-permute-start | bytes 688136 | tf_op jit(solution)/shard_map/ppermute | solution.py:76
  44.3 17.1 %collective-permute-start.15 = (bf16[320,512]{1,0:T(8,128)(2,1)S(1)}, bf16[320,512]{1,0:T(8,128)(2,1)S(1)}, u32[]{:S(2)}, u32[]{:S(2)}) collective-permute-start(bf16[320,512]{1,0:T(8,128)(2,1)S(1)} %pack.1.refs_0_), channel_id=1, source_target_pairs={{0,2},{1,3},{2,4},{3,5},{4,6},{5,7},{6,0},{7,1},{8,10},{9,11},{10,... | collective-permute-start | bytes 983048 | tf_op jit(solution)/shard_map/ppermute | solution.py:52
  45.6 15.7 %collective-permute-start.16 = (bf16[320,512]{1,0:T(8,128)(2,1)S(1)}, bf16[320,512]{1,0:T(8,128)(2,1)S(1)}, u32[]{:S(2)}, u32[]{:S(2)}) collective-permute-start(bf16[320,512]{1,0:T(8,128)(2,1)S(1)} %pack.1.refs_0_), channel_id=1, source_target_pairs={{0,4},{1,5},{2,6},{3,7},{4,0},{5,1},{6,2},{7,3},{8,12},{9,13},{10,... | collective-permute-start | bytes 983048 | tf_op jit(solution)/shard_map/ppermute | solution.py:52
  48.2 13.1 %collective-permute-start.17 = (bf16[320,512]{1,0:T(8,128)(2,1)S(1)}, bf16[320,512]{1,0:T(8,128)(2,1)S(1)}, u32[]{:S(2)}, u32[]{:S(2)}) collective-permute-start(bf16[320,512]{1,0:T(8,128)(2,1)S(1)} %pack.1.refs_0_), channel_id=1, source_target_pairs={{0,6},{1,7},{2,0},{3,1},{4,2},{5,3},{6,4},{7,5},{8,14},{9,15},{10,... | collective-permute-start | bytes 983048 | tf_op jit(solution)/shard_map/ppermute | solution.py:52
  51.0 6.3 %collective-permute-start.9 = (bf16[8,16,896]{2,1,0:T(8,128)(2,1)S(1)}, bf16[8,16,896]{2,1,0:T(8,128)(2,1)S(1)}, u32[]{:S(2)}, u32[]{:S(2)}) collective-permute-start(bf16[8,16,896]{2,1,0:T(8,128)(2,1)S(1)} %get-tuple-element.21), channel_id=1, source_target_pairs={{0,48},{8,56},{16,0},{24,8},{32,16},{40,24},{48,32},{56,40},{64,11... | collective-permute-start | bytes 688136 | tf_op jit(solution)/shard_map/ppermute | solution.py:61
  51.6 9.7 %collective-permute-start.10 = (bf16[8,16,896]{2,1,0:T(8,128)(2,1)S(1)}, bf16[8,16,896]{2,1,0:T(8,128)(2,1)S(1)}, u32[]{:S(2)}, u32[]{:S(2)}) collective-permute-start(bf16[8,16,896]{2,1,0:T(8,128)(2,1)S(1)} %get-tuple-element.22), channel_id=1, source_target_pairs={{0,16},{8,24},{16,32},{24,40},{32,48},{40,56},{48,0},{56,8},{64,80... | collective-permute-start | bytes 688136 | tf_op jit(solution)/shard_map/ppermute | solution.py:61
  61.4 26.5 %collective-permute-start.26 = (bf16[4,256,512]{2,1,0:T(8,128)(2,1)S(1)}, bf16[4,256,512]{2,1,0:T(8,128)(2,1)S(1)}, u32[]{:S(2)}, u32[]{:S(2)}) collective-permute-start(bf16[4,256,512]{2,1,0:T(8,128)(2,1)S(1)} %get-tuple-element.28.refs_0_), channel_id=1, source_target_pairs={{0,1},{1,0},{2,3},{3,2},{4,5},{5,4},{6,7},{7,6},{8,9},{9,8},{10,11... | collective-permute-start | bytes 3145736 | tf_op jit(solution)/shard_map/ppermute | solution.py:56
  73.0 8.2 %collective-permute-start.20 = (bf16[8,16,896]{2,1,0:T(8,128)(2,1)S(1)}, bf16[8,16,896]{2,1,0:T(8,128)(2,1)S(1)}, u32[]{:S(2)}, u32[]{:S(2)}) collective-permute-start(bf16[8,16,896]{2,1,0:T(8,128)(2,1)S(1)} %encode.1.refs_3_), channel_id=1, source_target_pairs={{0,2},{1,3},{2,4},{3,5},{4,6},{5,7},{6,0},{7,1},{8,10},{9,11},{10,... | collective-permute-start | bytes 688136 | tf_op jit(solution)/shard_map/ppermute | solution.py:52
  73.5 13.8 %collective-permute-start.22 = (bf16[8,16,896]{2,1,0:T(8,128)(2,1)S(1)}, bf16[8,16,896]{2,1,0:T(8,128)(2,1)S(1)}, u32[]{:S(2)}, u32[]{:S(2)}) collective-permute-start(bf16[8,16,896]{2,1,0:T(8,128)(2,1)S(1)} %encode.1.refs_3_), channel_id=1, source_target_pairs={{0,4},{1,5},{2,6},{3,7},{4,0},{5,1},{6,2},{7,3},{8,12},{9,13},{10,... | collective-permute-start | bytes 688136 | tf_op jit(solution)/shard_map/ppermute | solution.py:52
  75.7 11.6 %collective-permute-start.24 = (bf16[8,16,896]{2,1,0:T(8,128)(2,1)S(1)}, bf16[8,16,896]{2,1,0:T(8,128)(2,1)S(1)}, u32[]{:S(2)}, u32[]{:S(2)}) collective-permute-start(bf16[8,16,896]{2,1,0:T(8,128)(2,1)S(1)} %encode.1.refs_3_), channel_id=1, source_target_pairs={{0,6},{1,7},{2,0},{3,1},{4,2},{5,3},{6,4},{7,5},{8,14},{9,15},{10,... | collective-permute-start | bytes 688136 | tf_op jit(solution)/shard_map/ppermute | solution.py:52
  76.7 11.9 %collective-permute-start.19 = (bf16[8,16,896]{2,1,0:T(8,128)(2,1)S(1)}, bf16[8,16,896]{2,1,0:T(8,128)(2,1)S(1)}, u32[]{:S(2)}, u32[]{:S(2)}) collective-permute-start(bf16[8,16,896]{2,1,0:T(8,128)(2,1)S(1)} %encode.1.refs_3_), channel_id=1, source_target_pairs={{0,1},{1,0},{2,3},{3,2},{4,5},{5,4},{6,7},{7,6},{8,9},{9,8},{10,11... | collective-permute-start | bytes 688136 | tf_op jit(solution)/shard_map/ppermute | solution.py:56
  81.2 7.4 %collective-permute-start.21 = (bf16[8,16,896]{2,1,0:T(8,128)(2,1)S(1)}, bf16[8,16,896]{2,1,0:T(8,128)(2,1)S(1)}, u32[]{:S(2)}, u32[]{:S(2)}) collective-permute-start(bf16[8,16,896]{2,1,0:T(8,128)(2,1)S(1)} %collective-permute-done.20), channel_id=1, source_target_pairs={{0,1},{1,0},{2,3},{3,2},{4,5},{5,4},{6,7},{7,6},{8,9},{9,8},{10,11... | collective-permute-start | bytes 688136 | tf_op jit(solution)/shard_map/ppermute | solution.py:56
  93.1 8.7 %collective-permute-start.30 = (bf16[256,256]{1,0:T(8,128)(2,1)S(1)}, bf16[256,256]{1,0:T(8,128)(2,1)S(1)}, u32[]{:S(2)}, u32[]{:S(2)}) collective-permute-start(bf16[256,256]{1,0:T(8,128)(2,1)S(1)} %attend.1.refs_0_), channel_id=1, source_target_pairs={{0,4},{1,5},{2,6},{3,7},{4,0},{5,1},{6,2},{7,3},{8,12},{9,13},{10,... | collective-permute-start | bytes 393224 | tf_op jit(solution)/shard_map/ppermute | solution.py:52
  95.7 7.3 %collective-permute-start.32 = (bf16[256,256]{1,0:T(8,128)(2,1)S(1)}, bf16[256,256]{1,0:T(8,128)(2,1)S(1)}, u32[]{:S(2)}, u32[]{:S(2)}) collective-permute-start(bf16[256,256]{1,0:T(8,128)(2,1)S(1)} %attend.1.refs_0_), channel_id=1, source_target_pairs={{0,6},{1,7},{2,0},{3,1},{4,2},{5,3},{6,4},{7,5},{8,14},{9,15},{10,... | collective-permute-start | bytes 393224 | tf_op jit(solution)/shard_map/ppermute | solution.py:52
  95.8 7.2 %collective-permute-start.27 = (bf16[256,256]{1,0:T(8,128)(2,1)S(1)}, bf16[256,256]{1,0:T(8,128)(2,1)S(1)}, u32[]{:S(2)}, u32[]{:S(2)}) collective-permute-start(bf16[256,256]{1,0:T(8,128)(2,1)S(1)} %attend.1.refs_0_), channel_id=1, source_target_pairs={{0,1},{1,0},{2,3},{3,2},{4,5},{5,4},{6,7},{7,6},{8,9},{9,8},{10,11... | collective-permute-start | bytes 393224 | tf_op jit(solution)/shard_map/ppermute | solution.py:56
  (16 other events, 239.5 us)

commit v5 on v4

--- a/solution.py
+++ b/solution.py
@@ -77,7 +77,7 @@
 
 
 def chip_blocks(a):
-    one, three, two = [y_shift(a, r) for r in (1, 3, 2)]
+    two, one, three = [y_shift(a, r) for r in (2, 1, 3)]
     return [a, one, two, three]
 
 

time: 106 us -> 106 us (level)
  no operation moved by 1% of the time
where the time goes in v5:
time: 106 us
  starting transfers between devices  58.2 us (55%)
  waiting for transfers between devices  31.7 us (30%)
  Pallas kernels  10.1 us (10%)
  local copies, waits for them, and re-layouts  2.57 us (2%)
  matrix products  2.33 us (2%)
    ppermute x11, starting transfers between devices, core_swap(): return lax.ppermute(a, 'head', [(h, h ^ 1) for h in range(NH)])  20.2 us
    ppermute x12, starting transfers between devices, y_shift(): return lax.ppermute(a, 'head', pairs)  17.3 us
    ppermute x7, starting transfers between devices, z_shift(): return lax.ppermute(a, 'seq', pairs)  15.1 us
    ppermute x7, waiting for transfers between devices, z_shift(): return lax.ppermute(a, 'seq', pairs)  14.7 us
    ppermute x12, waiting for transfers between devices, y_shift(): return lax.ppermute(a, 'head', pairs)  12.1 us
    ppermute x3, starting transfers between devices, x_shift(): return lax.ppermute(a, 'seq', pairs)  5.72 us
    pallas_call x7, Pallas kernels, whole(): pl.pallas_call(functools.partial(without, len(after), len(lists) + len(ar...  5.52 us
    ppermute x11, waiting for transfers between devices, core_swap(): return lax.ppermute(a, 'head', [(h, h ^ 1) for h in range(NH)])  4.32 us
  transfers between devices with their start and end apart: 34, of which 16 were waited for; matrix products, arithmetic and copies ran while one was open for 4% of the time, Pallas kernels for 5%

profile of v5, /device:TPU:1, one launch (start us, length us, event | category | flops | bytes accessed | tf_op | source)
XLA Modules:
  0.0 105.8 jit_solution(14638231817072244411)
XLA Ops:
  1.2 2.1 %collective-permute-start.3 = (bf16[16,16,896]{2,1,0:T(8,128)(2,1)S(1)}, bf16[16,16,896]{2,1,0:T(8,128)(2,1)S(1)}, u32[]{:S(2)}, u32[]{:S(2)}) collective-permute-start(bf16[16,16,896]{2,1,0:T(8,128)(2,1)S(1)} %constant_dynamic-slice_fusion.refs_1_), channel_id=1, source_target_pairs={{0,64},{8,72},{16,80},{24,88},{32,96},{40,104},{48,112},{56,120},{... | collective-permute-start | bytes 1376264 | tf_op jit(solution)/shard_map/ppermute | solution.py:66
  3.3 2.5 %collective-permute-start.4 = (bf16[16,16,896]{2,1,0:T(8,128)(2,1)S(1)}, bf16[16,16,896]{2,1,0:T(8,128)(2,1)S(1)}, u32[]{:S(2)}, u32[]{:S(2)}) collective-permute-start(bf16[16,16,896]{2,1,0:T(8,128)(2,1)S(1)} %constant_dynamic-slice_fusion.refs_1_), channel_id=1, source_target_pairs={{0,128},{8,136},{16,144},{24,152},{32,160},{40,168},{48,176},{56,1... | collective-permute-start | bytes 1376264 | tf_op jit(solution)/shard_map/ppermute | solution.py:66
  9.4 2.3 %fusion = f32[256,896]{1,0:T(8,128)} fusion(bf16[256,512]{1,0:T(8,128)(2,1)} %refs_4_.1, bf16[512,896]{1,0:T(8,128)(2,1)S(1)} %copy-done), kind=kOutput, calls=%fused_computation.7 | convolution fusion | flops 234881024 | bytes 2097152 | tf_op jit(solution)/shard_map/dot_general | solution.py:127
  13.0 1.9 %collective-permute-start.11 = (f32[4,32,896]{2,1,0:T(8,128)S(1)}, f32[4,32,896]{2,1,0:T(8,128)S(1)}, u32[]{:S(2)}, u32[]{:S(2)}) collective-permute-start(f32[4,32,896]{2,1,0:T(8,128)S(1)} %get-tuple-element.29), channel_id=1, source_target_pairs={{0,1},{1,0},{2,3},{3,2},{4,5},{5,4},{6,7},{7,6},{8,9},{9,8},{10,11... | collective-permute-start | bytes 1376264 | tf_op jit(solution)/shard_map/ppermute | solution.py:56
  14.9 3.1 %collective-permute-start.1 = (s32[2,8]{1,0:T(2,128)S(1)}, s32[2,8]{1,0:T(2,128)S(1)}, u32[]{:S(2)}, u32[]{:S(2)}) collective-permute-start(s32[2,8]{1,0:T(2,128)S(1)} %pad_add_fusion.2), channel_id=1, source_target_pairs={{0,16},{8,24},{16,32},{24,40},{32,48},{40,56},{48,0},{56,8},{64,80... | collective-permute-start | bytes 200 | tf_op jit(solution)/shard_map/ppermute | solution.py:61
  17.9 3.4 %collective-permute-done.1 = s32[2,8]{1,0:T(2,128)S(1)} collective-permute-done((s32[2,8]{1,0:T(2,128)S(1)}, s32[2,8]{1,0:T(2,128)S(1)}, u32[]{:S(2)}, u32[]{:S(2)}) %collective-permute-start.1) | collective-permute-done | bytes 96 | tf_op jit(solution)/shard_map/ppermute | solution.py:61
  21.3 4.6 %collective-permute-start.2 = (s32[4,8]{1,0:T(4,128)S(1)}, s32[4,8]{1,0:T(4,128)S(1)}, u32[]{:S(2)}, u32[]{:S(2)}) collective-permute-start(s32[4,8]{1,0:T(4,128)S(1)} %pad_add_fusion.1), channel_id=1, source_target_pairs={{0,32},{8,40},{16,48},{24,56},{32,0},{40,8},{48,16},{56,24},{64,96... | collective-permute-start | bytes 392 | tf_op jit(solution)/shard_map/ppermute | solution.py:61
  29.1 3.3 %collective-permute-start.6 = (bf16[16,16,896]{2,1,0:T(8,128)(2,1)S(1)}, bf16[16,16,896]{2,1,0:T(8,128)(2,1)S(1)}, u32[]{:S(2)}, u32[]{:S(2)}) collective-permute-start(bf16[16,16,896]{2,1,0:T(8,128)(2,1)S(1)} %get-tuple-element.17), channel_id=1, source_target_pairs={{0,56},{8,0},{16,8},{24,16},{32,24},{40,32},{48,40},{56,48},{64,12... | collective-permute-start | bytes 1376264 | tf_op jit(solution)/shard_map/ppermute | solution.py:61
  35.5 2.0 %collective-permute-done.12.refs_1_ = f32[32,896]{1,0:T(8,128)S(1)} collective-permute-done((f32[32,896]{1,0:T(8,128)S(1)}, f32[32,896]{1,0:T(8,128)S(1)}, u32[]{:S(2)}, u32[]{:S(2)}) %collective-permute-start.12) | collective-permute-done | bytes 114720 | tf_op jit(solution)/shard_map/ppermute | solution.py:52
  37.5 1.9 %collective-permute-start.14 = (f32[32,896]{1,0:T(8,128)S(1)}, f32[32,896]{1,0:T(8,128)S(1)}, u32[]{:S(2)}, u32[]{:S(2)}) collective-permute-start(f32[32,896]{1,0:T(8,128)S(1)} %get-tuple-element.26), channel_id=1, source_target_pairs={{0,4},{1,5},{2,6},{3,7},{4,0},{5,1},{6,2},{7,3},{8,12},{9,13},{10,... | collective-permute-start | bytes 344072 | tf_op jit(solution)/shard_map/ppermute | solution.py:52
  39.4 3.2 %collective-permute-done.14.refs_3_ = f32[32,896]{1,0:T(8,128)S(1)} collective-permute-done((f32[32,896]{1,0:T(8,128)S(1)}, f32[32,896]{1,0:T(8,128)S(1)}, u32[]{:S(2)}, u32[]{:S(2)}) %collective-permute-start.14) | collective-permute-done | bytes 114720 | tf_op jit(solution)/shard_map/ppermute | solution.py:52
  45.6 2.6 %collective-permute-start.16 = (bf16[320,512]{1,0:T(8,128)(2,1)S(1)}, bf16[320,512]{1,0:T(8,128)(2,1)S(1)}, u32[]{:S(2)}, u32[]{:S(2)}) collective-permute-start(bf16[320,512]{1,0:T(8,128)(2,1)S(1)} %pack.1.refs_0_), channel_id=1, source_target_pairs={{0,4},{1,5},{2,6},{3,7},{4,0},{5,1},{6,2},{7,3},{8,12},{9,13},{10,... | collective-permute-start | bytes 983048 | tf_op jit(solution)/shard_map/ppermute | solution.py:52
  51.6 1.9 %collective-permute-start.10 = (bf16[8,16,896]{2,1,0:T(8,128)(2,1)S(1)}, bf16[8,16,896]{2,1,0:T(8,128)(2,1)S(1)}, u32[]{:S(2)}, u32[]{:S(2)}) collective-permute-start(bf16[8,16,896]{2,1,0:T(8,128)(2,1)S(1)} %get-tuple-element.22), channel_id=1, source_target_pairs={{0,16},{8,24},{16,32},{24,40},{32,48},{40,56},{48,0},{56,8},{64,80... | collective-permute-start | bytes 688136 | tf_op jit(solution)/shard_map/ppermute | solution.py:61
  53.4 3.8 %collective-permute-done.9.refs_4_.refs_2_ = bf16[8,16,896]{2,1,0:T(8,128)(2,1)S(1)} collective-permute-done((bf16[8,16,896]{2,1,0:T(8,128)(2,1)S(1)}, bf16[8,16,896]{2,1,0:T(8,128)(2,1)S(1)}, u32[]{:S(2)}, u32[]{:S(2)}) %collective-permute-start.9) | collective-permute-done | bytes 229408 | tf_op jit(solution)/shard_map/ppermute | solution.py:61
  57.3 4.0 %collective-permute-done.10.refs_5_.refs_3_ = bf16[8,16,896]{2,1,0:T(8,128)(2,1)S(1)} collective-permute-done((bf16[8,16,896]{2,1,0:T(8,128)(2,1)S(1)}, bf16[8,16,896]{2,1,0:T(8,128)(2,1)S(1)}, u32[]{:S(2)}, u32[]{:S(2)}) %collective-permute-start.10) | collective-permute-done | bytes 229408 | tf_op jit(solution)/shard_map/ppermute | solution.py:61
  61.4 6.8 %collective-permute-start.26 = (bf16[4,256,512]{2,1,0:T(8,128)(2,1)S(1)}, bf16[4,256,512]{2,1,0:T(8,128)(2,1)S(1)}, u32[]{:S(2)}, u32[]{:S(2)}) collective-permute-start(bf16[4,256,512]{2,1,0:T(8,128)(2,1)S(1)} %get-tuple-element.28.refs_0_), channel_id=1, source_target_pairs={{0,1},{1,0},{2,3},{3,2},{4,5},{5,4},{6,7},{7,6},{8,9},{9,8},{10,11... | collective-permute-start | bytes 3145736 | tf_op jit(solution)/shard_map/ppermute | solution.py:56
  68.3 2.5 %collective-permute-done.18.refs_5_ = bf16[4,32,896]{2,1,0:T(8,128)(2,1)S(1)} collective-permute-done((bf16[4,32,896]{2,1,0:T(8,128)(2,1)S(1)}, bf16[4,32,896]{2,1,0:T(8,128)(2,1)S(1)}, u32[]{:S(2)}, u32[]{:S(2)}) %collective-permute-start.18) | collective-permute-done | bytes 229408 | tf_op jit(solution)/shard_map/ppermute | solution.py:56
  70.8 2.2 %encode.1.refs_3_ = bf16[8,16,896]{2,1,0:T(8,128)(2,1)S(1)} custom-call(s32[8,8]{1,0:T(8,128)S(1)} %pad_add_fusion.refs_0_, bf16[8,16,896]{2,1,0:T(8,128)(2,1)S(1)} %get-tuple-element.20.refs_1_, bf16[8,16,896]{2,1,0:T(8,128)(2,1)S(1)} %collective-permute-done.9.refs_4_.refs_2_, bf16[8,16,896]{2,1,0:T(8,128)(2,1)S(1)} %collective-permute-done.10.refs_5_.refs_3_, ...), custom_call_target="tpu_custom_call" | custom-call | bytes 1376256 | tf_op jit(solution)/shard_map/encode/pallas_call | solution.py:38
  73.5 2.2 %collective-permute-start.22 = (bf16[8,16,896]{2,1,0:T(8,128)(2,1)S(1)}, bf16[8,16,896]{2,1,0:T(8,128)(2,1)S(1)}, u32[]{:S(2)}, u32[]{:S(2)}) collective-permute-start(bf16[8,16,896]{2,1,0:T(8,128)(2,1)S(1)} %encode.1.refs_3_), channel_id=1, source_target_pairs={{0,4},{1,5},{2,6},{3,7},{4,0},{5,1},{6,2},{7,3},{8,12},{9,13},{10,... | collective-permute-start | bytes 688136 | tf_op jit(solution)/shard_map/ppermute | solution.py:52
  77.9 3.3 %collective-permute-done.20 = bf16[8,16,896]{2,1,0:T(8,128)(2,1)S(1)} collective-permute-done((bf16[8,16,896]{2,1,0:T(8,128)(2,1)S(1)}, bf16[8,16,896]{2,1,0:T(8,128)(2,1)S(1)}, u32[]{:S(2)}, u32[]{:S(2)}) %collective-permute-start.20) | collective-permute-done | bytes 229408 | tf_op jit(solution)/shard_map/ppermute | solution.py:52
  81.2 6.0 %collective-permute-start.21 = (bf16[8,16,896]{2,1,0:T(8,128)(2,1)S(1)}, bf16[8,16,896]{2,1,0:T(8,128)(2,1)S(1)}, u32[]{:S(2)}, u32[]{:S(2)}) collective-permute-start(bf16[8,16,896]{2,1,0:T(8,128)(2,1)S(1)} %collective-permute-done.20), channel_id=1, source_target_pairs={{0,1},{1,0},{2,3},{3,2},{4,5},{5,4},{6,7},{7,6},{8,9},{9,8},{10,11... | collective-permute-start | bytes 688136 | tf_op jit(solution)/shard_map/ppermute | solution.py:56
  89.1 3.1 %attend.1.refs_0_ = bf16[256,256]{1,0:T(8,128)(2,1)S(1)} custom-call(bf16[4,32,896]{2,1,0:T(8,128)(2,1)S(1)} %bitcast.19, bf16[4,32,896]{2,1,0:T(8,128)(2,1)S(1)} %bitcast.23, bf16[4,32,896]{2,1,0:T(8,128)(2,1)S(1)} %bitcast.20, bf16[4,32,896]{2,1,0:T(8,128)(2,1)S(1)} %bitcast.24, bf16[4,32,896]{2,1,0:T(8,128)(2,1)S(1)} %bitcast.21, ...), custom_call_target="tpu_custom_call" | custom-call | flops 939524096 | bytes 3014656 | tf_op jit(solution)/shard_map/attend/pallas_call | solution.py:322
  93.1 2.6 %collective-permute-start.30 = (bf16[256,256]{1,0:T(8,128)(2,1)S(1)}, bf16[256,256]{1,0:T(8,128)(2,1)S(1)}, u32[]{:S(2)}, u32[]{:S(2)}) collective-permute-start(bf16[256,256]{1,0:T(8,128)(2,1)S(1)} %attend.1.refs_0_), channel_id=1, source_target_pairs={{0,4},{1,5},{2,6},{3,7},{4,0},{5,1},{6,2},{7,3},{8,12},{9,13},{10,... | collective-permute-start | bytes 393224 | tf_op jit(solution)/shard_map/ppermute | solution.py:52
  99.4 2.4 %collective-permute-done.30.refs_4_ = bf16[256,256]{1,0:T(8,128)(2,1)S(1)} collective-permute-done((bf16[256,256]{1,0:T(8,128)(2,1)S(1)}, bf16[256,256]{1,0:T(8,128)(2,1)S(1)}, u32[]{:S(2)}, u32[]{:S(2)}) %collective-permute-start.30) | collective-permute-done | bytes 131104 | tf_op jit(solution)/shard_map/ppermute | solution.py:52
  (74 shorter events, 31.9 us)
Async XLA Ops:
  1.2 26.6 %collective-permute-start.3 = (bf16[16,16,896]{2,1,0:T(8,128)(2,1)S(1)}, bf16[16,16,896]{2,1,0:T(8,128)(2,1)S(1)}, u32[]{:S(2)}, u32[]{:S(2)}) collective-permute-start(bf16[16,16,896]{2,1,0:T(8,128)(2,1)S(1)} %constant_dynamic-slice_fusion.refs_1_), channel_id=1, source_target_pairs={{0,64},{8,72},{16,80},{24,88},{32,96},{40,104},{48,112},{56,120},{... | collective-permute-start | bytes 1376264 | tf_op jit(solution)/shard_map/ppermute | solution.py:66
  3.3 24.5 %collective-permute-start.4 = (bf16[16,16,896]{2,1,0:T(8,128)(2,1)S(1)}, bf16[16,16,896]{2,1,0:T(8,128)(2,1)S(1)}, u32[]{:S(2)}, u32[]{:S(2)}) collective-permute-start(bf16[16,16,896]{2,1,0:T(8,128)(2,1)S(1)} %constant_dynamic-slice_fusion.refs_1_), channel_id=1, source_target_pairs={{0,128},{8,136},{16,144},{24,152},{32,160},{40,168},{48,176},{56,1... | collective-permute-start | bytes 1376264 | tf_op jit(solution)/shard_map/ppermute | solution.py:66
  5.7 22.1 %collective-permute-start.5 = (bf16[16,16,896]{2,1,0:T(8,128)(2,1)S(1)}, bf16[16,16,896]{2,1,0:T(8,128)(2,1)S(1)}, u32[]{:S(2)}, u32[]{:S(2)}) collective-permute-start(bf16[16,16,896]{2,1,0:T(8,128)(2,1)S(1)} %constant_dynamic-slice_fusion.refs_1_), channel_id=1, source_target_pairs={{0,192},{8,200},{16,208},{24,216},{32,224},{40,232},{48,240},{56,2... | collective-permute-start | bytes 1376264 | tf_op jit(solution)/shard_map/ppermute | solution.py:66
  7.8 7.1 %collective-permute-start = (s32[1,8]{1,0:T(1,128)S(1)}, s32[1,8]{1,0:T(1,128)S(1)}, u32[]{:S(2)}, u32[]{:S(2)}) collective-permute-start(s32[1,8]{1,0:T(1,128)S(1)} %reshape.30), channel_id=1, source_target_pairs={{0,8},{8,16},{16,24},{24,32},{32,40},{40,48},{48,56},{56,0},{64,72... | collective-permute-start | bytes 104 | tf_op jit(solution)/shard_map/ppermute | solution.py:61
  13.0 19.5 %collective-permute-start.11 = (f32[4,32,896]{2,1,0:T(8,128)S(1)}, f32[4,32,896]{2,1,0:T(8,128)S(1)}, u32[]{:S(2)}, u32[]{:S(2)}) collective-permute-start(f32[4,32,896]{2,1,0:T(8,128)S(1)} %get-tuple-element.29), channel_id=1, source_target_pairs={{0,1},{1,0},{2,3},{3,2},{4,5},{5,4},{6,7},{7,6},{8,9},{9,8},{10,11... | collective-permute-start | bytes 1376264 | tf_op jit(solution)/shard_map/ppermute | solution.py:56
  14.9 6.5 %collective-permute-start.1 = (s32[2,8]{1,0:T(2,128)S(1)}, s32[2,8]{1,0:T(2,128)S(1)}, u32[]{:S(2)}, u32[]{:S(2)}) collective-permute-start(s32[2,8]{1,0:T(2,128)S(1)} %pad_add_fusion.2), channel_id=1, source_target_pairs={{0,16},{8,24},{16,32},{24,40},{32,48},{40,56},{48,0},{56,8},{64,80... | collective-permute-start | bytes 200 | tf_op jit(solution)/shard_map/ppermute | solution.py:61
  21.3 6.4 %collective-permute-start.2 = (s32[4,8]{1,0:T(4,128)S(1)}, s32[4,8]{1,0:T(4,128)S(1)}, u32[]{:S(2)}, u32[]{:S(2)}) collective-permute-start(s32[4,8]{1,0:T(4,128)S(1)} %pad_add_fusion.1), channel_id=1, source_target_pairs={{0,32},{8,40},{16,48},{24,56},{32,0},{40,8},{48,16},{56,24},{64,96... | collective-permute-start | bytes 392 | tf_op jit(solution)/shard_map/ppermute | solution.py:61
  29.1 13.6 %collective-permute-start.6 = (bf16[16,16,896]{2,1,0:T(8,128)(2,1)S(1)}, bf16[16,16,896]{2,1,0:T(8,128)(2,1)S(1)}, u32[]{:S(2)}, u32[]{:S(2)}) collective-permute-start(bf16[16,16,896]{2,1,0:T(8,128)(2,1)S(1)} %get-tuple-element.17), channel_id=1, source_target_pairs={{0,56},{8,0},{16,8},{24,16},{32,24},{40,32},{48,40},{56,48},{64,12... | collective-permute-start | bytes 1376264 | tf_op jit(solution)/shard_map/ppermute | solution.py:61
  32.4 11.8 %collective-permute-start.7 = (bf16[16,16,896]{2,1,0:T(8,128)(2,1)S(1)}, bf16[16,16,896]{2,1,0:T(8,128)(2,1)S(1)}, u32[]{:S(2)}, u32[]{:S(2)}) collective-permute-start(bf16[16,16,896]{2,1,0:T(8,128)(2,1)S(1)} %get-tuple-element.18), channel_id=1, source_target_pairs={{0,8},{8,16},{16,24},{24,32},{32,40},{40,48},{48,56},{56,0},{64,72... | collective-permute-start | bytes 1376264 | tf_op jit(solution)/shard_map/ppermute | solution.py:61
  33.9 16.0 %collective-permute-start.8 = (bf16[8,16,896]{2,1,0:T(8,128)(2,1)S(1)}, bf16[8,16,896]{2,1,0:T(8,128)(2,1)S(1)}, u32[]{:S(2)}, u32[]{:S(2)}) collective-permute-start(bf16[8,16,896]{2,1,0:T(8,128)(2,1)S(1)} %get-tuple-element.19), channel_id=1, source_target_pairs={{0,48},{1,17},{2,50},{3,19},{4,52},{5,21},{6,54},{7,23},{8,56},{9,... | collective-permute-start | bytes 688136 | tf_op jit(solution)/shard_map/ppermute | solution.py:76
  44.3 17.1 %collective-permute-start.15 = (bf16[320,512]{1,0:T(8,128)(2,1)S(1)}, bf16[320,512]{1,0:T(8,128)(2,1)S(1)}, u32[]{:S(2)}, u32[]{:S(2)}) collective-permute-start(bf16[320,512]{1,0:T(8,128)(2,1)S(1)} %pack.1.refs_0_), channel_id=1, source_target_pairs={{0,2},{1,3},{2,4},{3,5},{4,6},{5,7},{6,0},{7,1},{8,10},{9,11},{10,... | collective-permute-start | bytes 983048 | tf_op jit(solution)/shard_map/ppermute | solution.py:52
  45.6 15.7 %collective-permute-start.16 = (bf16[320,512]{1,0:T(8,128)(2,1)S(1)}, bf16[320,512]{1,0:T(8,128)(2,1)S(1)}, u32[]{:S(2)}, u32[]{:S(2)}) collective-permute-start(bf16[320,512]{1,0:T(8,128)(2,1)S(1)} %pack.1.refs_0_), channel_id=1, source_target_pairs={{0,4},{1,5},{2,6},{3,7},{4,0},{5,1},{6,2},{7,3},{8,12},{9,13},{10,... | collective-permute-start | bytes 983048 | tf_op jit(solution)/shard_map/ppermute | solution.py:52
  48.2 13.1 %collective-permute-start.17 = (bf16[320,512]{1,0:T(8,128)(2,1)S(1)}, bf16[320,512]{1,0:T(8,128)(2,1)S(1)}, u32[]{:S(2)}, u32[]{:S(2)}) collective-permute-start(bf16[320,512]{1,0:T(8,128)(2,1)S(1)} %pack.1.refs_0_), channel_id=1, source_target_pairs={{0,6},{1,7},{2,0},{3,1},{4,2},{5,3},{6,4},{7,5},{8,14},{9,15},{10,... | collective-permute-start | bytes 983048 | tf_op jit(solution)/shard_map/ppermute | solution.py:52
  51.0 6.3 %collective-permute-start.9 = (bf16[8,16,896]{2,1,0:T(8,128)(2,1)S(1)}, bf16[8,16,896]{2,1,0:T(8,128)(2,1)S(1)}, u32[]{:S(2)}, u32[]{:S(2)}) collective-permute-start(bf16[8,16,896]{2,1,0:T(8,128)(2,1)S(1)} %get-tuple-element.21), channel_id=1, source_target_pairs={{0,48},{8,56},{16,0},{24,8},{32,16},{40,24},{48,32},{56,40},{64,11... | collective-permute-start | bytes 688136 | tf_op jit(solution)/shard_map/ppermute | solution.py:61
  51.6 9.7 %collective-permute-start.10 = (bf16[8,16,896]{2,1,0:T(8,128)(2,1)S(1)}, bf16[8,16,896]{2,1,0:T(8,128)(2,1)S(1)}, u32[]{:S(2)}, u32[]{:S(2)}) collective-permute-start(bf16[8,16,896]{2,1,0:T(8,128)(2,1)S(1)} %get-tuple-element.22), channel_id=1, source_target_pairs={{0,16},{8,24},{16,32},{24,40},{32,48},{40,56},{48,0},{56,8},{64,80... | collective-permute-start | bytes 688136 | tf_op jit(solution)/shard_map/ppermute | solution.py:61
  61.4 26.5 %collective-permute-start.26 = (bf16[4,256,512]{2,1,0:T(8,128)(2,1)S(1)}, bf16[4,256,512]{2,1,0:T(8,128)(2,1)S(1)}, u32[]{:S(2)}, u32[]{:S(2)}) collective-permute-start(bf16[4,256,512]{2,1,0:T(8,128)(2,1)S(1)} %get-tuple-element.28.refs_0_), channel_id=1, source_target_pairs={{0,1},{1,0},{2,3},{3,2},{4,5},{5,4},{6,7},{7,6},{8,9},{9,8},{10,11... | collective-permute-start | bytes 3145736 | tf_op jit(solution)/shard_map/ppermute | solution.py:56
  73.0 8.2 %collective-permute-start.20 = (bf16[8,16,896]{2,1,0:T(8,128)(2,1)S(1)}, bf16[8,16,896]{2,1,0:T(8,128)(2,1)S(1)}, u32[]{:S(2)}, u32[]{:S(2)}) collective-permute-start(bf16[8,16,896]{2,1,0:T(8,128)(2,1)S(1)} %encode.1.refs_3_), channel_id=1, source_target_pairs={{0,2},{1,3},{2,4},{3,5},{4,6},{5,7},{6,0},{7,1},{8,10},{9,11},{10,... | collective-permute-start | bytes 688136 | tf_op jit(solution)/shard_map/ppermute | solution.py:52
  73.5 13.8 %collective-permute-start.22 = (bf16[8,16,896]{2,1,0:T(8,128)(2,1)S(1)}, bf16[8,16,896]{2,1,0:T(8,128)(2,1)S(1)}, u32[]{:S(2)}, u32[]{:S(2)}) collective-permute-start(bf16[8,16,896]{2,1,0:T(8,128)(2,1)S(1)} %encode.1.refs_3_), channel_id=1, source_target_pairs={{0,4},{1,5},{2,6},{3,7},{4,0},{5,1},{6,2},{7,3},{8,12},{9,13},{10,... | collective-permute-start | bytes 688136 | tf_op jit(solution)/shard_map/ppermute | solution.py:52
  75.7 11.6 %collective-permute-start.24 = (bf16[8,16,896]{2,1,0:T(8,128)(2,1)S(1)}, bf16[8,16,896]{2,1,0:T(8,128)(2,1)S(1)}, u32[]{:S(2)}, u32[]{:S(2)}) collective-permute-start(bf16[8,16,896]{2,1,0:T(8,128)(2,1)S(1)} %encode.1.refs_3_), channel_id=1, source_target_pairs={{0,6},{1,7},{2,0},{3,1},{4,2},{5,3},{6,4},{7,5},{8,14},{9,15},{10,... | collective-permute-start | bytes 688136 | tf_op jit(solution)/shard_map/ppermute | solution.py:52
  76.7 11.9 %collective-permute-start.19 = (bf16[8,16,896]{2,1,0:T(8,128)(2,1)S(1)}, bf16[8,16,896]{2,1,0:T(8,128)(2,1)S(1)}, u32[]{:S(2)}, u32[]{:S(2)}) collective-permute-start(bf16[8,16,896]{2,1,0:T(8,128)(2,1)S(1)} %encode.1.refs_3_), channel_id=1, source_target_pairs={{0,1},{1,0},{2,3},{3,2},{4,5},{5,4},{6,7},{7,6},{8,9},{9,8},{10,11... | collective-permute-start | bytes 688136 | tf_op jit(solution)/shard_map/ppermute | solution.py:56
  81.2 7.4 %collective-permute-start.21 = (bf16[8,16,896]{2,1,0:T(8,128)(2,1)S(1)}, bf16[8,16,896]{2,1,0:T(8,128)(2,1)S(1)}, u32[]{:S(2)}, u32[]{:S(2)}) collective-permute-start(bf16[8,16,896]{2,1,0:T(8,128)(2,1)S(1)} %collective-permute-done.20), channel_id=1, source_target_pairs={{0,1},{1,0},{2,3},{3,2},{4,5},{5,4},{6,7},{7,6},{8,9},{9,8},{10,11... | collective-permute-start | bytes 688136 | tf_op jit(solution)/shard_map/ppermute | solution.py:56
  93.1 8.7 %collective-permute-start.30 = (bf16[256,256]{1,0:T(8,128)(2,1)S(1)}, bf16[256,256]{1,0:T(8,128)(2,1)S(1)}, u32[]{:S(2)}, u32[]{:S(2)}) collective-permute-start(bf16[256,256]{1,0:T(8,128)(2,1)S(1)} %attend.1.refs_0_), channel_id=1, source_target_pairs={{0,4},{1,5},{2,6},{3,7},{4,0},{5,1},{6,2},{7,3},{8,12},{9,13},{10,... | collective-permute-start | bytes 393224 | tf_op jit(solution)/shard_map/ppermute | solution.py:52
  95.7 7.3 %collective-permute-start.32 = (bf16[256,256]{1,0:T(8,128)(2,1)S(1)}, bf16[256,256]{1,0:T(8,128)(2,1)S(1)}, u32[]{:S(2)}, u32[]{:S(2)}) collective-permute-start(bf16[256,256]{1,0:T(8,128)(2,1)S(1)} %attend.1.refs_0_), channel_id=1, source_target_pairs={{0,6},{1,7},{2,0},{3,1},{4,2},{5,3},{6,4},{7,5},{8,14},{9,15},{10,... | collective-permute-start | bytes 393224 | tf_op jit(solution)/shard_map/ppermute | solution.py:52
  95.8 7.2 %collective-permute-start.27 = (bf16[256,256]{1,0:T(8,128)(2,1)S(1)}, bf16[256,256]{1,0:T(8,128)(2,1)S(1)}, u32[]{:S(2)}, u32[]{:S(2)}) collective-permute-start(bf16[256,256]{1,0:T(8,128)(2,1)S(1)} %attend.1.refs_0_), channel_id=1, source_target_pairs={{0,1},{1,0},{2,3},{3,2},{4,5},{5,4},{6,7},{7,6},{8,9},{9,8},{10,11... | collective-permute-start | bytes 393224 | tf_op jit(solution)/shard_map/ppermute | solution.py:56
  (16 other events, 239.5 us)
